TPU v7x, 128 devices: a whole 4x4x4 slice. The times are simulated.
128 devices in a mesh: mode: 4 (over z_lo, core), site: 32 (over y, z_hi, x).
Axes of the slice: x: 4, y: 4, z: 4 (z_hi: 2, z_lo: 2; z = z_hi * 2 + z_lo), core: 2. Of those that a mesh axis runs over, the one named last changes fastest.
Arguments:
- low_modes: bfloat16 [64, 4, 2, 3, 8, 65536], P('mode', None, None, None, None, 'site'), may hold values from -6 to 6
- high_modes: bfloat16 [64, 2, 3, 8, 65536], P('mode', None, None, None, 'site'), may hold values from -0.013671875 to 0.013671875
- pattern: int32 [64], replicated, may hold values from 0 to 3
- momenta: int32 [8, 3], replicated, may hold values from -2 to 2
Outputs:
- meson: float32 [4, 2, 64, 64, 64], P(None, None, 'site', None, 'mode')
All inputs are finite; a program needn't handle non-finite values.
Results may differ from a plain program's by a relative error of at most 0.0065.
Values may be sent and summed in bfloat16 or wider, within the bound.
No kernel may reach another device: no remote copies, remote signals or barrier semaphores. Data moves between devices by JAX's collectives and lax.ppermute only.
A program may use at most 320 MiB of HBM per device.

v0:
```python
import math

import jax
import jax.numpy as jnp
import numpy as np
from jax import lax
from jax.sharding import PartitionSpec as P


def shifted(block, axis, distance):
    devices = range(lax.axis_size(axis))
    route = [((i - distance) % len(devices), i) for i in devices]
    return lax.ppermute(block, axis, route)


def gamma_tables():
    real_table = np.zeros((4, 4, 4), np.float32)
    imag_table = np.zeros((4, 4, 4), np.float32)
    for spin in range(4):
        real_table[0, spin, spin] = 1.0
    for row_spin, col_spin in ((0, 2), (1, 3), (2, 0), (3, 1)):
        real_table[1, row_spin, col_spin] = 1.0
    for row_spin, col_spin, value in ((0, 3, 1.0), (1, 2, 1.0), (2, 1, -1.0), (3, 0, -1.0)):
        imag_table[2, row_spin, col_spin] = value
    for row_spin, col_spin, value in ((0, 1, -1.0), (1, 0, 1.0), (2, 3, -1.0), (3, 2, 1.0)):
        real_table[3, row_spin, col_spin] = value
    return (real_table, imag_table)


def phase_tables(momenta, first_site, count):
    sites = first_site + jnp.arange(count, dtype=jnp.int32)
    coords = jnp.stack([sites % 32, sites // 32 % 32, sites // 1024])
    turns = jnp.sum(momenta[:, :, None] * coords[None, :, :], axis=1)
    angles = turns.astype(jnp.float32) * (2.0 * math.pi / 96.0)
    return (jnp.cos(angles), jnp.sin(angles))


def contract(high_block, block_pattern, low_part, cosines, sines):
    real_table, imag_table = gamma_tables()
    real_part = high_block[None, :, 0].astype(jnp.float32)
    imag_part = high_block[None, :, 1].astype(jnp.float32)
    cos_b = cosines[:, None, None, None, :]
    sin_b = sines[:, None, None, None, :]
    phased_real = real_part * cos_b - imag_part * sin_b
    phased_imag = real_part * sin_b + imag_part * cos_b
    phased = jnp.stack([phased_real, phased_imag], axis=2).astype(jnp.bfloat16)
    products = jnp.einsum(
        "phrctx,lsuctx->tphrlsu", phased, low_part, preferred_element_type=jnp.float32
    )
    over_real = products[:, :, :, 0, :, :, 0] + products[:, :, :, 1, :, :, 1]
    over_imag = products[:, :, :, 0, :, :, 1] - products[:, :, :, 1, :, :, 0]
    select = (block_pattern[:, None] == jnp.arange(4, dtype=jnp.int32)[None, :]).astype(jnp.float32)
    coef_real = jnp.einsum("ha,gas->ghs", select, jnp.asarray(real_table, jnp.float32))
    coef_imag = jnp.einsum("ha,gas->ghs", select, jnp.asarray(imag_table, jnp.float32))
    meson_real = jnp.einsum("ghs,tphls->gtphl", coef_real, over_real) - jnp.einsum(
        "ghs,tphls->gtphl", coef_imag, over_imag
    )
    meson_imag = jnp.einsum("ghs,tphls->gtphl", coef_real, over_imag) + jnp.einsum(
        "ghs,tphls->gtphl", coef_imag, over_real
    )
    return jnp.stack([meson_real, meson_imag], axis=1)


def body(low_modes, high_modes, pattern, momenta):
    n_mode = lax.axis_size("mode")
    my_mode = lax.axis_index("mode")
    count = low_modes.shape[-1]
    cosines, sines = phase_tables(momenta, lax.axis_index("site") * count, count)
    block_rows = high_modes.shape[0]
    slices = high_modes.shape[3]
    n_moms = momenta.shape[0]
    n_low = low_modes.shape[0]
    totals = jnp.zeros((4, 2, slices, n_moms, block_rows * n_mode, n_low), jnp.float32)

    def block_pattern(source):
        return lax.dynamic_slice_in_dim(pattern, source * block_rows, block_rows, 0)

    def place(totals, partial_field, source, first_slice):
        return lax.dynamic_update_slice(
            totals, partial_field, (0, 0, first_slice, 0, source * block_rows, 0)
        )

    own = contract(high_modes, block_pattern(my_mode), low_modes, cosines, sines)
    totals = place(totals, own, my_mode, 0)
    moving = high_modes
    for rotation in range(1, n_mode):
        moving = shifted(moving, "mode", 1)
        source = (my_mode - rotation) % n_mode
        totals = place(
            totals, contract(moving, block_pattern(source), low_modes, cosines, sines), source, 0
        )
    flat = totals.reshape(4, 2, slices * n_moms, block_rows * n_mode, n_low)
    return lax.psum_scatter(flat, "site", scatter_dimension=2, tiled=True)


def solution(mesh):
    placed = (
        P("mode", None, None, None, None, "site"),
        P("mode", None, None, None, "site"),
        P(),
        P(),
    )
    return jax.shard_map(
        body,
        mesh=mesh,
        in_specs=placed,
        out_specs=P(None, None, "site", None, "mode"),
        check_vma=False,
    )
```

profile of v0, /device:TPU:0, one launch (start us, length us, event | category | flops | bytes accessed | tf_op | source)
XLA Modules:
  0.0 1030.5 jit_solution(537294402579699204)
XLA Ops:
  6.5 37.0 %collective-permute-done = bf16[16,2,3,8,2048]{4,3,2,1,0:T(8,128)(2,1)} collective-permute-done((bf16[16,2,3,8,2048]{4,3,2,1,0:T(8,128)(2,1)}, bf16[16,2,3,8,2048]{4,3,2,1,0:T(8,128)(2,1)}, u32[]{:S(2)}, u32[]{:S(2)}) %collective-permute-start) | collective-permute-done | bytes 3145760 | tf_op jit(solution)/shard_map/ppermute | solution.py:13
  56.1 24.4 %collective-permute-done.1 = bf16[16,2,3,8,2048]{4,3,2,1,0:T(8,128)(2,1)} collective-permute-done((bf16[16,2,3,8,2048]{4,3,2,1,0:T(8,128)(2,1)}, bf16[16,2,3,8,2048]{4,3,2,1,0:T(8,128)(2,1)}, u32[]{:S(2)}, u32[]{:S(2)}) %collective-permute-start.1) | collective-permute-done | bytes 3145760 | tf_op jit(solution)/shard_map/ppermute | solution.py:13
  96.1 3.5 copy.135
  103.1 14.6 %collective-permute-done.2 = bf16[16,2,3,8,2048]{4,3,2,1,0:T(8,128)(2,1)} collective-permute-done((bf16[16,2,3,8,2048]{4,3,2,1,0:T(8,128)(2,1)}, bf16[16,2,3,8,2048]{4,3,2,1,0:T(8,128)(2,1)}, u32[]{:S(2)}, u32[]{:S(2)}) %collective-permute-start.2) | collective-permute-done | bytes 3145760 | tf_op jit(solution)/shard_map/ppermute | solution.py:13
  120.4 3.5 copy.147
  123.9 3.7 copy.148
  127.6 45.9 %subtract_convert_fusion = (bf16[8,16,1,3,8,2048]{5,1,3,2,0,4:T(8,128)(2,1)}, bf16[8,16,1,3,8,2048]{5,1,3,2,0,4:T(8,128)(2,1)}, bf16[8,16,1,3,8,2048]{5,1,3,2,0,...) fusion(f32[16,3,8,2048]{3,0,1,2:T(8,128)} %copy.148, ...), kind=kLoop, calls=%fused_computation.17 | loop fusion | flops 201326592 | bytes 125960192 | tf_op jit(solution)/shard_map/convert.8
  173.5 35.2 %fusion.16 = f32[8,8,16,2,16,4,2]{4,2,6,5,3,1,0:T(8,128)} fusion(bf16[16,4,2,3,8,2048,1,1]{5,4,3,2,1,0,7,6:T(8,128)(2,1)} %bitcast.240, bf16[8,16,1,3,8,2048]{5,1,3,2,0,4:T(8,128)(2,1)} %get-tuple-element.14, bf16[8,16,1,3,8,2048]{5,1,3,2,0,4:T(8,128)(2,1)} %get-tuple-element.13), kind=kOutput, calls=%fused_computation.32 | convolution fusion | flops 3271557120 | bytes 38797312 | tf_op jit(solution)/shard_map/phrctx,lsuctx->tphrlsu/dot_general | solution.py:47
  208.7 4.6 fusion.29
  219.4 5.9 copy.158
  225.3 34.7 %fusion.19 = f32[8,8,16,2,16,4,2]{4,2,6,5,3,1,0:T(8,128)} fusion(bf16[16,4,2,3,8,2048,1,1]{5,4,3,2,1,0,7,6:T(8,128)(2,1)} %bitcast.241, bf16[8,16,1,3,8,2048]{5,1,3,2,0,4:T(8,128)(2,1)} %get-tuple-element.31, bf16[8,16,1,3,8,2048]{5,1,3,2,0,4:T(8,128)(2,1)} %get-tuple-element.32), kind=kOutput, calls=%fused_computation.33 | convolution fusion | flops 3271557120 | bytes 38797312 | tf_op jit(solution)/shard_map/phrctx,lsuctx->tphrlsu/dot_general | solution.py:47
  260.0 4.6 fusion.31
  270.8 5.7 copy.146
  276.5 34.9 %fusion.22 = f32[8,8,16,2,16,4,2]{4,2,6,5,3,1,0:T(8,128)} fusion(bf16[16,4,2,3,8,2048,1,1]{5,4,3,2,1,0,7,6:T(8,128)(2,1)} %bitcast.242, bf16[8,16,1,3,8,2048]{5,1,3,2,0,4:T(8,128)(2,1)} %get-tuple-element.29, bf16[8,16,1,3,8,2048]{5,1,3,2,0,4:T(8,128)(2,1)} %get-tuple-element.30), kind=kOutput, calls=%fused_computation.34 | convolution fusion | flops 3271557120 | bytes 38797312 | tf_op jit(solution)/shard_map/phrctx,lsuctx->tphrlsu/dot_general | solution.py:47
  311.4 4.6 fusion.33
  322.1 6.1 copy.134
  328.2 34.8 %fusion.25 = f32[8,8,16,2,16,4,2]{4,2,6,5,3,1,0:T(8,128)} fusion(bf16[16,4,2,3,8,2048,1,1]{5,4,3,2,1,0,7,6:T(8,128)(2,1)} %bitcast.243, bf16[8,16,1,3,8,2048]{5,1,3,2,0,4:T(8,128)(2,1)} %get-tuple-element.33, bf16[8,16,1,3,8,2048]{5,1,3,2,0,4:T(8,128)(2,1)} %get-tuple-element.34), kind=kOutput, calls=%fused_computation.35 | convolution fusion | flops 3271557120 | bytes 38797312 | tf_op jit(solution)/shard_map/phrctx,lsuctx->tphrlsu/dot_general | solution.py:47
  363.0 4.6 fusion.35
  373.7 5.7 copy.122
  381.9 23.1 %dynamic_update_slice.12 = f32[4,2,8,8,64,16]{4,5,3,2,1,0:T(8,128)} dynamic-update-slice(f32[4,2,8,8,64,16]{4,5,3,2,1,0:T(8,128)} %broadcast_in_dim.2, f32[4,2,8,8,16,16]{4,5,3,2,1,0:T(8,128)} %copy.122, s32[]{:T(128)} %constant.79.clone.1, s32[]{:T(128)} %constant.79.clone.1, s32[]{:T(128)} %constant.79.clone.1, s32[]{:T(128)} %constant.79.clone.1, s32[]{:T(128)S(6)} %select_n.81, s32[]{:T(128)} %constant.79.clone.1) | dynamic-update-slice | bytes 1048580 | tf_op jit(solution)/shard_map/dynamic_update_slice | solution.py:79
  405.0 83.0 %dynamic_update_slice.13 = f32[4,2,8,8,64,16]{4,5,3,2,1,0:T(8,128)} dynamic-update-slice(f32[4,2,8,8,64,16]{4,5,3,2,1,0:T(8,128)} %dynamic_update_slice.12, f32[4,2,8,8,16,16]{4,5,3,2,1,0:T(8,128)} %copy.134, s32[]{:T(128)} %constant.79.clone.1, s32[]{:T(128)} %constant.79.clone.1, s32[]{:T(128)} %constant.79.clone.1, s32[]{:T(128)} %constant.79.clone.1, s32[]{:T(128)S(6)} %select_n.83, ...) | dynamic-update-slice | bytes 1048580 | tf_op jit(solution)/shard_map/dynamic_update_slice | solution.py:79
  488.1 83.1 %dynamic_update_slice.14 = f32[4,2,8,8,64,16]{4,5,3,2,1,0:T(8,128)} dynamic-update-slice(f32[4,2,8,8,64,16]{4,5,3,2,1,0:T(8,128)} %dynamic_update_slice.13, f32[4,2,8,8,16,16]{4,5,3,2,1,0:T(8,128)} %copy.146, s32[]{:T(128)} %constant.79.clone.1, s32[]{:T(128)} %constant.79.clone.1, s32[]{:T(128)} %constant.79.clone.1, s32[]{:T(128)} %constant.79.clone.1, s32[]{:T(128)S(6)} %select_n.85, ...) | dynamic-update-slice | bytes 1048580 | tf_op jit(solution)/shard_map/dynamic_update_slice | solution.py:79
  571.1 83.1 %dynamic_update_slice.15 = f32[4,2,8,8,64,16]{4,5,3,2,1,0:T(8,128)} dynamic-update-slice(f32[4,2,8,8,64,16]{4,5,3,2,1,0:T(8,128)} %dynamic_update_slice.14, f32[4,2,8,8,16,16]{4,5,3,2,1,0:T(8,128)} %copy.158, s32[]{:T(128)} %constant.79.clone.1, s32[]{:T(128)} %constant.79.clone.1, s32[]{:T(128)} %constant.79.clone.1, s32[]{:T(128)} %constant.79.clone.1, s32[]{:T(128)S(6)} %select_n.87, ...) | dynamic-update-slice | bytes 1048580 | tf_op jit(solution)/shard_map/dynamic_update_slice | solution.py:79
  656.1 365.8 %all-reduce.3.cloned.1.call-done = f32[4,2,64,64,16]{3,4,2,1,0:T(8,128)} async-done(((f32[4,2,64,64,16]{3,4,2,1,0:T(8,128)}), f32[4,2,64,64,16]{3,4,2,1,0:T(8,128)}) %all-reduce.3.cloned.1.call-update) | async-done | bytes 2097168
  (79 shorter events, 63.9 us)
Async XLA Ops:
  6.5 1015.3 %all-reduce.3.cloned.1.call-start = ((), (), s32[]{:S(2)}) async-start(), calls=%async_computation | async-start | bytes 8388608
  6.5 37.0 %collective-permute-start = (bf16[16,2,3,8,2048]{4,3,2,1,0:T(8,128)(2,1)}, bf16[16,2,3,8,2048]{4,3,2,1,0:T(8,128)(2,1)}, u32[]{:S(2)}, u32[]{:S(2)}) collective-permute-start(bf16[16,2,3,8,2048]{4,3,2,1,0:T(8,128)(2,1)} %param.13), channel_id=1, source_target_pairs={{96,0},{0,32},{32,64},{64,96},{97,1},{1,33},{33,65},{65,97},{98,2}... | collective-permute-start | bytes 9437192 | tf_op jit(solution)/shard_map/ppermute | solution.py:13
  43.5 37.0 %collective-permute-start.1 = (bf16[16,2,3,8,2048]{4,3,2,1,0:T(8,128)(2,1)}, bf16[16,2,3,8,2048]{4,3,2,1,0:T(8,128)(2,1)}, u32[]{:S(2)}, u32[]{:S(2)}) collective-permute-start(bf16[16,2,3,8,2048]{4,3,2,1,0:T(8,128)(2,1)} %collective-permute-done), channel_id=1, source_target_pairs={{96,0},{0,32},{32,64},{64,96},{97,1},{1,33},{33,65},{65,97},{98,2}... | collective-permute-start | bytes 9437192 | tf_op jit(solution)/shard_map/ppermute | solution.py:13
  49.9 3.5 copy-start.6
  49.9 3.7 copy-start.7
  49.9 33.5 %copy-start.8 = (s32[8,3]{0,1:T(4,128)S(1)}, s32[8,3]{0,1:T(4,128)}, u32[]{:S(2)}) copy-start(s32[8,3]{0,1:T(4,128)} %param.15) | copy-start | bytes 292
  80.6 37.2 %collective-permute-start.2 = (bf16[16,2,3,8,2048]{4,3,2,1,0:T(8,128)(2,1)}, bf16[16,2,3,8,2048]{4,3,2,1,0:T(8,128)(2,1)}, u32[]{:S(2)}, u32[]{:S(2)}) collective-permute-start(bf16[16,2,3,8,2048]{4,3,2,1,0:T(8,128)(2,1)} %collective-permute-done.1), channel_id=1, source_target_pairs={{96,0},{0,32},{32,64},{64,96},{97,1},{1,33},{33,65},{65,97},{98,2}... | collective-permute-start | bytes 9437192 | tf_op jit(solution)/shard_map/ppermute | solution.py:13
  259.9 4.6 copy-start.4
  259.9 5.3 copy-start.5
  311.4 4.6 copy-start.1
  311.4 5.3 copy-start.3
  363.0 4.6 copy-start
  363.0 5.3 copy-start.2
  654.2 0.7 copy-start.9
Sparse Core Ops, SparseCore 0:
  654.4 367.4 all-reduce.2
where the time goes:
time: 1040 us; the launch traced here: 1030 us
  waiting for transfers between devices  442 us (42%)
  local copies, waits for them, and re-layouts  333 us (32%)
  matrix products  153 us (15%)
  other arithmetic  88.1 us (8%)
  between operations  14.6 us (1%)
    unnamed x2, waiting for transfers between devices  366 us
    dynamic_update_slice x4, local copies, waits for them, and re-layouts, place(): lax.dynamic_update_slice(totals, partial_field, (0, 0, first_slice, 0, so...  272 us
    dot_general x4, matrix products, contract(): jnp.einsum('phrctx,lsuctx->tphrlsu', phased, low_part, preferred_element_...  140 us
    ppermute x3, waiting for transfers between devices, shifted(): return lax.ppermute(block, axis, route)  76.1 us
    another operation x1, other arithmetic  45.9 us
    another operation x4, local copies, waits for them, and re-layouts, contract(): return jnp.stack([meson_real, meson_imag], axis=1)  23.3 us
  transfers between devices with their start and end apart: 4, of which 4 were waited for; matrix products, arithmetic and copies ran while one was open for 3% of the time, Pallas kernels for 0%

commit v1 on v0

v1 whole, which is shorter than its diff:
```python
import math

import jax
import jax.numpy as jnp
from jax import lax
from jax.experimental import pallas as pl
from jax.experimental.pallas import tpu as pltpu
from jax.sharding import PartitionSpec as P

NX, NY, NZ = 4, 4, 2
SLOTS = NY * NZ
PARTNER = ((0, 1, 2, 3), (2, 3, 0, 1), (3, 2, 1, 0), (1, 0, 3, 2))


def coords():
    site = lax.axis_index("site")
    return lax.rem(site, 4), lax.div(site, 8), lax.rem(lax.div(site, 4), 2)


def site_of(y, z, x):
    return ((y % NY) * NZ + z % NZ) * NX + x % NX


def move(block, dy, dz, dx):
    route = [
        (site_of(y, z, x), site_of(y + dy, z + dz, x + dx))
        for y in range(NY)
        for z in range(NZ)
        for x in range(NX)
    ]
    return lax.ppermute(block, "site", route)


def flip(block, mask):
    return lax.ppermute(block, "mode", [(i, i ^ mask) for i in range(4)])


def slot_of(t, y, z):
    distance = lax.rem(t // 2 - y + 2 * NY - 1, NY)
    same = 1 - jnp.abs(t % 2 - z)
    return same * NY + distance


def relayout_body(in_ref, out_ref):
    _, y, z = coords()
    rows = in_ref.shape[0]
    width = in_ref.shape[-1]
    lead = (0,) * (len(in_ref.shape) - 3)
    step = 512
    for j in range(0, width, step):
        values = in_ref[(slice(None),) + lead + (slice(None), pl.ds(j, step))].astype(jnp.float32)
        turned = jnp.swapaxes(values, 0, 1).astype(jnp.bfloat16)
        for t in range(SLOTS):
            out_ref[(slot_of(t, y, z),) + lead + (slice(None), pl.ds(j, step))] = turned[t]


def relayout_high(high):
    rows, two, colours, slices, count = high.shape
    return pl.pallas_call(
        relayout_body,
        grid=(two, colours),
        in_specs=[pl.BlockSpec((rows, 1, 1, slices, count), lambda r, c: (0, r, c, 0, 0))],
        out_specs=pl.BlockSpec((slices, 1, 1, rows, count), lambda r, c: (0, r, c, 0, 0)),
        out_shape=jax.ShapeDtypeStruct((slices, two, colours, rows, count), jnp.bfloat16),
        compiler_params=pltpu.CompilerParams(vmem_limit_bytes=16 * 2**20),
        cost_estimate=pl.CostEstimate(flops=0, bytes_accessed=2 * high.size * 2, transcendentals=0),
        name="relayout_high",
    )(high)


def relayout_low(low):
    rows, spins, two, colours, slices, count = low.shape
    return pl.pallas_call(
        relayout_body,
        grid=(colours, two, spins),
        in_specs=[
            pl.BlockSpec((rows, 1, 1, 1, slices, count), lambda c, u, s: (0, s, u, c, 0, 0))
        ],
        out_specs=pl.BlockSpec((slices, 1, 1, 1, rows, count), lambda c, u, s: (0, c, u, s, 0, 0)),
        out_shape=jax.ShapeDtypeStruct((slices, colours, two, spins, rows, count), jnp.bfloat16),
        compiler_params=pltpu.CompilerParams(vmem_limit_bytes=16 * 2**20),
        cost_estimate=pl.CostEstimate(flops=0, bytes_accessed=2 * low.size * 2, transcendentals=0),
        name="relayout_low",
    )(low)


def contract_body(pat_ref, cos_ref, sin_ref, high_ref, own_ref, oth_ref, *rest):
    outs, acc_ref = rest[:NX], rest[NX]
    colour = pl.program_id(1)
    n_moms = cos_ref.shape[0]
    count = high_ref.shape[-1]
    step = 512
    total = None
    for j in range(0, count, step):
        cut = pl.ds(j, step)
        real = high_ref[0, 0, 0, :, cut].astype(jnp.float32)
        imag = high_ref[0, 1, 0, :, cut].astype(jnp.float32)
        reals, imags = [], []
        for p in range(n_moms):
            cosine = jnp.concatenate([cos_ref[p, :, cut]] * 2, 0)
            sine = jnp.concatenate([sin_ref[p, :, cut]] * 2, 0)
            reals.append((real * cosine - imag * sine).astype(jnp.bfloat16))
            imags.append((real * sine + imag * cosine).astype(jnp.bfloat16))
        phased = jnp.concatenate(reals + imags, 0)
        low = jnp.concatenate([own_ref[0, 0, :, cut], oth_ref[0, 0, :, cut]], 0)
        part = lax.dot_general(
            low, phased, (((1,), (1,)), ((), ())), preferred_element_type=jnp.float32
        )
        total = part if total is None else total + part

    @pl.when(colour == 0)
    def _():
        acc_ref[...] = total

    @pl.when(colour > 0)
    def _():
        acc_ref[...] += total

    @pl.when(colour == pl.num_programs(1) - 1)
    def _():
        x, _, _ = coords()
        half = 128
        pattern = pat_ref[0:1, :]
        is_spin = [jnp.broadcast_to(pattern == a, (16, half)) for a in range(4)]
        low_pair = pattern < 2
        odd = jnp.logical_or(pattern == 1, pattern == 3)
        mesons = [[], [], [], []]
        for owner in range(2):
            over = []
            for s in range(4):
                u0 = owner * 128 + s * 16
                u1 = u0 + 64
                over.append(
                    (
                        acc_ref[u0 : u0 + 16, :half] + acc_ref[u1 : u1 + 16, half:],
                        acc_ref[u1 : u1 + 16, :half] - acc_ref[u0 : u0 + 16, half:],
                    )
                )
            for g in range(4):
                picked = []
                for u in range(2):
                    value = over[PARTNER[g][3]][u]
                    for a in range(3):
                        value = jnp.where(is_spin[a], over[PARTNER[g][a]][u], value)
                    picked.append(value)
                re, im = picked
                if g == 2:
                    re, im = jnp.where(low_pair, -im, im), jnp.where(low_pair, re, -re)
                if g == 3:
                    re, im = jnp.where(odd, re, -re), jnp.where(odd, im, -im)
                mesons[g] += [re, im]
        stacked = [jnp.concatenate(m, 0) for m in mesons]
        lane = lax.broadcasted_iota(jnp.int32, stacked[0].shape, 1) // 32
        for k in range(NX):
            group = lax.rem(x + k, NX)
            result = None
            for g in range(4):
                turned = pltpu.roll(stacked[g], lax.rem(g - group + NX, NX) * 32, 1)
                result = turned if result is None else jnp.where(lane == g, turned, result)
            outs[k][0] = result


def contract(pattern_lanes, cosines, sines, high, low_own, low_oth, first, number):
    colours, rows, count = low_own.shape[1:]
    offset = first if high.shape[0] == SLOTS else 0
    whole = lambda shape: pl.BlockSpec(shape, lambda i, c: (0,) * len(shape))
    low_spec = pl.BlockSpec((1, 1, rows, count), lambda i, c: (first + i, c, 0, 0))
    flops = 2 * number * colours * 256 * 256 * count
    return pl.pallas_call(
        contract_body,
        grid=(number, colours),
        in_specs=[
            whole(pattern_lanes.shape),
            whole(cosines.shape),
            whole(sines.shape),
            pl.BlockSpec((1, 2, 1, 16, count), lambda i, c: (offset + i, 0, c, 0, 0)),
            low_spec,
            low_spec,
        ],
        out_specs=[pl.BlockSpec((1, 64, 128), lambda i, c: (i, 0, 0))] * NX,
        out_shape=[jax.ShapeDtypeStruct((number, 64, 128), jnp.float32)] * NX,
        scratch_shapes=[pltpu.VMEM((256, 256), jnp.float32)],
        compiler_params=pltpu.CompilerParams(vmem_limit_bytes=20 * 2**20),
        cost_estimate=pl.CostEstimate(
            flops=flops, bytes_accessed=number * colours * rows * count * 4, transcendentals=0
        ),
        name="contract",
    )(pattern_lanes, cosines, sines, high, low_own, low_oth)


def assemble_body(a_ref, b_ref, c_ref, d_ref, out_ref):
    mode = lax.axis_index("mode")
    blocks = [mode, mode ^ 2, mode ^ 1, mode ^ 3]
    lane = lax.broadcasted_iota(jnp.int32, (32, 128), 1) // 16
    held = [a_ref[...], b_ref[...], c_ref[...], d_ref[...]]
    for g in range(4):
        for p in range(2):
            result = None
            for ref, block in zip(held, blocks):
                shift = lax.rem(block * 16 - (g * 32 + p * 16) + 128, 128)
                turned = pltpu.roll(ref, shift, 1)
                result = turned if result is None else jnp.where(lane == block, turned, result)
            for u in range(2):
                out_ref[g, u, p] = result[u * 16 : u * 16 + 16, :64]


def assemble(pieces):
    return pl.pallas_call(
        assemble_body,
        out_shape=jax.ShapeDtypeStruct((4, 2, 2, 16, 64), jnp.float32),
        name="assemble",
    )(*pieces)


def phase_tables(momenta, first_site, count):
    sites = first_site + jnp.arange(count, dtype=jnp.int32)
    coords = jnp.stack([sites % 32, sites // 32 % 32, sites // 1024])
    turns = jnp.sum(momenta[:, :, None] * coords[None, :, :], axis=1)
    angles = turns.astype(jnp.float32) * (2.0 * math.pi / 96.0)
    wide = lambda a: jnp.broadcast_to(a[:, None, :], (a.shape[0], 8, count))
    return wide(jnp.cos(angles)), wide(jnp.sin(angles))


def sum_x(parts):
    moved = [move(parts[k], 0, 0, k) for k in (1, 2, 3)]
    return parts[0] + moved[0] + moved[1] + moved[2]


def sum_y(slots):
    moved = [move(slots[:, k - 1], k, 0, 0) for k in (1, 2, 3)]
    total = moved[0] + moved[1] + moved[2]
    return total + slots[:, 3] if slots.shape[1] == NY else total


def body(low_modes, high_modes, pattern, momenta):
    count = low_modes.shape[-1]
    my_mode = lax.axis_index("mode")
    high = relayout_high(high_modes)
    chunks = ((0, 4), (4, 3), (7, 1))
    arrived = [flip(high[first : first + number], 2) for first, number in chunks]

    low_own = relayout_low(low_modes)
    low_own = low_own.reshape(low_own.shape[0], low_own.shape[1], -1, count)
    low_oth = flip(low_own, 1)
    cosines, sines = phase_tables(momenta, lax.axis_index("site") * count, count)

    def lanes(block):
        part = lax.dynamic_slice_in_dim(pattern, block * 16, 16, 0)
        return jnp.broadcast_to(jnp.tile(part, 8)[None, :], (8, 128))

    own = contract(lanes(my_mode), cosines, sines, high, low_own, low_oth, 0, SLOTS)
    lanes_recv = lanes(my_mode ^ 2)
    recv = [
        contract(lanes_recv, cosines, sines, block, low_own, low_oth, first, number)
        for block, (first, number) in zip(arrived, chunks)
    ]
    own_x = sum_x(own)
    own_y = sum_y(own_x.reshape(2, NY, 64, 128))
    first_y = sum_y(sum_x(recv[0])[None])
    across = move(jnp.concatenate([own_y[:1], first_y]), 0, 1, 0)
    second_y = sum_y(sum_x(recv[1])[None])
    last = sum_x(recv[2])
    total = jnp.concatenate([own_y[1:], second_y + last]) + across
    other = flip(total[:, 32:], 1)
    pieces = (total[0, :32], total[1, :32], other[0], other[1])
    return jnp.transpose(assemble(pieces), (0, 1, 2, 4, 3))


def solution(mesh):
    placed = (
        P("mode", None, None, None, None, "site"),
        P("mode", None, None, None, "site"),
        P(),
        P(),
    )
    return jax.shard_map(
        body,
        mesh=mesh,
        in_specs=placed,
        out_specs=P(None, None, "site", None, "mode"),
        check_vma=False,
    )
```

time: 1040 us -> 182 us (0.17)
  waiting for transfers between devices: 442 us -> 51.9 us
  local copies, waits for them, and re-layouts: 333 us -> 15.7 us
  matrix products: 153 us -> 0 us
  other arithmetic: 88.1 us -> 2.67 us
  Pallas kernels: 0 us -> 66.1 us
  starting transfers between devices: 0.16 us -> 42.2 us
  between operations: 14.6 us -> 0.23 us
    unnamed x2 -> x0, waiting for transfers between devices: 366 us -> none
    dynamic_update_slice x4 -> x0, local copies, waits for them, and re-layouts: 272 us -> none  [place(): lax.dynamic_update_slice(totals, partial_field, (0, 0, first_slice, 0, so...]
    dot_general x20 -> x0, matrix products: 152 us -> none  [the longest x4 140 us: contract(): jnp.einsum('phrctx,lsuctx->tphrlsu', phased, low_part, preferred_element_...]
    pallas_call x0 -> x7, Pallas kernels: none -> 66.1 us  [the longest x4 49.1 us: contract(): pl.pallas_call(contract_body, grid=(number, colours), in_specs=[whole(pat...]
    another operation x5 -> x0, other arithmetic: 58.3 us -> none
    ppermute x3 -> x27, starting transfers between devices: 0.16 us -> 42.2 us  [the longest x22 38.1 us: move(): return lax.ppermute(block, 'site', route)]
    convert_element_type x8 -> x0, local copies, waits for them, and re-layouts: 26.3 us -> none  [the longest x4 14 us: contract(): imag_part = high_block[None, :, 1].astype(jnp.float32)]
    ppermute x3 -> x27, waiting for transfers between devices: 76.1 us -> 51.9 us  [the longest x5 41.3 us: flip(): return lax.ppermute(block, 'mode', [(i, i ^ mask) for i in range(4)])]
  transfers between devices with their start and end apart: 4 -> 27, of which waited for: 4 -> 9; matrix products, arithmetic and copies ran while one was open for 3% -> 7% of each run, Pallas kernels for 0% -> 29%
where the time goes in v1:
time: 182 us; the launch traced here: 179 us
  Pallas kernels  66.1 us (36%)
  waiting for transfers between devices  51.9 us (29%)
  starting transfers between devices  42.2 us (23%)
  local copies, waits for them, and re-layouts  15.7 us (9%)
  other arithmetic  2.67 us (1%)
    pallas_call x4, Pallas kernels, contract(): pl.pallas_call(contract_body, grid=(number, colours), in_specs=[whole(pat...  49.1 us
    ppermute x5, waiting for transfers between devices, flip(): return lax.ppermute(block, 'mode', [(i, i ^ mask) for i in range(4)])  41.3 us
    ppermute x22, starting transfers between devices, move(): return lax.ppermute(block, 'site', route)  38.1 us
    pallas_call x1, Pallas kernels, relayout_low(): pl.pallas_call(relayout_body, grid=(colours, two, spins), in_specs=[pl.Bl...  13.4 us
    ppermute x22, waiting for transfers between devices, move(): return lax.ppermute(block, 'site', route)  10.6 us
    unnamed x6, local copies, waits for them, and re-layouts  4.58 us
    ppermute x5, starting transfers between devices, flip(): return lax.ppermute(block, 'mode', [(i, i ^ mask) for i in range(4)])  4.11 us
  transfers between devices with their start and end apart: 27, of which 9 were waited for; matrix products, arithmetic and copies ran while one was open for 7% of the time, Pallas kernels for 29%

profile of v1, /device:TPU:0, one launch (start us, length us, event | category | flops | bytes accessed | tf_op | source)
XLA Modules:
  0.0 178.8 jit_solution(3598542460288761208)
XLA Ops:
  0.0 4.6 %copy-done = bf16[16,4,2,3,8,2048]{5,4,3,2,1,0:T(8,128)(2,1)S(1)} copy-done((bf16[16,4,2,3,8,2048]{5,4,3,2,1,0:T(8,128)(2,1)S(1)}, bf16[16,4,2,3,8,2048]{5,4,3,2,1,0:T(8,128)(2,1)}, u32[]{:S(2)}) %copy-start) | copy-done | bytes 12582936
  4.6 13.4 %relayout_low.1 = bf16[8,3,2,4,16,2048]{5,4,3,2,1,0:T(8,128)(2,1)} custom-call(bf16[16,4,2,3,8,2048]{5,4,3,2,1,0:T(8,128)(2,1)S(1)} %copy-done), custom_call_target="tpu_custom_call" | custom-call | bytes 25165824 | tf_op jit(solution)/shard_map/relayout_low/pallas_call | solution.py:73
  18.0 1.9 %relayout_high.1.high_ref = bf16[8,2,3,16,2048]{4,3,2,1,0:T(8,128)(2,1)S(1)} custom-call(bf16[16,2,3,8,2048]{4,3,2,1,0:T(8,128)(2,1)S(1)} %copy-done.1), custom_call_target="tpu_custom_call" | custom-call | bytes 6291456 | tf_op jit(solution)/shard_map/relayout_high/pallas_call | solution.py:59
  21.2 2.0 %collective-permute-start.18 = (bf16[4,2,3,16,2048]{4,3,2,1,0:T(8,128)(2,1)}, bf16[4,2,3,16,2048]{4,3,2,1,0:T(8,128)(2,1)}, u32[]{:S(2)}, u32[]{:S(2)}) collective-permute-start(bf16[4,2,3,16,2048]{4,3,2,1,0:T(8,128)(2,1)} %slice.95), channel_id=1, source_target_pairs={{0,64},{32,96},{64,0},{96,32},{1,65},{33,97},{65,1},{97,33},{2,66}... | collective-permute-start | bytes 4718600 | tf_op jit(solution)/shard_map/ppermute | solution.py:35
  25.2 2.0 %collective-permute-start.7 = (bf16[3,2,3,16,2048]{4,3,2,1,0:T(8,128)(2,1)}, bf16[3,2,3,16,2048]{4,3,2,1,0:T(8,128)(2,1)}, u32[]{:S(2)}, u32[]{:S(2)}) collective-permute-start(bf16[3,2,3,16,2048]{4,3,2,1,0:T(8,128)(2,1)} %slice.89), channel_id=1, source_target_pairs={{0,64},{32,96},{64,0},{96,32},{1,65},{33,97},{65,1},{97,33},{2,66}... | collective-permute-start | bytes 3538952 | tf_op jit(solution)/shard_map/ppermute | solution.py:35
  35.6 23.2 %collective-permute-done.18.high_ref = bf16[4,2,3,16,2048]{4,3,2,1,0:T(8,128)(2,1)} collective-permute-done((bf16[4,2,3,16,2048]{4,3,2,1,0:T(8,128)(2,1)}, bf16[4,2,3,16,2048]{4,3,2,1,0:T(8,128)(2,1)}, u32[]{:S(2)}, u32[]{:S(2)}) %collective-permute-start.18) | collective-permute-done | bytes 1572896 | tf_op jit(solution)/shard_map/ppermute | solution.py:35
  59.6 12.4 %contract.7 = (f32[4,64,128]{2,1,0:T(8,128)S(1)}, f32[4,64,128]{2,1,0:T(8,128)S(1)}, f32[4,64,128]{2,1,0:T(8,128)S(1)}, f32[4,64,128]{2,1,0:T(8,128)S(1)}) custom-call(s32[8,128]{1,0:T(8,128)S(1)} %broadcast_in_dim.39.pat_ref, f32[8,8,2048]{2,1,0:T(8,128)S(1)} %broadcast_in_dim.36.cos_ref, f32[8,8,2048]{2,1,0:T(8,128)S(1)} %broadcast_in_dim.37.sin_ref, ...), custom_call_target="tpu_custom_call" | custom-call | flops 3221225472 | bytes 12582912 | tf_op jit(solution)/shard_map/contract/pallas_call | solution.py:169
  72.0 2.9 %collective-permute-start.21 = (f32[4,64,128]{2,1,0:T(8,128)S(1)}, f32[4,64,128]{2,1,0:T(8,128)S(1)}, u32[]{:S(2)}, u32[]{:S(2)}) collective-permute-start(f32[4,64,128]{2,1,0:T(8,128)S(1)} %get-tuple-element.36), channel_id=1, source_target_pairs={{0,3},{1,0},{2,1},{3,2},{4,7},{5,4},{6,5},{7,6},{8,11},{9,8},{10,9... | collective-permute-start | bytes 393224 | tf_op jit(solution)/shard_map/ppermute | solution.py:31
  74.9 17.5 %collective-permute-done.7.high_ref = bf16[3,2,3,16,2048]{4,3,2,1,0:T(8,128)(2,1)} collective-permute-done((bf16[3,2,3,16,2048]{4,3,2,1,0:T(8,128)(2,1)}, bf16[3,2,3,16,2048]{4,3,2,1,0:T(8,128)(2,1)}, u32[]{:S(2)}, u32[]{:S(2)}) %collective-permute-start.7) | collective-permute-done | bytes 1179680 | tf_op jit(solution)/shard_map/ppermute | solution.py:35
  92.3 9.6 %contract.5 = (f32[3,64,128]{2,1,0:T(8,128)S(1)}, f32[3,64,128]{2,1,0:T(8,128)S(1)}, f32[3,64,128]{2,1,0:T(8,128)S(1)}, f32[3,64,128]{2,1,0:T(8,128)S(1)}) custom-call(s32[8,128]{1,0:T(8,128)S(1)} %broadcast_in_dim.39.pat_ref, f32[8,8,2048]{2,1,0:T(8,128)S(1)} %broadcast_in_dim.36.cos_ref, f32[8,8,2048]{2,1,0:T(8,128)S(1)} %broadcast_in_dim.37.sin_ref, ...), custom_call_target="tpu_custom_call" | custom-call | flops 2415919104 | bytes 9437184 | tf_op jit(solution)/shard_map/contract/pallas_call | solution.py:169
  101.9 2.8 %collective-permute-start.10 = (f32[3,64,128]{2,1,0:T(8,128)S(1)}, f32[3,64,128]{2,1,0:T(8,128)S(1)}, u32[]{:S(2)}, u32[]{:S(2)}) collective-permute-start(f32[3,64,128]{2,1,0:T(8,128)S(1)} %get-tuple-element.28), channel_id=1, source_target_pairs={{0,3},{1,0},{2,1},{3,2},{4,7},{5,4},{6,5},{7,6},{8,11},{9,8},{10,9... | collective-permute-start | bytes 294920 | tf_op jit(solution)/shard_map/ppermute | solution.py:31
  106.4 23.4 %contract.4 = (f32[8,64,128]{2,1,0:T(8,128)S(1)}, f32[8,64,128]{2,1,0:T(8,128)S(1)}, f32[8,64,128]{2,1,0:T(8,128)S(1)}, f32[8,64,128]{2,1,0:T(8,128)S(1)}) custom-call(s32[8,128]{1,0:T(8,128)S(1)} %broadcast_in_dim.17.pat_ref, f32[8,8,2048]{2,1,0:T(8,128)S(1)} %broadcast_in_dim.36.cos_ref, f32[8,8,2048]{2,1,0:T(8,128)S(1)} %broadcast_in_dim.37.sin_ref, ...), custom_call_target="tpu_custom_call" | custom-call | flops 6442450944 | bytes 25165824 | tf_op jit(solution)/shard_map/contract/pallas_call | solution.py:169
  129.9 1.9 %collective-permute-start.20 = (f32[4,64,128]{2,1,0:T(8,128)S(1)}, f32[4,64,128]{2,1,0:T(8,128)S(1)}, u32[]{:S(2)}, u32[]{:S(2)}) collective-permute-start(f32[4,64,128]{2,1,0:T(8,128)S(1)} %get-tuple-element.35), channel_id=1, source_target_pairs={{0,2},{1,3},{2,0},{3,1},{4,6},{5,7},{6,4},{7,5},{8,10},{9,11},{10,... | collective-permute-start | bytes 393224 | tf_op jit(solution)/shard_map/ppermute | solution.py:31
  131.8 3.7 %contract.6 = (f32[1,64,128]{2,1,0:T(8,128)S(1)}, f32[1,64,128]{2,1,0:T(8,128)S(1)}, f32[1,64,128]{2,1,0:T(8,128)S(1)}, f32[1,64,128]{2,1,0:T(8,128)S(1)}) custom-call(s32[8,128]{1,0:T(8,128)S(1)} %broadcast_in_dim.39.pat_ref, f32[8,8,2048]{2,1,0:T(8,128)S(1)} %broadcast_in_dim.36.cos_ref, f32[8,8,2048]{2,1,0:T(8,128)S(1)} %broadcast_in_dim.37.sin_ref, ...), custom_call_target="tpu_custom_call" | custom-call | flops 805306368 | bytes 3145728 | tf_op jit(solution)/shard_map/contract/pallas_call | solution.py:169
  137.0 1.9 %collective-permute-start.3 = (f32[8,64,128]{2,1,0:T(8,128)S(1)}, f32[8,64,128]{2,1,0:T(8,128)S(1)}, u32[]{:S(2)}, u32[]{:S(2)}) collective-permute-start(f32[8,64,128]{2,1,0:T(8,128)S(1)} %get-tuple-element.24), channel_id=1, source_target_pairs={{0,3},{1,0},{2,1},{3,2},{4,7},{5,4},{6,5},{7,6},{8,11},{9,8},{10,9... | collective-permute-start | bytes 786440 | tf_op jit(solution)/shard_map/ppermute | solution.py:31
  141.2 1.9 %collective-permute-start.17 = (f32[1,64,128]{2,1,0:T(8,128)S(1)}, f32[1,64,128]{2,1,0:T(8,128)S(1)}, u32[]{:S(2)}, u32[]{:S(2)}) collective-permute-start(f32[1,64,128]{2,1,0:T(8,128)S(1)} %get-tuple-element.32), channel_id=1, source_target_pairs={{0,3},{1,0},{2,1},{3,2},{4,7},{5,4},{6,5},{7,6},{8,11},{9,8},{10,9... | collective-permute-start | bytes 98312 | tf_op jit(solution)/shard_map/ppermute | solution.py:31
  144.6 5.4 %collective-permute-done.3 = f32[8,64,128]{2,1,0:T(8,128)S(1)} collective-permute-done((f32[8,64,128]{2,1,0:T(8,128)S(1)}, f32[8,64,128]{2,1,0:T(8,128)S(1)}, u32[]{:S(2)}, u32[]{:S(2)}) %collective-permute-start.3) | collective-permute-done | bytes 262176 | tf_op jit(solution)/shard_map/ppermute | solution.py:31
  150.0 3.0 %collective-permute-start.24 = (f32[1,64,128]{2,1,0:T(8,128)S(1)}, f32[1,64,128]{2,1,0:T(8,128)S(1)}, u32[]{:S(2)}, u32[]{:S(2)}) collective-permute-start(f32[1,64,128]{2,1,0:T(8,128)S(1)} %get-tuple-element.41), channel_id=1, source_target_pairs={{0,24},{1,25},{2,26},{3,27},{4,28},{5,29},{6,30},{7,31},{8,0},{9,1... | collective-permute-start | bytes 98312 | tf_op jit(solution)/shard_map/ppermute | solution.py:31
  153.4 3.2 %collective-permute-start.23 = (f32[1,64,128]{2,1,0:T(8,128)S(1)}, f32[1,64,128]{2,1,0:T(8,128)S(1)}, u32[]{:S(2)}, u32[]{:S(2)}) collective-permute-start(f32[1,64,128]{2,1,0:T(8,128)S(1)} %get-tuple-element.40), channel_id=1, source_target_pairs={{0,16},{1,17},{2,18},{3,19},{4,20},{5,21},{6,22},{7,23},{8,24},{9,... | collective-permute-start | bytes 98312 | tf_op jit(solution)/shard_map/ppermute | solution.py:31
  159.0 3.1 %collective-permute-start.5 = (f32[2,64,128]{2,1,0:T(8,128)S(1)}, f32[2,64,128]{2,1,0:T(8,128)S(1)}, u32[]{:S(2)}, u32[]{:S(2)}) collective-permute-start(f32[2,64,128]{2,1,0:T(8,128)S(1)} %get-tuple-element.37), channel_id=1, source_target_pairs={{0,16},{1,17},{2,18},{3,19},{4,20},{5,21},{6,22},{7,23},{8,24},{9,... | collective-permute-start | bytes 196616 | tf_op jit(solution)/shard_map/ppermute | solution.py:31
  166.2 3.0 %collective-permute-start.12 = (f32[1,64,128]{2,1,0:T(8,128)S(1)}, f32[1,64,128]{2,1,0:T(8,128)S(1)}, u32[]{:S(2)}, u32[]{:S(2)}) collective-permute-start(f32[1,64,128]{2,1,0:T(8,128)S(1)} %get-tuple-element.43), channel_id=1, source_target_pairs={{0,16},{1,17},{2,18},{3,19},{4,20},{5,21},{6,22},{7,23},{8,24},{9,... | collective-permute-start | bytes 98312 | tf_op jit(solution)/shard_map/ppermute | solution.py:31
  169.2 3.8 %collective-permute-start.25 = (f32[2,64,128]{2,1,0:T(8,128)S(1)}, f32[2,64,128]{2,1,0:T(8,128)S(1)}, u32[]{:S(2)}, u32[]{:S(2)}) collective-permute-start(f32[2,64,128]{2,1,0:T(8,128)S(1)} %pad_maximum_fusion), channel_id=1, source_target_pairs={{0,4},{1,5},{2,6},{3,7},{4,0},{5,1},{6,2},{7,3},{8,12},{9,13},{10,... | collective-permute-start | bytes 196616 | tf_op jit(solution)/shard_map/ppermute | solution.py:31
  173.0 2.2 %collective-permute-done.25 = f32[2,64,128]{2,1,0:T(8,128)S(1)} collective-permute-done((f32[2,64,128]{2,1,0:T(8,128)S(1)}, f32[2,64,128]{2,1,0:T(8,128)S(1)}, u32[]{:S(2)}, u32[]{:S(2)}) %collective-permute-start.25) | collective-permute-done | bytes 65568 | tf_op jit(solution)/shard_map/ppermute | solution.py:31
  177.1 1.6 assemble.1
  (75 shorter events, 28.0 us)
Async XLA Ops:
  18.0 40.8 %collective-permute-start = (bf16[8,3,128,2048]{3,2,1,0:T(8,128)(2,1)}, bf16[8,3,128,2048]{3,2,1,0:T(8,128)(2,1)}, u32[]{:S(2)}, u32[]{:S(2)}) collective-permute-start(bf16[8,3,128,2048]{3,2,1,0:T(8,128)(2,1)} %bitcast.own_ref), channel_id=1, source_target_pairs={{0,32},{32,0},{64,96},{96,64},{1,33},{33,1},{65,97},{97,65},{2,34}... | collective-permute-start | bytes 37748744 | tf_op jit(solution)/shard_map/ppermute | solution.py:35
  21.2 37.6 %collective-permute-start.18 = (bf16[4,2,3,16,2048]{4,3,2,1,0:T(8,128)(2,1)}, bf16[4,2,3,16,2048]{4,3,2,1,0:T(8,128)(2,1)}, u32[]{:S(2)}, u32[]{:S(2)}) collective-permute-start(bf16[4,2,3,16,2048]{4,3,2,1,0:T(8,128)(2,1)} %slice.95), channel_id=1, source_target_pairs={{0,64},{32,96},{64,0},{96,32},{1,65},{33,97},{65,1},{97,33},{2,66}... | collective-permute-start | bytes 4718600 | tf_op jit(solution)/shard_map/ppermute | solution.py:35
  24.0 105.9 %collective-permute-start.14 = (bf16[1,2,3,16,2048]{4,3,2,1,0:T(8,128)(2,1)}, bf16[1,2,3,16,2048]{4,3,2,1,0:T(8,128)(2,1)S(1)}, u32[]{:S(2)}, u32[]{:S(2)}) collective-permute-start(bf16[1,2,3,16,2048]{4,3,2,1,0:T(8,128)(2,1)} %slice.93), channel_id=1, source_target_pairs={{0,64},{32,96},{64,0},{96,32},{1,65},{33,97},{65,1},{97,33},{2,66}... | collective-permute-start | bytes 1179656 | tf_op jit(solution)/shard_map/ppermute | solution.py:35
  25.2 67.1 %collective-permute-start.7 = (bf16[3,2,3,16,2048]{4,3,2,1,0:T(8,128)(2,1)}, bf16[3,2,3,16,2048]{4,3,2,1,0:T(8,128)(2,1)}, u32[]{:S(2)}, u32[]{:S(2)}) collective-permute-start(bf16[3,2,3,16,2048]{4,3,2,1,0:T(8,128)(2,1)} %slice.89), channel_id=1, source_target_pairs={{0,64},{32,96},{64,0},{96,32},{1,65},{33,97},{65,1},{97,33},{2,66}... | collective-permute-start | bytes 3538952 | tf_op jit(solution)/shard_map/ppermute | solution.py:35
  72.0 67.9 %collective-permute-start.21 = (f32[4,64,128]{2,1,0:T(8,128)S(1)}, f32[4,64,128]{2,1,0:T(8,128)S(1)}, u32[]{:S(2)}, u32[]{:S(2)}) collective-permute-start(f32[4,64,128]{2,1,0:T(8,128)S(1)} %get-tuple-element.36), channel_id=1, source_target_pairs={{0,3},{1,0},{2,1},{3,2},{4,7},{5,4},{6,5},{7,6},{8,11},{9,8},{10,9... | collective-permute-start | bytes 393224 | tf_op jit(solution)/shard_map/ppermute | solution.py:31
  101.9 33.6 %collective-permute-start.10 = (f32[3,64,128]{2,1,0:T(8,128)S(1)}, f32[3,64,128]{2,1,0:T(8,128)S(1)}, u32[]{:S(2)}, u32[]{:S(2)}) collective-permute-start(f32[3,64,128]{2,1,0:T(8,128)S(1)} %get-tuple-element.28), channel_id=1, source_target_pairs={{0,3},{1,0},{2,1},{3,2},{4,7},{5,4},{6,5},{7,6},{8,11},{9,8},{10,9... | collective-permute-start | bytes 294920 | tf_op jit(solution)/shard_map/ppermute | solution.py:31
  104.7 32.2 %collective-permute-start.9 = (f32[3,64,128]{2,1,0:T(8,128)S(1)}, f32[3,64,128]{2,1,0:T(8,128)S(1)}, u32[]{:S(2)}, u32[]{:S(2)}) collective-permute-start(f32[3,64,128]{2,1,0:T(8,128)S(1)} %get-tuple-element.27), channel_id=1, source_target_pairs={{0,2},{1,3},{2,0},{3,1},{4,6},{5,7},{6,4},{7,5},{8,10},{9,11},{10,... | collective-permute-start | bytes 294920 | tf_op jit(solution)/shard_map/ppermute | solution.py:31
  105.5 33.3 %collective-permute-start.8 = (f32[3,64,128]{2,1,0:T(8,128)S(1)}, f32[3,64,128]{2,1,0:T(8,128)S(1)}, u32[]{:S(2)}, u32[]{:S(2)}) collective-permute-start(f32[3,64,128]{2,1,0:T(8,128)S(1)} %get-tuple-element.26), channel_id=1, source_target_pairs={{0,1},{1,2},{2,3},{3,0},{4,5},{5,6},{6,7},{7,4},{8,9},{9,10},{10,1... | collective-permute-start | bytes 294920 | tf_op jit(solution)/shard_map/ppermute | solution.py:31
  129.9 11.4 %collective-permute-start.20 = (f32[4,64,128]{2,1,0:T(8,128)S(1)}, f32[4,64,128]{2,1,0:T(8,128)S(1)}, u32[]{:S(2)}, u32[]{:S(2)}) collective-permute-start(f32[4,64,128]{2,1,0:T(8,128)S(1)} %get-tuple-element.35), channel_id=1, source_target_pairs={{0,2},{1,3},{2,0},{3,1},{4,6},{5,7},{6,4},{7,5},{8,10},{9,11},{10,... | collective-permute-start | bytes 393224 | tf_op jit(solution)/shard_map/ppermute | solution.py:31
  135.5 7.6 %collective-permute-start.19 = (f32[4,64,128]{2,1,0:T(8,128)S(1)}, f32[4,64,128]{2,1,0:T(8,128)S(1)}, u32[]{:S(2)}, u32[]{:S(2)}) collective-permute-start(f32[4,64,128]{2,1,0:T(8,128)S(1)} %get-tuple-element.34), channel_id=1, source_target_pairs={{0,1},{1,2},{2,3},{3,0},{4,5},{5,6},{6,7},{7,4},{8,9},{9,10},{10,1... | collective-permute-start | bytes 393224 | tf_op jit(solution)/shard_map/ppermute | solution.py:31
  137.0 13.0 %collective-permute-start.3 = (f32[8,64,128]{2,1,0:T(8,128)S(1)}, f32[8,64,128]{2,1,0:T(8,128)S(1)}, u32[]{:S(2)}, u32[]{:S(2)}) collective-permute-start(f32[8,64,128]{2,1,0:T(8,128)S(1)} %get-tuple-element.24), channel_id=1, source_target_pairs={{0,3},{1,0},{2,1},{3,2},{4,7},{5,4},{6,5},{7,6},{8,11},{9,8},{10,9... | collective-permute-start | bytes 786440 | tf_op jit(solution)/shard_map/ppermute | solution.py:31
  138.9 14.2 %collective-permute-start.2 = (f32[8,64,128]{2,1,0:T(8,128)S(1)}, f32[8,64,128]{2,1,0:T(8,128)S(1)}, u32[]{:S(2)}, u32[]{:S(2)}) collective-permute-start(f32[8,64,128]{2,1,0:T(8,128)S(1)} %get-tuple-element.23), channel_id=1, source_target_pairs={{0,2},{1,3},{2,0},{3,1},{4,6},{5,7},{6,4},{7,5},{8,10},{9,11},{10,... | collective-permute-start | bytes 786440 | tf_op jit(solution)/shard_map/ppermute | solution.py:31
  139.8 13.5 %collective-permute-start.1 = (f32[8,64,128]{2,1,0:T(8,128)S(1)}, f32[8,64,128]{2,1,0:T(8,128)S(1)}, u32[]{:S(2)}, u32[]{:S(2)}) collective-permute-start(f32[8,64,128]{2,1,0:T(8,128)S(1)} %get-tuple-element.22), channel_id=1, source_target_pairs={{0,1},{1,2},{2,3},{3,0},{4,5},{5,6},{6,7},{7,4},{8,9},{9,10},{10,1... | collective-permute-start | bytes 786440 | tf_op jit(solution)/shard_map/ppermute | solution.py:31
  141.2 24.9 %collective-permute-start.17 = (f32[1,64,128]{2,1,0:T(8,128)S(1)}, f32[1,64,128]{2,1,0:T(8,128)S(1)}, u32[]{:S(2)}, u32[]{:S(2)}) collective-permute-start(f32[1,64,128]{2,1,0:T(8,128)S(1)} %get-tuple-element.32), channel_id=1, source_target_pairs={{0,3},{1,0},{2,1},{3,2},{4,7},{5,4},{6,5},{7,6},{8,11},{9,8},{10,9... | collective-permute-start | bytes 98312 | tf_op jit(solution)/shard_map/ppermute | solution.py:31
  143.2 26.0 %collective-permute-start.16 = (f32[1,64,128]{2,1,0:T(8,128)S(1)}, f32[1,64,128]{2,1,0:T(8,128)S(1)}, u32[]{:S(2)}, u32[]{:S(2)}) collective-permute-start(f32[1,64,128]{2,1,0:T(8,128)S(1)} %get-tuple-element.31), channel_id=1, source_target_pairs={{0,2},{1,3},{2,0},{3,1},{4,6},{5,7},{6,4},{7,5},{8,10},{9,11},{10,... | collective-permute-start | bytes 98312 | tf_op jit(solution)/shard_map/ppermute | solution.py:31
  150.0 6.7 %collective-permute-start.24 = (f32[1,64,128]{2,1,0:T(8,128)S(1)}, f32[1,64,128]{2,1,0:T(8,128)S(1)}, u32[]{:S(2)}, u32[]{:S(2)}) collective-permute-start(f32[1,64,128]{2,1,0:T(8,128)S(1)} %get-tuple-element.41), channel_id=1, source_target_pairs={{0,24},{1,25},{2,26},{3,27},{4,28},{5,29},{6,30},{7,31},{8,0},{9,1... | collective-permute-start | bytes 98312 | tf_op jit(solution)/shard_map/ppermute | solution.py:31
  153.4 5.7 %collective-permute-start.23 = (f32[1,64,128]{2,1,0:T(8,128)S(1)}, f32[1,64,128]{2,1,0:T(8,128)S(1)}, u32[]{:S(2)}, u32[]{:S(2)}) collective-permute-start(f32[1,64,128]{2,1,0:T(8,128)S(1)} %get-tuple-element.40), channel_id=1, source_target_pairs={{0,16},{1,17},{2,18},{3,19},{4,20},{5,21},{6,22},{7,23},{8,24},{9,... | collective-permute-start | bytes 98312 | tf_op jit(solution)/shard_map/ppermute | solution.py:31
  158.1 5.5 %collective-permute-start.4 = (f32[2,64,128]{2,1,0:T(8,128)S(1)}, f32[2,64,128]{2,1,0:T(8,128)S(1)}, u32[]{:S(2)}, u32[]{:S(2)}) collective-permute-start(f32[2,64,128]{2,1,0:T(8,128)S(1)} %get-tuple-element.39), channel_id=1, source_target_pairs={{0,8},{1,9},{2,10},{3,11},{4,12},{5,13},{6,14},{7,15},{8,16},{9,17... | collective-permute-start | bytes 196616 | tf_op jit(solution)/shard_map/ppermute | solution.py:31
  159.0 5.8 %collective-permute-start.5 = (f32[2,64,128]{2,1,0:T(8,128)S(1)}, f32[2,64,128]{2,1,0:T(8,128)S(1)}, u32[]{:S(2)}, u32[]{:S(2)}) collective-permute-start(f32[2,64,128]{2,1,0:T(8,128)S(1)} %get-tuple-element.37), channel_id=1, source_target_pairs={{0,16},{1,17},{2,18},{3,19},{4,20},{5,21},{6,22},{7,23},{8,24},{9,... | collective-permute-start | bytes 196616 | tf_op jit(solution)/shard_map/ppermute | solution.py:31
  162.2 10.8 %collective-permute-start.15 = (f32[1,64,128]{2,1,0:T(8,128)S(1)}, f32[1,64,128]{2,1,0:T(8,128)S(1)}, u32[]{:S(2)}, u32[]{:S(2)}) collective-permute-start(f32[1,64,128]{2,1,0:T(8,128)S(1)} %get-tuple-element.30), channel_id=1, source_target_pairs={{0,1},{1,2},{2,3},{3,0},{4,5},{5,6},{6,7},{7,4},{8,9},{9,10},{10,1... | collective-permute-start | bytes 98312 | tf_op jit(solution)/shard_map/ppermute | solution.py:31
  163.6 9.4 %collective-permute-start.13 = (f32[1,64,128]{2,1,0:T(8,128)S(1)}, f32[1,64,128]{2,1,0:T(8,128)S(1)}, u32[]{:S(2)}, u32[]{:S(2)}) collective-permute-start(f32[1,64,128]{2,1,0:T(8,128)S(1)} %get-tuple-element.44), channel_id=1, source_target_pairs={{0,24},{1,25},{2,26},{3,27},{4,28},{5,29},{6,30},{7,31},{8,0},{9,1... | collective-permute-start | bytes 98312 | tf_op jit(solution)/shard_map/ppermute | solution.py:31
  164.8 8.2 %collective-permute-start.11 = (f32[1,64,128]{2,1,0:T(8,128)S(1)}, f32[1,64,128]{2,1,0:T(8,128)S(1)}, u32[]{:S(2)}, u32[]{:S(2)}) collective-permute-start(f32[1,64,128]{2,1,0:T(8,128)S(1)} %get-tuple-element.45), channel_id=1, source_target_pairs={{0,8},{1,9},{2,10},{3,11},{4,12},{5,13},{6,14},{7,15},{8,16},{9,17... | collective-permute-start | bytes 98312 | tf_op jit(solution)/shard_map/ppermute | solution.py:31
  166.2 6.8 %collective-permute-start.12 = (f32[1,64,128]{2,1,0:T(8,128)S(1)}, f32[1,64,128]{2,1,0:T(8,128)S(1)}, u32[]{:S(2)}, u32[]{:S(2)}) collective-permute-start(f32[1,64,128]{2,1,0:T(8,128)S(1)} %get-tuple-element.43), channel_id=1, source_target_pairs={{0,16},{1,17},{2,18},{3,19},{4,20},{5,21},{6,22},{7,23},{8,24},{9,... | collective-permute-start | bytes 98312 | tf_op jit(solution)/shard_map/ppermute | solution.py:31
  169.2 6.0 %collective-permute-start.25 = (f32[2,64,128]{2,1,0:T(8,128)S(1)}, f32[2,64,128]{2,1,0:T(8,128)S(1)}, u32[]{:S(2)}, u32[]{:S(2)}) collective-permute-start(f32[2,64,128]{2,1,0:T(8,128)S(1)} %pad_maximum_fusion), channel_id=1, source_target_pairs={{0,4},{1,5},{2,6},{3,7},{4,0},{5,1},{6,2},{7,3},{8,12},{9,13},{10,... | collective-permute-start | bytes 196616 | tf_op jit(solution)/shard_map/ppermute | solution.py:31
  (6 other events, 64.4 us)

commit v2 on v1

v2 whole, which is shorter than its diff:
```python
import functools
import math

import jax
import jax.numpy as jnp
from jax import lax
from jax.experimental import pallas as pl
from jax.experimental.pallas import tpu as pltpu
from jax.sharding import PartitionSpec as P

NX, NY, NZ = 4, 4, 2
SLOTS = NY * NZ
PARTNER = ((0, 1, 2, 3), (2, 3, 0, 1), (3, 2, 1, 0), (1, 0, 3, 2))
OWNERS = (2, 1, 3, 0)


def coords():
    site = lax.axis_index("site")
    return lax.rem(site, 4), lax.div(site, 8), lax.rem(lax.div(site, 4), 2)


def site_of(y, z, x):
    return ((y % NY) * NZ + z % NZ) * NX + x % NX


def trade(block, ymask, zmask, xmask):
    route = [
        (site_of(y, z, x), site_of(y ^ ymask, z ^ zmask, x ^ xmask))
        for y in range(NY)
        for z in range(NZ)
        for x in range(NX)
    ]
    return lax.ppermute(block, "site", route)


def flip(block, mask):
    return lax.ppermute(block, "mode", [(i, i ^ mask) for i in range(4)])


def slot_of(t, y, z):
    far = (t // 2) ^ y
    place = jnp.where(far == 2, 0, jnp.where(far == 1, 1, jnp.where(far == 3, 2, 3)))
    return jnp.where(t % 2 == z, NY, 0) + place


def time_of(slot, y, z):
    plane = z if slot >= NY else 1 - z
    return 2 * (y ^ OWNERS[slot % NY]) + plane


VMEM = pl.BlockSpec(memory_space=pltpu.VMEM)
STEP = 512
HIGH_LIMIT = 4 * 2**20
LOW_LIMIT = 10 * 2**20
SMALL = pltpu.CompilerParams(vmem_limit_bytes=4 * 2**20)
TOKEN = jax.ShapeDtypeStruct((8, 128), jnp.float32)
TINY = pl.CostEstimate(flops=0, bytes_accessed=0, transcendentals=0)


def whole(shape):
    return pl.BlockSpec(shape, lambda *_: (0,) * len(shape))


def relayout_high_body(in_ref, *refs):
    outs, token_ref, turned_ref = refs[:-2], refs[-2], refs[-1]
    _, y, z = coords()
    token_ref[...] = jnp.zeros_like(token_ref)

    def one(index, carry):
        r, c = lax.div(index, 3), lax.rem(index, 3)
        for j in range(0, in_ref.shape[-1], STEP):
            cut = pl.ds(j, STEP)
            values = in_ref[:, r, c, :, cut].astype(jnp.float32)
            turned_ref[...] = jnp.swapaxes(values, 0, 1).astype(jnp.bfloat16)
            slot = 0
            for out in outs:
                for k in range(out.shape[0]):
                    out[k, r, c, :, cut] = turned_ref[time_of(slot, y, z)]
                    slot += 1
        return carry

    lax.fori_loop(0, 6, one, 0)


def relayout_high(high, sizes):
    rows, two, colours, slices, count = high.shape
    return pl.pallas_call(
        relayout_high_body,
        in_specs=[VMEM],
        out_specs=[VMEM] * (len(sizes) + 1),
        out_shape=[
            jax.ShapeDtypeStruct((n, two, colours, rows, count), jnp.bfloat16) for n in sizes
        ]
        + [jax.ShapeDtypeStruct((8, 128), jnp.float32)],
        scratch_shapes=[pltpu.VMEM((slices, rows, STEP), jnp.bfloat16)],
        compiler_params=pltpu.CompilerParams(vmem_limit_bytes=HIGH_LIMIT),
        cost_estimate=TINY,
        name="relayout_high",
    )(high)


def relayout_low_body(in_ref, after_ref, out_ref, token_ref):
    token_ref[...] = jnp.zeros_like(token_ref)
    _, y, z = coords()

    def one(s, carry):
        for j in range(0, in_ref.shape[-1], STEP):
            cut = pl.ds(j, STEP)
            values = in_ref[:, s, 0, 0, :, cut].astype(jnp.float32)
            turned = jnp.swapaxes(values, 0, 1).astype(jnp.bfloat16)
            for t in range(SLOTS):
                out_ref[slot_of(t, y, z), 0, 0, s, :, cut] = turned[t]
        return carry

    lax.fori_loop(0, in_ref.shape[1], one, 0)


def relayout_low(low, token):
    rows, spins, two, colours, slices, count = low.shape
    turned, token = pl.pallas_call(
        relayout_low_body,
        grid=(colours, two),
        in_specs=[
            pl.BlockSpec((rows, spins, 1, 1, slices, count), lambda c, u: (0, 0, u, c, 0, 0)),
            whole((8, 128)),
        ],
        out_specs=[
            pl.BlockSpec((slices, 1, 1, spins, rows, count), lambda c, u: (0, c, u, 0, 0, 0)),
            whole((8, 128)),
        ],
        out_shape=[
            jax.ShapeDtypeStruct((slices, colours, two, spins, rows, count), jnp.bfloat16),
            jax.ShapeDtypeStruct((8, 128), jnp.float32),
        ],
        compiler_params=pltpu.CompilerParams(vmem_limit_bytes=LOW_LIMIT),
        cost_estimate=TINY,
        name="relayout_low",
    )(low, token)
    return turned.reshape(slices, colours, two * spins * rows, count), token


def contract_body(by_part, added, pat_ref, cos_ref, sin_ref, own_ref, oth_ref, *refs):
    highs, adds, outs = refs[:2], refs[2 : 2 + added], refs[3 + added : -2]
    token_ref, acc_ref = refs[-2:]
    token_ref[...] = jnp.zeros_like(token_ref)
    n_moms, count = cos_ref.shape
    x, _, _ = coords()
    acc_ref[...] = jnp.zeros_like(acc_ref)

    def one(colour, carry):
        total = None
        for j in range(0, count, STEP):
            cut = pl.ds(j, STEP)
            rows = []
            for high_ref in highs:
                real = high_ref[0, 0, colour, :, cut].astype(jnp.float32)
                imag = high_ref[0, 1, colour, :, cut].astype(jnp.float32)
                reals, imags = [], []
                for p in range(n_moms):
                    cosine = cos_ref[p : p + 1, cut]
                    sine = sin_ref[p : p + 1, cut]
                    reals.append((real * cosine - imag * sine).astype(jnp.bfloat16))
                    imags.append((real * sine + imag * cosine).astype(jnp.bfloat16))
                rows += reals + imags
            phased = jnp.concatenate(rows, 0)
            low = jnp.concatenate([own_ref[0, colour, :, cut], oth_ref[0, colour, :, cut]], 0)
            part = lax.dot_general(
                low, phased, (((1,), (1,)), ((), ())), preferred_element_type=jnp.float32
            )
            total = part if total is None else total + part
        acc_ref[...] += total
        return carry

    lax.fori_loop(0, 3, one, 0)
    half = 128
    for block in range(2):
        base = block * 256
        pattern = pat_ref[0:1, block * half : block * half + half]
        is_spin = [jnp.broadcast_to(pattern == a, (16, half)) for a in range(4)]
        low_pair = pattern < 2
        odd = jnp.logical_or(pattern == 1, pattern == 3)
        mesons = [[], [], [], []]
        for owner in range(2):
            over = []
            for s in range(4):
                u0 = slice(owner * 128 + s * 16, owner * 128 + s * 16 + 16)
                u1 = slice(owner * 128 + s * 16 + 64, owner * 128 + s * 16 + 80)
                r0, r1 = slice(base, base + half), slice(base + half, base + 2 * half)
                over.append((acc_ref[u0, r0] + acc_ref[u1, r1], acc_ref[u1, r0] - acc_ref[u0, r1]))
            for g in range(4):
                picked = []
                for u in range(2):
                    value = over[PARTNER[g][3]][u]
                    for a in range(3):
                        value = jnp.where(is_spin[a], over[PARTNER[g][a]][u], value)
                    picked.append(value)
                re, im = picked
                if g == 2:
                    re, im = jnp.where(low_pair, -im, im), jnp.where(low_pair, re, -re)
                if g == 3:
                    re, im = jnp.where(odd, re, -re), jnp.where(odd, im, -im)
                mesons[g] += [re, im]
        stacked = [jnp.concatenate(m, 0) for m in mesons]
        lane = lax.broadcasted_iota(jnp.int32, stacked[0].shape, 1) // 32
        for k in range(NX):
            group = x ^ OWNERS[k]
            result = None
            for g in range(4):
                turned = pltpu.roll(stacked[g], lax.rem(g - group + NX, NX) * 32, 1)
                result = turned if result is None else jnp.where(lane == g, turned, result)
            for add in adds:
                result = result + add[k, block].astype(jnp.float32)
            if by_part:
                outs[k // 2][k % 2, 0, block] = result.astype(outs[k // 2].dtype)
            else:
                outs[0][0, k, block] = result.astype(outs[0].dtype)


def contract(tables, low_own, low_oth, own, received, first, by_part, sent, after, adds=()):
    colours, rows, count = low_own.shape[1:]
    number = own.shape[0]
    unit = (2, 64, 128)
    if by_part:
        shapes = [
            jax.ShapeDtypeStruct((2, number) + unit, sent),
            jax.ShapeDtypeStruct((2, number) + unit, jnp.float32),
        ]
        out_specs = [pl.BlockSpec((2, 1) + unit, lambda i: (0, i, 0, 0, 0))] * 2
    else:
        shapes = [jax.ShapeDtypeStruct((number, NX) + unit, sent)]
        out_specs = [pl.BlockSpec((1, NX) + unit, lambda i: (i, 0, 0, 0, 0))]
    high_spec = pl.BlockSpec((1, 2, colours, 16, count), lambda i: (i, 0, 0, 0, 0))
    low_spec = pl.BlockSpec((1, colours, rows, count), lambda i: (first + i, 0, 0, 0))
    return pl.pallas_call(
        functools.partial(contract_body, by_part, len(adds)),
        grid=(number,),
        in_specs=[whole(t.shape) for t in tables]
        + [low_spec, low_spec, high_spec, high_spec]
        + [whole(a.shape) for a in adds]
        + [whole((8, 128))],
        out_specs=out_specs + [whole((8, 128))],
        out_shape=shapes + [TOKEN],
        scratch_shapes=[pltpu.VMEM((256, 512), jnp.float32)],
        compiler_params=pltpu.CompilerParams(vmem_limit_bytes=14 * 2**20),
        cost_estimate=TINY,
        name=f"contract_{first}_{number}",
    )(*tables, low_own, low_oth, own, received, *adds, after)


def fold_body(axis, kept_ref, got_ref, after_ref, first_ref, second_ref, token_ref):
    half = kept_ref.shape[axis] // 2
    for out_ref, cut in ((first_ref, slice(0, half)), (second_ref, slice(half, 2 * half))):
        index = (slice(None),) * axis + (cut,)
        total = kept_ref[index] + got_ref[index].astype(jnp.float32)
        out_ref[...] = total.astype(out_ref.dtype)
    token_ref[...] = jnp.zeros_like(token_ref)


def fold(kept, got, axis, sent, after):
    shape = kept.shape[:axis] + (kept.shape[axis] // 2,) + kept.shape[axis + 1 :]
    return pl.pallas_call(
        functools.partial(fold_body, axis),
        in_specs=[VMEM] * 3,
        out_specs=[VMEM] * 3,
        out_shape=[
            jax.ShapeDtypeStruct(shape, sent),
            jax.ShapeDtypeStruct(shape, jnp.float32),
            TOKEN,
        ],
        compiler_params=SMALL,
        cost_estimate=TINY,
        name="fold",
    )(kept, got, after)


def finish_body(kept_ref, last_ref, across_ref, mine_ref, other_ref):
    for out_ref, rows in ((mine_ref, slice(0, 32)), (other_ref, slice(32, 64))):
        out_ref[...] = kept_ref[0, :, rows] + last_ref[0, :, rows] + across_ref[0, :, rows]


def finish(kept, last, across):
    return pl.pallas_call(
        finish_body,
        in_specs=[VMEM] * 3,
        out_specs=[VMEM] * 2,
        out_shape=[jax.ShapeDtypeStruct((2, 32, 128), jnp.float32)] * 2,
        compiler_params=SMALL,
        cost_estimate=TINY,
        name="finish",
    )(kept, last, across)


def assemble_body(mine_ref, other_ref, out_ref):
    mode = lax.axis_index("mode")
    blocks = [mode, mode ^ 2, mode ^ 1, mode ^ 3]
    lane = lax.broadcasted_iota(jnp.int32, (32, 128), 1) // 16
    held = [mine_ref[0], mine_ref[1], other_ref[0], other_ref[1]]
    for g in range(4):
        for p in range(2):
            result = None
            for values, block in zip(held, blocks):
                shift = lax.rem(block * 16 - (g * 32 + p * 16) + 128, 128)
                turned = pltpu.roll(values, shift, 1)
                result = turned if result is None else jnp.where(lane == block, turned, result)
            for u in range(2):
                out_ref[g, u, p] = result[u * 16 : u * 16 + 16, :64]


def assemble(pieces):
    return pl.pallas_call(
        assemble_body,
        out_shape=jax.ShapeDtypeStruct((4, 2, 2, 16, 64), jnp.float32),
        compiler_params=SMALL,
        cost_estimate=TINY,
        name="assemble",
    )(*pieces)


def phase_tables(momenta, first_site, count):
    sites = first_site + jnp.arange(count, dtype=jnp.int32)
    coords = jnp.stack([sites % 32, sites // 32 % 32, sites // 1024])
    turns = jnp.sum(momenta[:, :, None] * coords[None, :, :], axis=1)
    angles = turns.astype(jnp.float32) * (2.0 * math.pi / 96.0)
    return jnp.cos(angles), jnp.sin(angles)


def body(low_modes, high_modes, pattern, momenta):
    count = low_modes.shape[-1]
    my_mode = lax.axis_index("mode")
    wide, narrow = jnp.float32, jnp.bfloat16
    *high, token = relayout_high(high_modes, (4, 2, 1, 1))
    arrived = [flip(chunk, 2) for chunk in high]

    low_oth = flip(low_modes, 1)
    low_own, token = relayout_low(low_modes, token)
    low_oth, _ = relayout_low(low_oth, token)
    cosines, sines = phase_tables(momenta, lax.axis_index("site") * count, count)

    def lanes(block):
        part = lax.dynamic_slice_in_dim(pattern, block * 16, 16, 0)
        return jnp.broadcast_to(jnp.tile(part, 8)[None, :], (8, 128))

    tables = (jnp.concatenate([lanes(my_mode), lanes(my_mode ^ 2)], 1), cosines, sines)
    away, far, token = contract(
        tables, low_own, low_oth, high[0], arrived[0], 0, True, narrow, token
    )
    far_got = trade(away, 0, 0, 1)
    away, token = contract(
        tables, low_own, low_oth, high[1], arrived[1], 4, False, narrow, token
    )
    near_got = trade(away, 1, 0, 0)
    away, far, token = fold(far, far_got, 0, narrow, token)
    far_got = trade(away, 0, 0, 3)
    near, token = contract(tables, low_own, low_oth, high[2], arrived[2], 6, False, wide, token)
    near_last = trade((near[0] + near_got[0].astype(wide)).astype(narrow), 3, 0, 0)
    away, far, token = fold(far[0], far_got[0], 0, wide, token)
    far_got = trade(away, 1, 0, 0)
    adds = (near_got[1], near_last)
    away, near, token = contract(
        tables, low_own, low_oth, high[3], arrived[3], 7, True, wide, token, adds
    )
    near_got = trade(away, 0, 0, 1)
    away, far, token = fold(far, far_got, 0, wide, token)
    far_got = trade(away, 3, 0, 0)
    away, near, token = fold(near[:, 0], near_got[:, 0], 0, wide, token)
    near_got = trade(away, 0, 0, 3)
    across = trade(far + far_got, 0, 1, 0)
    mine, other = finish(near, near_got, across)
    pieces = (mine, flip(other, 1))
    return jnp.transpose(assemble(pieces), (0, 1, 2, 4, 3))


def solution(mesh):
    placed = (
        P("mode", None, None, None, None, "site"),
        P("mode", None, None, None, "site"),
        P(),
        P(),
    )
    return jax.shard_map(
        body,
        mesh=mesh,
        in_specs=placed,
        out_specs=P(None, None, "site", None, "mode"),
        check_vma=False,
    )
```

time: 182 us -> 101 us (0.55)
  waiting for transfers between devices: 51.9 us -> 14 us
  Pallas kernels: 66.1 us -> 45.1 us
  starting transfers between devices: 42.2 us -> 21.8 us
    ppermute x5 -> x6, waiting for transfers between devices: 41.3 us -> 5.97 us  [flip(): return lax.ppermute(block, 'mode', [(i, i ^ mask) for i in range(4)])]
    ppermute x22 -> x9, starting transfers between devices: 38.1 us -> 15.9 us  [trade(): return lax.ppermute(block, 'site', route)]
    pallas_call x6 -> x12, Pallas kernels: 64.5 us -> 44.2 us  [the longest x4 23.3 us: contract(): pl.pallas_call(functools.partial(contract_body, by_part, len(adds)), grid...]
    unnamed x6 -> x12, local copies, waits for them, and re-layouts: 4.58 us -> 16.3 us
    broadcast_in_dim x4 -> x2, local copies, waits for them, and re-layouts: 3.35 us -> 0.16 us  [lanes(): return jnp.broadcast_to(jnp.tile(part, 8)[None, :], (8, 128))]
    slice x5 -> x0, local copies, waits for them, and re-layouts: 3.18 us -> none  [the longest x3 3.17 us: body(): arrived = [flip(high[first:first + number], 2) for first, number in chunks]]
    ppermute x22 -> x9, waiting for transfers between devices: 10.6 us -> 7.98 us  [trade(): return lax.ppermute(block, 'site', route)]
    another operation x2, local copies, waits for them, and re-layouts: 1.85 us -> 0.01 us  [lanes(): return jnp.broadcast_to(jnp.tile(part, 8)[None, :], (8, 128))]
  transfers between devices with their start and end apart: 27 -> 15, of which waited for: 9 -> 7; matrix products, arithmetic and copies ran while one was open for 7% -> 2% of each run, Pallas kernels for 29% -> 44%
where the time goes in v2:
time: 101 us; the launch traced here: 99.6 us
  Pallas kernels  45.1 us (45%)
  starting transfers between devices  21.8 us (22%)
  local copies, waits for them, and re-layouts  17.3 us (17%)
  waiting for transfers between devices  14 us (14%)
  other arithmetic  1.24 us (1%)
    pallas_call x4, Pallas kernels, contract(): pl.pallas_call(functools.partial(contract_body, by_part, len(adds)), grid...  23.3 us
    pallas_call x2, Pallas kernels, relayout_low(): pl.pallas_call(relayout_low_body, grid=(colours, two), in_specs=[pl.Block...  17.3 us
    unnamed x12, local copies, waits for them, and re-layouts  16.3 us
    ppermute x9, starting transfers between devices, trade(): return lax.ppermute(block, 'site', route)  15.9 us
    ppermute x9, waiting for transfers between devices, trade(): return lax.ppermute(block, 'site', route)  7.98 us
    ppermute x6, waiting for transfers between devices, flip(): return lax.ppermute(block, 'mode', [(i, i ^ mask) for i in range(4)])  5.97 us
    ppermute x6, starting transfers between devices, flip(): return lax.ppermute(block, 'mode', [(i, i ^ mask) for i in range(4)])  5.95 us
    pallas_call x1, Pallas kernels, relayout_high(): pl.pallas_call(relayout_high_body, in_specs=[VMEM], out_specs=[VMEM] * (l...  2.87 us
  transfers between devices with their start and end apart: 15, of which 7 were waited for; matrix products, arithmetic and copies ran while one was open for 2% of the time, Pallas kernels for 44%

profile of v2, /device:TPU:0, one launch (start us, length us, event | category | flops | bytes accessed | tf_op | source)
XLA Modules:
  0.0 99.6 jit_solution(13617766902683022207)
XLA Ops:
  0.0 1.9 %copy-done.3 = bf16[16,2,3,8,2048]{4,3,2,1,0:T(8,128)(2,1)S(1)} copy-done((bf16[16,2,3,8,2048]{4,3,2,1,0:T(8,128)(2,1)S(1)}, bf16[16,2,3,8,2048]{4,3,2,1,0:T(8,128)(2,1)}, u32[]{:S(2)}) %copy-start.3) | copy-done | bytes 3145752
  1.9 2.9 %relayout_high.1 = (bf16[4,2,3,16,2048]{4,3,2,1,0:T(8,128)(2,1)S(1)}, bf16[2,2,3,16,2048]{4,3,2,1,0:T(8,128)(2,1)}, bf16[1,2,3,16,2048]{4,3,2,1,0:T(8,128)(2,1)}...) custom-call(bf16[16,2,3,8,2048]{4,3,2,1,0:T(8,128)(2,1)S(1)} %copy-done.3), custom_call_target="tpu_custom_call" | custom-call | tf_op jit(solution)/shard_map/relayout_high/pallas_call | solution.py:87
  5.5 2.0 %collective-permute-start.3 = (bf16[4,2,3,16,2048]{4,3,2,1,0:T(8,128)(2,1)S(1)}, bf16[4,2,3,16,2048]{4,3,2,1,0:T(8,128)(2,1)S(1)}, u32[]{:S(2)}, u32[]{:S(2)}) collective-permute-start(bf16[4,2,3,16,2048]{4,3,2,1,0:T(8,128)(2,1)S(1)} %get-tuple-element.42.refs_0_), channel_id=1, source_target_pairs={{0,64},{32,96},{64,0},{96,32},{1,65},{33,97},{65,1},{97,33},{2,66}... | collective-permute-start | bytes 4718600 | tf_op jit(solution)/shard_map/ppermute | solution.py:37
  7.6 2.0 %collective-permute-start.5 = (bf16[1,2,3,16,2048]{4,3,2,1,0:T(8,128)(2,1)}, bf16[1,2,3,16,2048]{4,3,2,1,0:T(8,128)(2,1)}, u32[]{:S(2)}, u32[]{:S(2)}) collective-permute-start(bf16[1,2,3,16,2048]{4,3,2,1,0:T(8,128)(2,1)} %get-tuple-element.45.refs_0_), channel_id=1, source_target_pairs={{0,64},{32,96},{64,0},{96,32},{1,65},{33,97},{65,1},{97,33},{2,66}... | collective-permute-start | bytes 1179656 | tf_op jit(solution)/shard_map/ppermute | solution.py:37
  11.8 4.6 %copy-done.2 = bf16[16,4,2,3,8,2048]{5,4,3,2,1,0:T(8,128)(2,1)S(1)} copy-done((bf16[16,4,2,3,8,2048]{5,4,3,2,1,0:T(8,128)(2,1)S(1)}, bf16[16,4,2,3,8,2048]{5,4,3,2,1,0:T(8,128)(2,1)}, u32[]{:S(2)}) %copy-start.2) | copy-done | bytes 12582936
  16.3 7.4 %relayout_low.2 = (bf16[8,3,2,4,16,2048]{5,4,3,2,1,0:T(8,128)(2,1)S(1)}, f32[8,128]{1,0:T(8,128)S(1)}) custom-call(bf16[16,4,2,3,8,2048]{5,4,3,2,1,0:T(8,128)(2,1)S(1)} %copy-done.2, f32[8,128]{1,0:T(8,128)S(1)} %get-tuple-element.36.after_ref), custom_call_target="tpu_custom_call" | custom-call | tf_op jit(solution)/shard_map/relayout_low/pallas_call | solution.py:120
  23.8 9.9 %relayout_low.3 = (bf16[8,3,2,4,16,2048]{5,4,3,2,1,0:T(8,128)(2,1)S(1)}, f32[8,128]{1,0:T(8,128)}) custom-call(bf16[16,4,2,3,8,2048]{5,4,3,2,1,0:T(8,128)(2,1)} %collective-permute-done.in_ref, f32[8,128]{1,0:T(8,128)S(1)} %get-tuple-element.38.after_ref.refs_2_), custom_call_target="tpu_custom_call" | custom-call | tf_op jit(solution)/shard_map/relayout_low/pallas_call | solution.py:120
  33.7 4.5 %copy-done = bf16[8,3,2,4,16,2048]{5,4,3,2,1,0:T(8,128)(2,1)} copy-done((bf16[8,3,2,4,16,2048]{5,4,3,2,1,0:T(8,128)(2,1)}, bf16[8,3,2,4,16,2048]{5,4,3,2,1,0:T(8,128)(2,1)S(1)}, u32[]{:S(2)}) %copy-start) | copy-done | bytes 12582936
  38.2 4.6 %collective-permute-done.3.refs_1_ = bf16[4,2,3,16,2048]{4,3,2,1,0:T(8,128)(2,1)S(1)} collective-permute-done((bf16[4,2,3,16,2048]{4,3,2,1,0:T(8,128)(2,1)S(1)}, bf16[4,2,3,16,2048]{4,3,2,1,0:T(8,128)(2,1)S(1)}, u32[]{:S(2)}, u32[]{:S(2)}) %collective-permute-start.3) | collective-permute-done | bytes 1572896 | tf_op jit(solution)/shard_map/ppermute | solution.py:37
  42.8 4.6 %copy-done.1 = bf16[8,3,2,4,16,2048]{5,4,3,2,1,0:T(8,128)(2,1)S(1)} copy-done((bf16[8,3,2,4,16,2048]{5,4,3,2,1,0:T(8,128)(2,1)S(1)}, bf16[8,3,2,4,16,2048]{5,4,3,2,1,0:T(8,128)(2,1)}, u32[]{:S(2)}) %copy-start.1) | copy-done | bytes 12582936
  47.4 10.5 %contract_0_4.1 = (bf16[2,4,2,64,128]{4,3,2,1,0:T(8,128)(2,1)S(1)}, f32[2,4,2,64,128]{4,3,2,1,0:T(8,128)S(1)}, f32[8,128]{1,0:T(8,128)S(1)}) custom-call(s32[8,256]{1,0:T(8,128)S(1)} %broadcast.183.pat_ref, f32[8,2048]{1,0:T(8,128)S(1)} %get-tuple-element.68.cos_ref, f32[8,2048]{1,0:T(8,128)S(1)} %get-tuple-element.67.sin_ref, ...), custom_call_target="tpu_custom_call" | custom-call | tf_op jit(solution)/shard_map/contract_0_4/pallas_call | solution.py:234
  57.9 1.7 %collective-permute-start.6 = (bf16[2,4,2,64,128]{4,3,2,1,0:T(8,128)(2,1)S(1)}, bf16[2,4,2,64,128]{4,3,2,1,0:T(8,128)(2,1)S(1)}, u32[]{:S(2)}, u32[]{:S(2)}) collective-permute-start(bf16[2,4,2,64,128]{4,3,2,1,0:T(8,128)(2,1)S(1)} %get-tuple-element.47), channel_id=1, source_target_pairs={{0,1},{1,0},{2,3},{3,2},{4,5},{5,4},{6,7},{7,6},{8,9},{9,8},{10,11... | collective-permute-start | bytes 786440 | tf_op jit(solution)/shard_map/ppermute | solution.py:33
  59.8 6.3 %contract_4_2.1 = (bf16[2,4,2,64,128]{4,3,2,1,0:T(8,128)(2,1)S(1)}, f32[8,128]{1,0:T(8,128)S(1)}) custom-call(s32[8,256]{1,0:T(8,128)S(1)} %broadcast.183.pat_ref, f32[8,2048]{1,0:T(8,128)S(1)} %get-tuple-element.68.cos_ref, f32[8,2048]{1,0:T(8,128)S(1)} %get-tuple-element.67.sin_ref, bf16[8,3,128,2048]{3,2,1,0:T(8,128)(2,1)S(1)} %bitcast.13, ...), custom_call_target="tpu_custom_call" | custom-call | tf_op jit(solution)/shard_map/contract_4_2/pallas_call | solution.py:234
  66.1 1.8 %collective-permute-start.4 = (bf16[2,4,2,64,128]{4,3,2,1,0:T(8,128)(2,1)S(1)}, bf16[2,4,2,64,128]{4,3,2,1,0:T(8,128)(2,1)S(1)}, u32[]{:S(2)}, u32[]{:S(2)}) collective-permute-start(bf16[2,4,2,64,128]{4,3,2,1,0:T(8,128)(2,1)S(1)} %get-tuple-element.44), channel_id=1, source_target_pairs={{0,8},{1,9},{2,10},{3,11},{4,12},{5,13},{6,14},{7,15},{8,0},{9,1},... | collective-permute-start | bytes 786440 | tf_op jit(solution)/shard_map/ppermute | solution.py:33
  67.8 1.8 %collective-permute-start.1 = (bf16[1,2,3,16,2048]{4,3,2,1,0:T(8,128)(2,1)S(1)}, bf16[1,2,3,16,2048]{4,3,2,1,0:T(8,128)(2,1)S(1)}, u32[]{:S(2)}, u32[]{:S(2)}) collective-permute-start(bf16[1,2,3,16,2048]{4,3,2,1,0:T(8,128)(2,1)S(1)} %copy-done.5), channel_id=1, source_target_pairs={{0,64},{32,96},{64,0},{96,32},{1,65},{33,97},{65,1},{97,33},{2,66}... | collective-permute-start | bytes 1179656 | tf_op jit(solution)/shard_map/ppermute | solution.py:37
  69.7 2.8 %collective-permute-start.8 = (bf16[1,4,2,64,128]{4,3,2,1,0:T(8,128)(2,1)S(1)}, bf16[1,4,2,64,128]{4,3,2,1,0:T(8,128)(2,1)S(1)}, u32[]{:S(2)}, u32[]{:S(2)}) collective-permute-start(bf16[1,4,2,64,128]{4,3,2,1,0:T(8,128)(2,1)S(1)} %get-tuple-element.52), channel_id=1, source_target_pairs={{0,3},{1,2},{2,1},{3,0},{4,7},{5,6},{6,5},{7,4},{8,11},{9,10},{10,... | collective-permute-start | bytes 393224 | tf_op jit(solution)/shard_map/ppermute | solution.py:33
  72.6 3.8 %contract_6_1.1 = (f32[1,4,2,64,128]{4,3,2,1,0:T(8,128)S(1)}, f32[8,128]{1,0:T(8,128)S(1)}) custom-call(s32[8,256]{1,0:T(8,128)S(1)} %broadcast.183.pat_ref, f32[8,2048]{1,0:T(8,128)S(1)} %get-tuple-element.68.cos_ref, f32[8,2048]{1,0:T(8,128)S(1)} %get-tuple-element.67.sin_ref, bf16[8,3,128,2048]{3,2,1,0:T(8,128)(2,1)S(1)} %bitcast.14, ...), custom_call_target="tpu_custom_call" | custom-call | tf_op jit(solution)/shard_map/contract_6_1/pallas_call | solution.py:234
  76.4 2.2 %collective-permute-start.7 = (bf16[4,2,64,128]{3,2,1,0:T(8,128)(2,1)S(1)}, bf16[4,2,64,128]{3,2,1,0:T(8,128)(2,1)S(1)}, u32[]{:S(2)}, u32[]{:S(2)}) collective-permute-start(bf16[4,2,64,128]{3,2,1,0:T(8,128)(2,1)S(1)} %fusion), channel_id=1, source_target_pairs={{0,24},{1,25},{2,26},{3,27},{4,28},{5,29},{6,30},{7,31},{8,16},{9,... | collective-permute-start | bytes 393224 | tf_op jit(solution)/shard_map/ppermute | solution.py:33
  79.4 3.2 %collective-permute-done.7.refs_3_ = bf16[4,2,64,128]{3,2,1,0:T(8,128)(2,1)S(1)} collective-permute-done((bf16[4,2,64,128]{3,2,1,0:T(8,128)(2,1)S(1)}, bf16[4,2,64,128]{3,2,1,0:T(8,128)(2,1)S(1)}, u32[]{:S(2)}, u32[]{:S(2)}) %collective-permute-start.7) | collective-permute-done | bytes 131104 | tf_op jit(solution)/shard_map/ppermute | solution.py:33
  82.7 2.7 %contract_7_1.1 = (f32[2,1,2,64,128]{4,3,2,1,0:T(8,128)S(1)}, f32[2,1,2,64,128]{4,3,2,1,0:T(8,128)S(1)}, f32[8,128]{1,0:T(8,128)S(1)}) custom-call(s32[8,256]{1,0:T(8,128)S(1)} %broadcast.183.pat_ref, f32[8,2048]{1,0:T(8,128)S(1)} %get-tuple-element.68.cos_ref, f32[8,2048]{1,0:T(8,128)S(1)} %get-tuple-element.67.sin_ref, ...), custom_call_target="tpu_custom_call" | custom-call | tf_op jit(solution)/shard_map/contract_7_1/pallas_call | solution.py:234
  85.7 2.2 %collective-permute-start.12 = (f32[1,2,64,128]{3,2,1,0:T(8,128)S(1)}, f32[1,2,64,128]{3,2,1,0:T(8,128)S(1)}, u32[]{:S(2)}, u32[]{:S(2)}) collective-permute-start(f32[1,2,64,128]{3,2,1,0:T(8,128)S(1)} %get-tuple-element.64), channel_id=1, source_target_pairs={{0,24},{1,25},{2,26},{3,27},{4,28},{5,29},{6,30},{7,31},{8,16},{9,... | collective-permute-start | bytes 196616 | tf_op jit(solution)/shard_map/ppermute | solution.py:33
  87.9 2.5 %collective-permute-done.9 = f32[2,1,2,64,128]{4,3,2,0,1:T(8,128)S(1)} collective-permute-done((f32[2,1,2,64,128]{4,3,2,0,1:T(8,128)S(1)}, f32[2,1,2,64,128]{4,3,2,0,1:T(8,128)S(1)}, u32[]{:S(2)}, u32[]{:S(2)}) %collective-permute-start.9) | collective-permute-done | bytes 131104 | tf_op jit(solution)/shard_map/ppermute | solution.py:33
  91.5 3.7 %collective-permute-start.13 = (f32[1,2,64,128]{3,2,1,0:T(8,128)S(1)}, f32[1,2,64,128]{3,2,1,0:T(8,128)S(1)}, u32[]{:S(2)}, u32[]{:S(2)}) collective-permute-start(f32[1,2,64,128]{3,2,1,0:T(8,128)S(1)} %add.81), channel_id=1, source_target_pairs={{0,4},{1,5},{2,6},{3,7},{4,0},{5,1},{6,2},{7,3},{8,12},{9,13},{10,... | collective-permute-start | bytes 196616 | tf_op jit(solution)/shard_map/ppermute | solution.py:33
  95.2 1.3 %collective-permute-done.11.last_ref = f32[1,2,64,128]{3,2,1,0:T(8,128)S(1)} collective-permute-done((f32[1,2,64,128]{3,2,1,0:T(8,128)S(1)}, f32[1,2,64,128]{3,2,1,0:T(8,128)S(1)}, u32[]{:S(2)}, u32[]{:S(2)}) %collective-permute-start.11) | collective-permute-done | bytes 65568 | tf_op jit(solution)/shard_map/ppermute | solution.py:33
  (46 shorter events, 8.5 us)
Async XLA Ops:
  0.0 23.8 %collective-permute-start = (bf16[16,4,2,3,8,2048]{5,4,3,2,1,0:T(8,128)(2,1)}, bf16[16,4,2,3,8,2048]{5,4,3,2,1,0:T(8,128)(2,1)}, u32[]{:S(2)}, u32[]{:S(2)}) collective-permute-start(bf16[16,4,2,3,8,2048]{5,4,3,2,1,0:T(8,128)(2,1)} %in_ref.3), channel_id=1, source_target_pairs={{0,32},{32,0},{64,96},{96,64},{1,33},{33,1},{65,97},{97,65},{2,34}... | collective-permute-start | bytes 37748744 | tf_op jit(solution)/shard_map/ppermute | solution.py:37
  0.0 1.9 %copy-start.3 = (bf16[16,2,3,8,2048]{4,3,2,1,0:T(8,128)(2,1)S(1)}, bf16[16,2,3,8,2048]{4,3,2,1,0:T(8,128)(2,1)}, u32[]{:S(2)}) copy-start(bf16[16,2,3,8,2048]{4,3,2,1,0:T(8,128)(2,1)} %in_ref.2) | copy-start | bytes 9437188
  4.8 0.8 copy-start.4
  5.5 37.3 %collective-permute-start.3 = (bf16[4,2,3,16,2048]{4,3,2,1,0:T(8,128)(2,1)S(1)}, bf16[4,2,3,16,2048]{4,3,2,1,0:T(8,128)(2,1)S(1)}, u32[]{:S(2)}, u32[]{:S(2)}) collective-permute-start(bf16[4,2,3,16,2048]{4,3,2,1,0:T(8,128)(2,1)S(1)} %get-tuple-element.42.refs_0_), channel_id=1, source_target_pairs={{0,64},{32,96},{64,0},{96,32},{1,65},{33,97},{65,1},{97,33},{2,66}... | collective-permute-start | bytes 4718600 | tf_op jit(solution)/shard_map/ppermute | solution.py:37
  7.5 52.2 %collective-permute-start.2 = (bf16[2,2,3,16,2048]{4,3,2,1,0:T(8,128)(2,1)}, bf16[2,2,3,16,2048]{4,3,2,1,0:T(8,128)(2,1)}, u32[]{:S(2)}, u32[]{:S(2)}) collective-permute-start(bf16[2,2,3,16,2048]{4,3,2,1,0:T(8,128)(2,1)} %get-tuple-element.41.refs_0_), channel_id=1, source_target_pairs={{0,64},{32,96},{64,0},{96,32},{1,65},{33,97},{65,1},{97,33},{2,66}... | collective-permute-start | bytes 2359304 | tf_op jit(solution)/shard_map/ppermute | solution.py:37
  7.6 65.0 %collective-permute-start.5 = (bf16[1,2,3,16,2048]{4,3,2,1,0:T(8,128)(2,1)}, bf16[1,2,3,16,2048]{4,3,2,1,0:T(8,128)(2,1)}, u32[]{:S(2)}, u32[]{:S(2)}) collective-permute-start(bf16[1,2,3,16,2048]{4,3,2,1,0:T(8,128)(2,1)} %get-tuple-element.45.refs_0_), channel_id=1, source_target_pairs={{0,64},{32,96},{64,0},{96,32},{1,65},{33,97},{65,1},{97,33},{2,66}... | collective-permute-start | bytes 1179656 | tf_op jit(solution)/shard_map/ppermute | solution.py:37
  11.8 4.6 %copy-start.2 = (bf16[16,4,2,3,8,2048]{5,4,3,2,1,0:T(8,128)(2,1)S(1)}, bf16[16,4,2,3,8,2048]{5,4,3,2,1,0:T(8,128)(2,1)}, u32[]{:S(2)}) copy-start(bf16[16,4,2,3,8,2048]{5,4,3,2,1,0:T(8,128)(2,1)} %in_ref.3) | copy-start | bytes 37748740
  33.7 4.5 %copy-start = (bf16[8,3,2,4,16,2048]{5,4,3,2,1,0:T(8,128)(2,1)}, bf16[8,3,2,4,16,2048]{5,4,3,2,1,0:T(8,128)(2,1)S(1)}, u32[]{:S(2)}) copy-start(bf16[8,3,2,4,16,2048]{5,4,3,2,1,0:T(8,128)(2,1)S(1)} %get-tuple-element.39) | copy-start | bytes 37748740
  42.8 4.6 %copy-start.1 = (bf16[8,3,2,4,16,2048]{5,4,3,2,1,0:T(8,128)(2,1)S(1)}, bf16[8,3,2,4,16,2048]{5,4,3,2,1,0:T(8,128)(2,1)}, u32[]{:S(2)}) copy-start(bf16[8,3,2,4,16,2048]{5,4,3,2,1,0:T(8,128)(2,1)} %copy-done) | copy-start | bytes 37748740
  57.9 11.8 %collective-permute-start.6 = (bf16[2,4,2,64,128]{4,3,2,1,0:T(8,128)(2,1)S(1)}, bf16[2,4,2,64,128]{4,3,2,1,0:T(8,128)(2,1)S(1)}, u32[]{:S(2)}, u32[]{:S(2)}) collective-permute-start(bf16[2,4,2,64,128]{4,3,2,1,0:T(8,128)(2,1)S(1)} %get-tuple-element.47), channel_id=1, source_target_pairs={{0,1},{1,0},{2,3},{3,2},{4,5},{5,4},{6,7},{7,6},{8,9},{9,8},{10,11... | collective-permute-start | bytes 786440 | tf_op jit(solution)/shard_map/ppermute | solution.py:33
  59.8 8.1 %copy-start.5 = (bf16[1,2,3,16,2048]{4,3,2,1,0:T(8,128)(2,1)S(1)}, bf16[1,2,3,16,2048]{4,3,2,1,0:T(8,128)(2,1)}, u32[]{:S(2)}) copy-start(bf16[1,2,3,16,2048]{4,3,2,1,0:T(8,128)(2,1)} %copy-done.4) | copy-start | bytes 1179652
  66.1 10.3 %collective-permute-start.4 = (bf16[2,4,2,64,128]{4,3,2,1,0:T(8,128)(2,1)S(1)}, bf16[2,4,2,64,128]{4,3,2,1,0:T(8,128)(2,1)S(1)}, u32[]{:S(2)}, u32[]{:S(2)}) collective-permute-start(bf16[2,4,2,64,128]{4,3,2,1,0:T(8,128)(2,1)S(1)} %get-tuple-element.44), channel_id=1, source_target_pairs={{0,8},{1,9},{2,10},{3,11},{4,12},{5,13},{6,14},{7,15},{8,0},{9,1},... | collective-permute-start | bytes 786440 | tf_op jit(solution)/shard_map/ppermute | solution.py:33
  67.8 11.6 %collective-permute-start.1 = (bf16[1,2,3,16,2048]{4,3,2,1,0:T(8,128)(2,1)S(1)}, bf16[1,2,3,16,2048]{4,3,2,1,0:T(8,128)(2,1)S(1)}, u32[]{:S(2)}, u32[]{:S(2)}) collective-permute-start(bf16[1,2,3,16,2048]{4,3,2,1,0:T(8,128)(2,1)S(1)} %copy-done.5), channel_id=1, source_target_pairs={{0,64},{32,96},{64,0},{96,32},{1,65},{33,97},{65,1},{97,33},{2,66}... | collective-permute-start | bytes 1179656 | tf_op jit(solution)/shard_map/ppermute | solution.py:37
  69.7 8.9 %collective-permute-start.8 = (bf16[1,4,2,64,128]{4,3,2,1,0:T(8,128)(2,1)S(1)}, bf16[1,4,2,64,128]{4,3,2,1,0:T(8,128)(2,1)S(1)}, u32[]{:S(2)}, u32[]{:S(2)}) collective-permute-start(bf16[1,4,2,64,128]{4,3,2,1,0:T(8,128)(2,1)S(1)} %get-tuple-element.52), channel_id=1, source_target_pairs={{0,3},{1,2},{2,1},{3,0},{4,7},{5,6},{6,5},{7,4},{8,11},{9,10},{10,... | collective-permute-start | bytes 393224 | tf_op jit(solution)/shard_map/ppermute | solution.py:33
  76.4 6.3 %collective-permute-start.7 = (bf16[4,2,64,128]{3,2,1,0:T(8,128)(2,1)S(1)}, bf16[4,2,64,128]{3,2,1,0:T(8,128)(2,1)S(1)}, u32[]{:S(2)}, u32[]{:S(2)}) collective-permute-start(bf16[4,2,64,128]{3,2,1,0:T(8,128)(2,1)S(1)} %fusion), channel_id=1, source_target_pairs={{0,24},{1,25},{2,26},{3,27},{4,28},{5,29},{6,30},{7,31},{8,16},{9,... | collective-permute-start | bytes 393224 | tf_op jit(solution)/shard_map/ppermute | solution.py:33
  78.7 7.0 %collective-permute-start.10 = (f32[2,2,64,128]{3,2,1,0:T(8,128)S(1)}, f32[2,2,64,128]{3,2,1,0:T(8,128)S(1)}, u32[]{:S(2)}, u32[]{:S(2)}) collective-permute-start(f32[2,2,64,128]{3,2,1,0:T(8,128)S(1)} %get-tuple-element.58), channel_id=1, source_target_pairs={{0,8},{1,9},{2,10},{3,11},{4,12},{5,13},{6,14},{7,15},{8,0},{9,1},... | collective-permute-start | bytes 393224 | tf_op jit(solution)/shard_map/ppermute | solution.py:33
  85.3 5.0 %collective-permute-start.9 = (f32[2,1,2,64,128]{4,3,2,0,1:T(8,128)S(1)}, f32[2,1,2,64,128]{4,3,2,0,1:T(8,128)S(1)}, u32[]{:S(2)}, u32[]{:S(2)}) collective-permute-start(f32[2,1,2,64,128]{4,3,2,0,1:T(8,128)S(1)} %bitcast.24), channel_id=1, source_target_pairs={{0,1},{1,0},{2,3},{3,2},{4,5},{5,4},{6,7},{7,6},{8,9},{9,8},{10,11... | collective-permute-start | bytes 393224 | tf_op jit(solution)/shard_map/ppermute | solution.py:33
  85.7 5.8 %collective-permute-start.12 = (f32[1,2,64,128]{3,2,1,0:T(8,128)S(1)}, f32[1,2,64,128]{3,2,1,0:T(8,128)S(1)}, u32[]{:S(2)}, u32[]{:S(2)}) collective-permute-start(f32[1,2,64,128]{3,2,1,0:T(8,128)S(1)} %get-tuple-element.64), channel_id=1, source_target_pairs={{0,24},{1,25},{2,26},{3,27},{4,28},{5,29},{6,30},{7,31},{8,16},{9,... | collective-permute-start | bytes 196616 | tf_op jit(solution)/shard_map/ppermute | solution.py:33
  91.0 5.5 %collective-permute-start.11 = (f32[1,2,64,128]{3,2,1,0:T(8,128)S(1)}, f32[1,2,64,128]{3,2,1,0:T(8,128)S(1)}, u32[]{:S(2)}, u32[]{:S(2)}) collective-permute-start(f32[1,2,64,128]{3,2,1,0:T(8,128)S(1)} %get-tuple-element.62), channel_id=1, source_target_pairs={{0,3},{1,2},{2,1},{3,0},{4,7},{5,6},{6,5},{7,4},{8,11},{9,10},{10,... | collective-permute-start | bytes 196616 | tf_op jit(solution)/shard_map/ppermute | solution.py:33
  91.5 5.9 %collective-permute-start.13 = (f32[1,2,64,128]{3,2,1,0:T(8,128)S(1)}, f32[1,2,64,128]{3,2,1,0:T(8,128)S(1)}, u32[]{:S(2)}, u32[]{:S(2)}) collective-permute-start(f32[1,2,64,128]{3,2,1,0:T(8,128)S(1)} %add.81), channel_id=1, source_target_pairs={{0,4},{1,5},{2,6},{3,7},{4,0},{5,1},{6,2},{7,3},{8,12},{9,13},{10,... | collective-permute-start | bytes 196616 | tf_op jit(solution)/shard_map/ppermute | solution.py:33
  97.4 1.3 %collective-permute-start.14 = (f32[2,32,128]{2,1,0:T(8,128)S(1)}, f32[2,32,128]{2,1,0:T(8,128)S(1)}, u32[]{:S(2)}, u32[]{:S(2)}) collective-permute-start(f32[2,32,128]{2,1,0:T(8,128)S(1)} %get-tuple-element.66), channel_id=1, source_target_pairs={{0,32},{32,0},{64,96},{96,64},{1,33},{33,1},{65,97},{97,65},{2,34}... | collective-permute-start | bytes 98312 | tf_op jit(solution)/shard_map/ppermute | solution.py:37

commit v3 on v2

--- a/solution.py
+++ b/solution.py
@@ -50,74 +50,86 @@
 
 VMEM = pl.BlockSpec(memory_space=pltpu.VMEM)
 STEP = 512
-HIGH_LIMIT = 4 * 2**20
-LOW_LIMIT = 10 * 2**20
+HIGH_LIMIT = 12 * 2**20
+LOW_LIMIT = 16 * 2**20
+MANY_LIMIT = 24 * 2**20
+FEW_LIMIT = 14 * 2**20
 SMALL = pltpu.CompilerParams(vmem_limit_bytes=4 * 2**20)
 TOKEN = jax.ShapeDtypeStruct((8, 128), jnp.float32)
 TINY = pl.CostEstimate(flops=0, bytes_accessed=0, transcendentals=0)
 
 
+def stay(array):
+    return pltpu.with_memory_space_constraint(array, pltpu.HBM)
+
+
 def whole(shape):
     return pl.BlockSpec(shape, lambda *_: (0,) * len(shape))
 
 
+def turn(values, turned_ref, outs, index, cut, y, z):
+    turned_ref[...] = jnp.swapaxes(values, 0, 1)
+    slot = 0
+    for out in outs:
+        for k in range(out.shape[0]):
+            out[(k,) + index + (slice(None), cut)] = turned_ref[time_of(slot, y, z)]
+            slot += 1
+
+
 def relayout_high_body(in_ref, *refs):
-    outs, token_ref, turned_ref = refs[:-2], refs[-2], refs[-1]
+    outs, (token_ref, held_ref, turned_ref, sems) = refs[:-4], refs[-4:]
     _, y, z = coords()
     token_ref[...] = jnp.zeros_like(token_ref)
-
-    def one(index, carry):
-        r, c = lax.div(index, 3), lax.rem(index, 3)
-        for j in range(0, in_ref.shape[-1], STEP):
+    pieces = [(r, c) for r in range(2) for c in range(3)]
+    copies = [
+        pltpu.make_async_copy(in_ref.at[:, r, c], held_ref.at[i], sems.at[i])
+        for i, (r, c) in enumerate(pieces)
+    ]
+    for copy in copies:
+        copy.start()
+    for i, (r, c) in enumerate(pieces):
+        copies[i].wait()
+        for j in range(0, held_ref.shape[-1], STEP):
             cut = pl.ds(j, STEP)
-            values = in_ref[:, r, c, :, cut].astype(jnp.float32)
-            turned_ref[...] = jnp.swapaxes(values, 0, 1).astype(jnp.bfloat16)
-            slot = 0
-            for out in outs:
-                for k in range(out.shape[0]):
-                    out[k, r, c, :, cut] = turned_ref[time_of(slot, y, z)]
-                    slot += 1
-        return carry
-
-    lax.fori_loop(0, 6, one, 0)
+            turn(held_ref[i, :, :, cut], turned_ref, outs, (r, c), cut, y, z)
 
 
 def relayout_high(high, sizes):
     rows, two, colours, slices, count = high.shape
     return pl.pallas_call(
         relayout_high_body,
-        in_specs=[VMEM],
+        in_specs=[pl.BlockSpec(memory_space=pl.ANY)],
         out_specs=[VMEM] * (len(sizes) + 1),
-        out_shape=[
-            jax.ShapeDtypeStruct((n, two, colours, rows, count), jnp.bfloat16) for n in sizes
-        ]
-        + [jax.ShapeDtypeStruct((8, 128), jnp.float32)],
-        scratch_shapes=[pltpu.VMEM((slices, rows, STEP), jnp.bfloat16)],
+        out_shape=[pltpu.VMEM((n, two, colours, rows, count), jnp.bfloat16) for n in sizes]
+        + [TOKEN],
+        scratch_shapes=[
+            pltpu.VMEM((two * colours, rows, slices, count), jnp.bfloat16),
+            pltpu.VMEM((slices, rows, STEP), jnp.bfloat16),
+            pltpu.SemaphoreType.DMA((two * colours,)),
+        ],
         compiler_params=pltpu.CompilerParams(vmem_limit_bytes=HIGH_LIMIT),
         cost_estimate=TINY,
         name="relayout_high",
-    )(high)
-
-
-def relayout_low_body(in_ref, after_ref, out_ref, token_ref):
+    )(stay(high))
+
+
+def relayout_low_body(in_ref, after_ref, many_ref, few_ref, token_ref, turned_ref):
+    _, y, z = coords()
     token_ref[...] = jnp.zeros_like(token_ref)
-    _, y, z = coords()
 
     def one(s, carry):
         for j in range(0, in_ref.shape[-1], STEP):
             cut = pl.ds(j, STEP)
-            values = in_ref[:, s, 0, 0, :, cut].astype(jnp.float32)
-            turned = jnp.swapaxes(values, 0, 1).astype(jnp.bfloat16)
-            for t in range(SLOTS):
-                out_ref[slot_of(t, y, z), 0, 0, s, :, cut] = turned[t]
+            values = in_ref[:, s, 0, 0, :, cut]
+            turn(values, turned_ref, (many_ref, few_ref), (0, 0, s), cut, y, z)
         return carry
 
     lax.fori_loop(0, in_ref.shape[1], one, 0)
 
 
-def relayout_low(low, token):
+def relayout_low(low, after, sizes):
     rows, spins, two, colours, slices, count = low.shape
-    turned, token = pl.pallas_call(
+    *turned, token = pl.pallas_call(
         relayout_low_body,
         grid=(colours, two),
         in_specs=[
@@ -125,18 +137,22 @@
             whole((8, 128)),
         ],
         out_specs=[
-            pl.BlockSpec((slices, 1, 1, spins, rows, count), lambda c, u: (0, c, u, 0, 0, 0)),
-            whole((8, 128)),
-        ],
+            pl.BlockSpec((n, 1, 1, spins, rows, count), lambda c, u: (0, c, u, 0, 0, 0))
+            for n in sizes
+        ]
+        + [whole((8, 128))],
         out_shape=[
-            jax.ShapeDtypeStruct((slices, colours, two, spins, rows, count), jnp.bfloat16),
-            jax.ShapeDtypeStruct((8, 128), jnp.float32),
-        ],
+            space((n, colours, two, spins, rows, count), jnp.bfloat16)
+            for n, space in zip(sizes, (pltpu.HBM, pltpu.VMEM))
+        ]
+        + [TOKEN],
+        scratch_shapes=[pltpu.VMEM((slices, rows, STEP), jnp.bfloat16)],
         compiler_params=pltpu.CompilerParams(vmem_limit_bytes=LOW_LIMIT),
         cost_estimate=TINY,
         name="relayout_low",
-    )(low, token)
-    return turned.reshape(slices, colours, two * spins * rows, count), token
+    )(stay(low), after)
+    turned = [t.reshape(t.shape[0], colours, two * spins * rows, count) for t in turned]
+    return turned, token
 
 
 def contract_body(by_part, added, pat_ref, cos_ref, sin_ref, own_ref, oth_ref, *refs):
@@ -209,18 +225,24 @@
                 turned = pltpu.roll(stacked[g], lax.rem(g - group + NX, NX) * 32, 1)
                 result = turned if result is None else jnp.where(lane == g, turned, result)
             for add in adds:
-                result = result + add[k, block].astype(jnp.float32)
-            if by_part:
+                result = result + add[add.shape[0] - 1, k, block].astype(jnp.float32)
+            if by_part == "each":
+                outs[k][0, block] = result.astype(outs[k].dtype)
+            elif by_part:
                 outs[k // 2][k % 2, 0, block] = result.astype(outs[k // 2].dtype)
             else:
                 outs[0][0, k, block] = result.astype(outs[0].dtype)
 
 
-def contract(tables, low_own, low_oth, own, received, first, by_part, sent, after, adds=()):
-    colours, rows, count = low_own.shape[1:]
+def contract(tables, lows, own, received, first, by_part, sent, after, limit, adds=()):
+    colours, rows, count = lows[0].shape[1:]
     number = own.shape[0]
     unit = (2, 64, 128)
-    if by_part:
+    if by_part == "each":
+        kinds = [sent] * (NX - 1) + [jnp.float32]
+        shapes = [jax.ShapeDtypeStruct((number,) + unit, kind) for kind in kinds]
+        out_specs = [pl.BlockSpec((1,) + unit, lambda i: (i, 0, 0, 0))] * NX
+    elif by_part:
         shapes = [
             jax.ShapeDtypeStruct((2, number) + unit, sent),
             jax.ShapeDtypeStruct((2, number) + unit, jnp.float32),
@@ -241,26 +263,29 @@
         out_specs=out_specs + [whole((8, 128))],
         out_shape=shapes + [TOKEN],
         scratch_shapes=[pltpu.VMEM((256, 512), jnp.float32)],
-        compiler_params=pltpu.CompilerParams(vmem_limit_bytes=14 * 2**20),
+        compiler_params=pltpu.CompilerParams(vmem_limit_bytes=limit),
         cost_estimate=TINY,
         name=f"contract_{first}_{number}",
-    )(*tables, low_own, low_oth, own, received, *adds, after)
-
-
-def fold_body(axis, kept_ref, got_ref, after_ref, first_ref, second_ref, token_ref):
-    half = kept_ref.shape[axis] // 2
+    )(*tables, *lows, own, received, *adds, after)
+
+
+def fold_body(number, *refs):
+    parts, (first_ref, second_ref, token_ref) = refs[:number], refs[-3:]
+    half = parts[0].shape[0] // 2
     for out_ref, cut in ((first_ref, slice(0, half)), (second_ref, slice(half, 2 * half))):
-        index = (slice(None),) * axis + (cut,)
-        total = kept_ref[index] + got_ref[index].astype(jnp.float32)
+        total = None
+        for part in parts:
+            value = part[cut].astype(jnp.float32)
+            total = value if total is None else total + value
         out_ref[...] = total.astype(out_ref.dtype)
     token_ref[...] = jnp.zeros_like(token_ref)
 
 
-def fold(kept, got, axis, sent, after):
-    shape = kept.shape[:axis] + (kept.shape[axis] // 2,) + kept.shape[axis + 1 :]
-    return pl.pallas_call(
-        functools.partial(fold_body, axis),
-        in_specs=[VMEM] * 3,
+def fold(parts, sent, after):
+    shape = (parts[0].shape[0] // 2,) + parts[0].shape[1:]
+    return pl.pallas_call(
+        functools.partial(fold_body, len(parts)),
+        in_specs=[VMEM] * (len(parts) + 1),
         out_specs=[VMEM] * 3,
         out_shape=[
             jax.ShapeDtypeStruct(shape, sent),
@@ -270,12 +295,35 @@
         compiler_params=SMALL,
         cost_estimate=TINY,
         name="fold",
-    )(kept, got, after)
+    )(*parts, after)
+
+
+def plus_body(number, *refs):
+    parts, out_ref, token_ref = refs[:number], refs[-2], refs[-1]
+    total = None
+    for part in parts:
+        value = part[: out_ref.shape[0]].astype(jnp.float32)
+        total = value if total is None else total + value
+    out_ref[...] = total.astype(out_ref.dtype)
+    token_ref[...] = jnp.zeros_like(token_ref)
+
+
+def plus(parts, sent, after):
+    length = min(part.shape[0] for part in parts)
+    return pl.pallas_call(
+        functools.partial(plus_body, len(parts)),
+        in_specs=[VMEM] * (len(parts) + 1),
+        out_specs=[VMEM] * 2,
+        out_shape=[jax.ShapeDtypeStruct((length,) + parts[0].shape[1:], sent), TOKEN],
+        compiler_params=SMALL,
+        cost_estimate=TINY,
+        name="plus",
+    )(*parts, after)
 
 
 def finish_body(kept_ref, last_ref, across_ref, mine_ref, other_ref):
     for out_ref, rows in ((mine_ref, slice(0, 32)), (other_ref, slice(32, 64))):
-        out_ref[...] = kept_ref[0, :, rows] + last_ref[0, :, rows] + across_ref[0, :, rows]
+        out_ref[...] = kept_ref[0, :, rows] + last_ref[0, :, rows].astype(jnp.float32) + across_ref[0, :, rows]
 
 
 def finish(kept, last, across):
@@ -328,12 +376,13 @@
     count = low_modes.shape[-1]
     my_mode = lax.axis_index("mode")
     wide, narrow = jnp.float32, jnp.bfloat16
-    *high, token = relayout_high(high_modes, (4, 2, 1, 1))
+    *high, token = relayout_high(high_modes, (2, 2, 2, 1, 1))
     arrived = [flip(chunk, 2) for chunk in high]
-
     low_oth = flip(low_modes, 1)
-    low_own, token = relayout_low(low_modes, token)
-    low_oth, _ = relayout_low(low_oth, token)
+    low_own, token = relayout_low(low_modes, token, (4, 4))
+    low_oth, token = relayout_low(low_oth, token, (4, 4))
+    many, few = zip(low_own, low_oth)
+    many = [stay(a) for a in many]
     cosines, sines = phase_tables(momenta, lax.axis_index("site") * count, count)
 
     def lanes(block):
@@ -341,31 +390,37 @@
         return jnp.broadcast_to(jnp.tile(part, 8)[None, :], (8, 128))
 
     tables = (jnp.concatenate([lanes(my_mode), lanes(my_mode ^ 2)], 1), cosines, sines)
-    away, far, token = contract(
-        tables, low_own, low_oth, high[0], arrived[0], 0, True, narrow, token
-    )
+    away, token = contract(
+        tables, many, high[0], arrived[0], 0, False, narrow, token, MANY_LIMIT
+    )
+    far_got = trade(away, 1, 0, 0)
+    far, token = contract(
+        tables, many, high[1], arrived[1], 2, False, wide, token, MANY_LIMIT
+    )
+    away, far, token = fold((far, far_got), narrow, token)
+    far_got = trade(away, 3, 0, 0)
+    away, far, token = fold((far[0], far_got[0]), narrow, token)
     far_got = trade(away, 0, 0, 1)
     away, token = contract(
-        tables, low_own, low_oth, high[1], arrived[1], 4, False, narrow, token
+        tables, few, high[2], arrived[2], 0, False, narrow, token, FEW_LIMIT
     )
     near_got = trade(away, 1, 0, 0)
-    away, far, token = fold(far, far_got, 0, narrow, token)
+    near, token = contract(
+        tables, few, high[3], arrived[3], 2, False, wide, token, FEW_LIMIT
+    )
+    away, far, token = fold((far, far_got), narrow, token)
     far_got = trade(away, 0, 0, 3)
-    near, token = contract(tables, low_own, low_oth, high[2], arrived[2], 6, False, wide, token)
-    near_last = trade((near[0] + near_got[0].astype(wide)).astype(narrow), 3, 0, 0)
-    away, far, token = fold(far[0], far_got[0], 0, wide, token)
-    far_got = trade(away, 1, 0, 0)
-    adds = (near_got[1], near_last)
+    away, token = plus((near, near_got), narrow, token)
+    adds = (near_got, trade(away, 3, 0, 0))
+    away, token = plus((far, far_got), wide, token)
+    across = trade(away, 0, 1, 0)
     away, near, token = contract(
-        tables, low_own, low_oth, high[3], arrived[3], 7, True, wide, token, adds
-    )
-    near_got = trade(away, 0, 0, 1)
-    away, far, token = fold(far, far_got, 0, wide, token)
-    far_got = trade(away, 3, 0, 0)
-    away, near, token = fold(near[:, 0], near_got[:, 0], 0, wide, token)
-    near_got = trade(away, 0, 0, 3)
-    across = trade(far + far_got, 0, 1, 0)
-    mine, other = finish(near, near_got, across)
+        tables, few, high[4], arrived[4], 3, True, narrow, token, FEW_LIMIT, adds
+    )
+    last_got = trade(away, 0, 0, 1)
+    away, near, token = fold((near[:, 0], last_got[:, 0]), narrow, token)
+    last_got = trade(away, 0, 0, 3)
+    mine, other = finish(near, last_got, across)
     pieces = (mine, flip(other, 1))
     return jnp.transpose(assemble(pieces), (0, 1, 2, 4, 3))
 

time: 101 us -> 95.7 us (0.948)
  local copies, waits for them, and re-layouts: 17.3 us -> 1.73 us
  starting transfers between devices: 21.8 us -> 28.4 us
  Pallas kernels: 45.1 us -> 49.4 us
    unnamed x12 -> x8, local copies, waits for them, and re-layouts: 16.3 us -> 0.76 us
    ppermute x9, starting transfers between devices: 15.9 us -> 20.6 us  [trade(): return lax.ppermute(block, 'site', route)]
    pallas_call x2, Pallas kernels: 17.3 us -> 19.8 us  [relayout_low(): pl.pallas_call(relayout_low_body, grid=(colours, two), in_specs=[pl.Block...]
    ppermute x6 -> x7, starting transfers between devices: 5.95 us -> 7.79 us  [flip(): return lax.ppermute(block, 'mode', [(i, i ^ mask) for i in range(4)])]
    pallas_call x4 -> x5, Pallas kernels: 23.3 us -> 25 us  [contract(): pl.pallas_call(functools.partial(contract_body, by_part, len(adds)), grid...]
    ppermute x9, waiting for transfers between devices: 7.98 us -> 6.73 us  [trade(): return lax.ppermute(block, 'site', route)]
    ppermute x6 -> x7, waiting for transfers between devices: 5.97 us -> 6.77 us  [flip(): return lax.ppermute(block, 'mode', [(i, i ^ mask) for i in range(4)])]
    pallas_call x5 -> x7, Pallas kernels: 3.57 us -> 3.7 us  [the longest x1 2.98 us: relayout_high(): pl.pallas_call(relayout_high_body, in_specs=[pl.BlockSpec(memory_space=pl...]
  transfers between devices with their start and end apart: 15 -> 16, of which waited for: 7 -> 9; matrix products, arithmetic and copies ran while one was open for 2% -> 2% of each run, Pallas kernels for 44% -> 49%
where the time goes in v3:
time: 95.7 us; the launch traced here: 94.3 us
  Pallas kernels  49.4 us (52%)
  starting transfers between devices  28.4 us (30%)
  waiting for transfers between devices  13.5 us (14%)
  local copies, waits for them, and re-layouts  1.73 us (2%)
  other arithmetic  1.12 us (1%)
    pallas_call x5, Pallas kernels, contract(): pl.pallas_call(functools.partial(contract_body, by_part, len(adds)), grid...  25 us
    ppermute x9, starting transfers between devices, trade(): return lax.ppermute(block, 'site', route)  20.6 us
    pallas_call x2, Pallas kernels, relayout_low(): pl.pallas_call(relayout_low_body, grid=(colours, two), in_specs=[pl.Block...  19.8 us
    ppermute x7, starting transfers between devices, flip(): return lax.ppermute(block, 'mode', [(i, i ^ mask) for i in range(4)])  7.79 us
    ppermute x7, waiting for transfers between devices, flip(): return lax.ppermute(block, 'mode', [(i, i ^ mask) for i in range(4)])  6.77 us
    ppermute x9, waiting for transfers between devices, trade(): return lax.ppermute(block, 'site', route)  6.73 us
    pallas_call x1, Pallas kernels, relayout_high(): pl.pallas_call(relayout_high_body, in_specs=[pl.BlockSpec(memory_space=pl...  2.98 us
  transfers between devices with their start and end apart: 16, of which 9 were waited for; matrix products, arithmetic and copies ran while one was open for 2% of the time, Pallas kernels for 49%

profile of v3, /device:TPU:0, one launch (start us, length us, event | category | flops | bytes accessed | tf_op | source)
XLA Modules:
  0.0 94.3 jit_solution(6446185981067250636)
XLA Ops:
  0.0 3.0 %relayout_high.1 = (bf16[2,2,3,16,2048]{4,3,2,1,0:T(8,128)(2,1)}, bf16[2,2,3,16,2048]{4,3,2,1,0:T(8,128)(2,1)S(1)}, bf16[2,2,3,16,2048]{4,3,2,1,0:T(8,128)(2,1)S...) custom-call(bf16[16,2,3,8,2048]{4,3,2,1,0:T(8,128)(2,1)} %in_ref.2), custom_call_target="tpu_custom_call" | custom-call | tf_op jit(solution)/shard_map/relayout_high/pallas_call | solution.py:99
  3.8 2.0 %collective-permute-start.4 = (bf16[2,2,3,16,2048]{4,3,2,1,0:T(8,128)(2,1)}, bf16[2,2,3,16,2048]{4,3,2,1,0:T(8,128)(2,1)}, u32[]{:S(2)}, u32[]{:S(2)}) collective-permute-start(bf16[2,2,3,16,2048]{4,3,2,1,0:T(8,128)(2,1)} %get-tuple-element.54.refs_0_), channel_id=1, source_target_pairs={{0,64},{32,96},{64,0},{96,32},{1,65},{33,97},{65,1},{97,33},{2,66}... | collective-permute-start | bytes 2359304 | tf_op jit(solution)/shard_map/ppermute | solution.py:37
  5.8 2.0 %collective-permute-start.2 = (bf16[2,2,3,16,2048]{4,3,2,1,0:T(8,128)(2,1)S(1)}, bf16[2,2,3,16,2048]{4,3,2,1,0:T(8,128)(2,1)S(1)}, u32[]{:S(2)}, u32[]{:S(2)}) collective-permute-start(bf16[2,2,3,16,2048]{4,3,2,1,0:T(8,128)(2,1)S(1)} %get-tuple-element.50.refs_0_), channel_id=1, source_target_pairs={{0,64},{32,96},{64,0},{96,32},{1,65},{33,97},{65,1},{97,33},{2,66}... | collective-permute-start | bytes 2359304 | tf_op jit(solution)/shard_map/ppermute | solution.py:37
  9.6 9.9 %relayout_low.2 = (bf16[4,3,2,4,16,2048]{5,4,3,2,1,0:T(8,128)(2,1)}, bf16[4,3,2,4,16,2048]{5,4,3,2,1,0:T(8,128)(2,1)S(1)}, f32[8,128]{1,0:T(8,128)S(1)}) custom-call(bf16[16,4,2,3,8,2048]{5,4,3,2,1,0:T(8,128)(2,1)} %in_ref.3, f32[8,128]{1,0:T(8,128)S(1)} %get-tuple-element.45.after_ref), custom_call_target="tpu_custom_call" | custom-call | tf_op jit(solution)/shard_map/relayout_low/pallas_call | solution.py:132
  19.8 9.9 %relayout_low.3 = (bf16[4,3,2,4,16,2048]{5,4,3,2,1,0:T(8,128)(2,1)}, bf16[4,3,2,4,16,2048]{5,4,3,2,1,0:T(8,128)(2,1)S(1)}, f32[8,128]{1,0:T(8,128)S(1)}) custom-call(bf16[16,4,2,3,8,2048]{5,4,3,2,1,0:T(8,128)(2,1)} %collective-permute-done.in_ref, f32[8,128]{1,0:T(8,128)S(1)} %get-tuple-element.47.after_ref), custom_call_target="tpu_custom_call" | custom-call | tf_op jit(solution)/shard_map/relayout_low/pallas_call | solution.py:132
  29.7 7.2 %contract_0_2.2 = (bf16[2,4,2,64,128]{4,3,2,1,0:T(8,128)(2,1)S(1)}, f32[8,128]{1,0:T(8,128)S(1)}) custom-call(s32[8,256]{1,0:T(8,128)S(1)} %broadcast.183.pat_ref, f32[8,2048]{1,0:T(8,128)S(1)} %get-tuple-element.86.cos_ref, f32[8,2048]{1,0:T(8,128)S(1)} %get-tuple-element.85.sin_ref, bf16[4,3,128,2048]{3,2,1,0:T(8,128)(2,1)} %bitcast.21, ...), custom_call_target="tpu_custom_call" | custom-call | tf_op jit(solution)/shard_map/contract_0_2/pallas_call | solution.py:256
  37.0 1.7 %collective-permute-start.5 = (bf16[2,4,2,64,128]{4,3,2,1,0:T(8,128)(2,1)S(1)}, bf16[2,4,2,64,128]{4,3,2,1,0:T(8,128)(2,1)S(1)}, u32[]{:S(2)}, u32[]{:S(2)}) collective-permute-start(bf16[2,4,2,64,128]{4,3,2,1,0:T(8,128)(2,1)S(1)} %get-tuple-element.58), channel_id=1, source_target_pairs={{0,8},{1,9},{2,10},{3,11},{4,12},{5,13},{6,14},{7,15},{8,0},{9,1},... | collective-permute-start | bytes 786440 | tf_op jit(solution)/shard_map/ppermute | solution.py:33
  38.7 2.5 %collective-permute-done.3.refs_1_ = bf16[2,2,3,16,2048]{4,3,2,1,0:T(8,128)(2,1)S(1)} collective-permute-done((bf16[2,2,3,16,2048]{4,3,2,1,0:T(8,128)(2,1)S(1)}, bf16[2,2,3,16,2048]{4,3,2,1,0:T(8,128)(2,1)S(1)}, u32[]{:S(2)}, u32[]{:S(2)}) %collective-permute-start.3) | collective-permute-done | bytes 786464 | tf_op jit(solution)/shard_map/ppermute | solution.py:37
  41.2 7.3 %contract_2_2.1 = (f32[2,4,2,64,128]{4,3,2,1,0:T(8,128)S(1)}, f32[8,128]{1,0:T(8,128)S(1)}) custom-call(s32[8,256]{1,0:T(8,128)S(1)} %broadcast.183.pat_ref, f32[8,2048]{1,0:T(8,128)S(1)} %get-tuple-element.86.cos_ref, f32[8,2048]{1,0:T(8,128)S(1)} %get-tuple-element.85.sin_ref, bf16[4,3,128,2048]{3,2,1,0:T(8,128)(2,1)} %bitcast.22, ...), custom_call_target="tpu_custom_call" | custom-call | tf_op jit(solution)/shard_map/contract_2_2/pallas_call | solution.py:256
  48.6 3.2 %collective-permute-start.6 = (bf16[1,4,2,64,128]{4,3,2,1,0:T(8,128)(2,1)S(1)}, bf16[1,4,2,64,128]{4,3,2,1,0:T(8,128)(2,1)S(1)}, u32[]{:S(2)}, u32[]{:S(2)}) collective-permute-start(bf16[1,4,2,64,128]{4,3,2,1,0:T(8,128)(2,1)S(1)} %get-tuple-element.61), channel_id=1, source_target_pairs={{0,24},{1,25},{2,26},{3,27},{4,28},{5,29},{6,30},{7,31},{8,16},{9,... | collective-permute-start | bytes 393224 | tf_op jit(solution)/shard_map/ppermute | solution.py:33
  51.8 1.8 %collective-permute-start.8 = (bf16[1,2,3,16,2048]{4,3,2,1,0:T(8,128)(2,1)S(1)}, bf16[1,2,3,16,2048]{4,3,2,1,0:T(8,128)(2,1)S(1)}, u32[]{:S(2)}, u32[]{:S(2)}) collective-permute-start(bf16[1,2,3,16,2048]{4,3,2,1,0:T(8,128)(2,1)S(1)} %copy-done.1), channel_id=1, source_target_pairs={{0,64},{32,96},{64,0},{96,32},{1,65},{33,97},{65,1},{97,33},{2,66}... | collective-permute-start | bytes 1179656 | tf_op jit(solution)/shard_map/ppermute | solution.py:37
  55.0 3.0 %collective-permute-done.2.refs_1_ = bf16[2,2,3,16,2048]{4,3,2,1,0:T(8,128)(2,1)S(1)} collective-permute-done((bf16[2,2,3,16,2048]{4,3,2,1,0:T(8,128)(2,1)S(1)}, bf16[2,2,3,16,2048]{4,3,2,1,0:T(8,128)(2,1)S(1)}, u32[]{:S(2)}, u32[]{:S(2)}) %collective-permute-start.2) | collective-permute-done | bytes 786464 | tf_op jit(solution)/shard_map/ppermute | solution.py:37
  58.1 5.1 %contract_0_2.3 = (bf16[2,4,2,64,128]{4,3,2,1,0:T(8,128)(2,1)S(1)}, f32[8,128]{1,0:T(8,128)S(1)}) custom-call(s32[8,256]{1,0:T(8,128)S(1)} %broadcast.183.pat_ref, f32[8,2048]{1,0:T(8,128)S(1)} %get-tuple-element.86.cos_ref, f32[8,2048]{1,0:T(8,128)S(1)} %get-tuple-element.85.sin_ref, bf16[4,3,128,2048]{3,2,1,0:T(8,128)(2,1)S(1)} %bitcast.10, ...), custom_call_target="tpu_custom_call" | custom-call | tf_op jit(solution)/shard_map/contract_0_2/pallas_call | solution.py:256
  63.2 1.7 %collective-permute-start.7 = (bf16[2,4,2,64,128]{4,3,2,1,0:T(8,128)(2,1)S(1)}, bf16[2,4,2,64,128]{4,3,2,1,0:T(8,128)(2,1)S(1)}, u32[]{:S(2)}, u32[]{:S(2)}) collective-permute-start(bf16[2,4,2,64,128]{4,3,2,1,0:T(8,128)(2,1)S(1)} %get-tuple-element.64), channel_id=1, source_target_pairs={{0,8},{1,9},{2,10},{3,11},{4,12},{5,13},{6,14},{7,15},{8,0},{9,1},... | collective-permute-start | bytes 786440 | tf_op jit(solution)/shard_map/ppermute | solution.py:33
  65.0 1.8 %collective-permute-start.1 = (bf16[1,2,3,16,2048]{4,3,2,1,0:T(8,128)(2,1)S(1)}, bf16[1,2,3,16,2048]{4,3,2,1,0:T(8,128)(2,1)S(1)}, u32[]{:S(2)}, u32[]{:S(2)}) collective-permute-start(bf16[1,2,3,16,2048]{4,3,2,1,0:T(8,128)(2,1)S(1)} %get-tuple-element.49.refs_0_), channel_id=1, source_target_pairs={{0,64},{32,96},{64,0},{96,32},{1,65},{33,97},{65,1},{97,33},{2,66}... | collective-permute-start | bytes 1179656 | tf_op jit(solution)/shard_map/ppermute | solution.py:37
  66.8 1.5 %collective-permute-start.9 = (bf16[2,2,64,128]{3,2,1,0:T(8,128)(2,1)S(1)}, bf16[2,2,64,128]{3,2,1,0:T(8,128)(2,1)S(1)}, u32[]{:S(2)}, u32[]{:S(2)}) collective-permute-start(bf16[2,2,64,128]{3,2,1,0:T(8,128)(2,1)S(1)} %get-tuple-element.69), channel_id=1, source_target_pairs={{0,1},{1,0},{2,3},{3,2},{4,5},{5,4},{6,7},{7,6},{8,9},{9,8},{10,11... | collective-permute-start | bytes 196616 | tf_op jit(solution)/shard_map/ppermute | solution.py:33
  68.3 2.7 %contract_2_1.1 = (f32[1,4,2,64,128]{4,3,2,1,0:T(8,128)S(1)}, f32[8,128]{1,0:T(8,128)S(1)}) custom-call(s32[8,256]{1,0:T(8,128)S(1)} %broadcast.183.pat_ref, f32[8,2048]{1,0:T(8,128)S(1)} %get-tuple-element.86.cos_ref, f32[8,2048]{1,0:T(8,128)S(1)} %get-tuple-element.85.sin_ref, bf16[4,3,128,2048]{3,2,1,0:T(8,128)(2,1)S(1)} %bitcast.11, ...), custom_call_target="tpu_custom_call" | custom-call | tf_op jit(solution)/shard_map/contract_2_1/pallas_call | solution.py:256
  71.2 3.0 %collective-permute-start.10 = (bf16[1,4,2,64,128]{4,3,2,1,0:T(8,128)(2,1)S(1)}, bf16[1,4,2,64,128]{4,3,2,1,0:T(8,128)(2,1)S(1)}, u32[]{:S(2)}, u32[]{:S(2)}) collective-permute-start(bf16[1,4,2,64,128]{4,3,2,1,0:T(8,128)(2,1)S(1)} %get-tuple-element.72), channel_id=1, source_target_pairs={{0,24},{1,25},{2,26},{3,27},{4,28},{5,29},{6,30},{7,31},{8,16},{9,... | collective-permute-start | bytes 393224 | tf_op jit(solution)/shard_map/ppermute | solution.py:33
  74.2 2.8 %collective-permute-start.11 = (bf16[1,2,64,128]{3,2,1,0:T(8,128)(2,1)S(1)}, bf16[1,2,64,128]{3,2,1,0:T(8,128)(2,1)S(1)}, u32[]{:S(2)}, u32[]{:S(2)}) collective-permute-start(bf16[1,2,64,128]{3,2,1,0:T(8,128)(2,1)S(1)} %get-tuple-element.74), channel_id=1, source_target_pairs={{0,3},{1,2},{2,1},{3,0},{4,7},{5,6},{6,5},{7,4},{8,11},{9,10},{10,... | collective-permute-start | bytes 98312 | tf_op jit(solution)/shard_map/ppermute | solution.py:33
  77.0 2.4 %collective-permute-done.11.refs_1_ = bf16[1,2,64,128]{3,2,1,0:T(8,128)(2,1)S(1)} collective-permute-done((bf16[1,2,64,128]{3,2,1,0:T(8,128)(2,1)S(1)}, bf16[1,2,64,128]{3,2,1,0:T(8,128)(2,1)S(1)}, u32[]{:S(2)}, u32[]{:S(2)}) %collective-permute-start.11) | collective-permute-done | bytes 32800 | tf_op jit(solution)/shard_map/ppermute | solution.py:33
  79.4 2.7 %contract_3_1.1 = (bf16[2,1,2,64,128]{4,3,2,1,0:T(8,128)(2,1)S(1)}, f32[2,1,2,64,128]{4,3,2,1,0:T(8,128)S(1)}, f32[8,128]{1,0:T(8,128)S(1)}) custom-call(s32[8,256]{1,0:T(8,128)S(1)} %broadcast.183.pat_ref, f32[8,2048]{1,0:T(8,128)S(1)} %get-tuple-element.86.cos_ref, f32[8,2048]{1,0:T(8,128)S(1)} %get-tuple-element.85.sin_ref, ...), custom_call_target="tpu_custom_call" | custom-call | tf_op jit(solution)/shard_map/contract_3_1/pallas_call | solution.py:256
  82.5 3.6 %collective-permute-start.14 = (f32[1,2,64,128]{3,2,1,0:T(8,128)S(1)}, f32[1,2,64,128]{3,2,1,0:T(8,128)S(1)}, u32[]{:S(2)}, u32[]{:S(2)}) collective-permute-start(f32[1,2,64,128]{3,2,1,0:T(8,128)S(1)} %get-tuple-element.82), channel_id=1, source_target_pairs={{0,4},{1,5},{2,6},{3,7},{4,0},{5,1},{6,2},{7,3},{8,12},{9,13},{10,... | collective-permute-start | bytes 196616 | tf_op jit(solution)/shard_map/ppermute | solution.py:33
  87.0 2.8 %collective-permute-start.13 = (bf16[1,2,64,128]{3,2,1,0:T(8,128)(2,1)S(1)}, bf16[1,2,64,128]{3,2,1,0:T(8,128)(2,1)S(1)}, u32[]{:S(2)}, u32[]{:S(2)}) collective-permute-start(bf16[1,2,64,128]{3,2,1,0:T(8,128)(2,1)S(1)} %get-tuple-element.81), channel_id=1, source_target_pairs={{0,3},{1,2},{2,1},{3,0},{4,7},{5,6},{6,5},{7,4},{8,11},{9,10},{10,... | collective-permute-start | bytes 98312 | tf_op jit(solution)/shard_map/ppermute | solution.py:33
  89.8 2.4 %collective-permute-done.13.last_ref = bf16[1,2,64,128]{3,2,1,0:T(8,128)(2,1)S(1)} collective-permute-done((bf16[1,2,64,128]{3,2,1,0:T(8,128)(2,1)S(1)}, bf16[1,2,64,128]{3,2,1,0:T(8,128)(2,1)S(1)}, u32[]{:S(2)}, u32[]{:S(2)}) %collective-permute-start.13) | collective-permute-done | bytes 32800 | tf_op jit(solution)/shard_map/ppermute | solution.py:33
  (44 shorter events, 8.1 us)
Async XLA Ops:
  0.0 19.8 %collective-permute-start = (bf16[16,4,2,3,8,2048]{5,4,3,2,1,0:T(8,128)(2,1)}, bf16[16,4,2,3,8,2048]{5,4,3,2,1,0:T(8,128)(2,1)}, u32[]{:S(2)}, u32[]{:S(2)}) collective-permute-start(bf16[16,4,2,3,8,2048]{5,4,3,2,1,0:T(8,128)(2,1)} %in_ref.3), channel_id=1, source_target_pairs={{0,32},{32,0},{64,96},{96,64},{1,33},{33,1},{65,97},{97,65},{2,34}... | collective-permute-start | bytes 37748744 | tf_op jit(solution)/shard_map/ppermute | solution.py:37
  3.0 0.8 copy-start
  3.8 26.0 %collective-permute-start.4 = (bf16[2,2,3,16,2048]{4,3,2,1,0:T(8,128)(2,1)}, bf16[2,2,3,16,2048]{4,3,2,1,0:T(8,128)(2,1)}, u32[]{:S(2)}, u32[]{:S(2)}) collective-permute-start(bf16[2,2,3,16,2048]{4,3,2,1,0:T(8,128)(2,1)} %get-tuple-element.54.refs_0_), channel_id=1, source_target_pairs={{0,64},{32,96},{64,0},{96,32},{1,65},{33,97},{65,1},{97,33},{2,66}... | collective-permute-start | bytes 2359304 | tf_op jit(solution)/shard_map/ppermute | solution.py:37
  5.8 35.5 %collective-permute-start.3 = (bf16[2,2,3,16,2048]{4,3,2,1,0:T(8,128)(2,1)S(1)}, bf16[2,2,3,16,2048]{4,3,2,1,0:T(8,128)(2,1)S(1)}, u32[]{:S(2)}, u32[]{:S(2)}) collective-permute-start(bf16[2,2,3,16,2048]{4,3,2,1,0:T(8,128)(2,1)S(1)} %get-tuple-element.53.refs_0_), channel_id=1, source_target_pairs={{0,64},{32,96},{64,0},{96,32},{1,65},{33,97},{65,1},{97,33},{2,66}... | collective-permute-start | bytes 2359304 | tf_op jit(solution)/shard_map/ppermute | solution.py:37
  5.8 52.3 %collective-permute-start.2 = (bf16[2,2,3,16,2048]{4,3,2,1,0:T(8,128)(2,1)S(1)}, bf16[2,2,3,16,2048]{4,3,2,1,0:T(8,128)(2,1)S(1)}, u32[]{:S(2)}, u32[]{:S(2)}) collective-permute-start(bf16[2,2,3,16,2048]{4,3,2,1,0:T(8,128)(2,1)S(1)} %get-tuple-element.50.refs_0_), channel_id=1, source_target_pairs={{0,64},{32,96},{64,0},{96,32},{1,65},{33,97},{65,1},{97,33},{2,66}... | collective-permute-start | bytes 2359304 | tf_op jit(solution)/shard_map/ppermute | solution.py:37
  9.5 9.9 %copy-start.2 = (s32[3,2048]{1,0:T(4,128)S(1)}, s32[3,2048]{1,0:T(4,128)}, u32[]{:S(2)}) copy-start(s32[3,2048]{1,0:T(4,128)} %pad_add_fusion) | copy-start | bytes 73732
  9.5 9.9 %copy-start.3 = (s32[8,3]{0,1:T(4,128)S(1)}, s32[8,3]{0,1:T(4,128)}, u32[]{:S(2)}) copy-start(s32[8,3]{0,1:T(4,128)} %param.7) | copy-start | bytes 292
  37.0 11.6 %collective-permute-start.5 = (bf16[2,4,2,64,128]{4,3,2,1,0:T(8,128)(2,1)S(1)}, bf16[2,4,2,64,128]{4,3,2,1,0:T(8,128)(2,1)S(1)}, u32[]{:S(2)}, u32[]{:S(2)}) collective-permute-start(bf16[2,4,2,64,128]{4,3,2,1,0:T(8,128)(2,1)S(1)} %get-tuple-element.58), channel_id=1, source_target_pairs={{0,8},{1,9},{2,10},{3,11},{4,12},{5,13},{6,14},{7,15},{8,0},{9,1},... | collective-permute-start | bytes 786440 | tf_op jit(solution)/shard_map/ppermute | solution.py:33
  41.2 10.6 %copy-start.1 = (bf16[1,2,3,16,2048]{4,3,2,1,0:T(8,128)(2,1)S(1)}, bf16[1,2,3,16,2048]{4,3,2,1,0:T(8,128)(2,1)}, u32[]{:S(2)}) copy-start(bf16[1,2,3,16,2048]{4,3,2,1,0:T(8,128)(2,1)} %copy-done) | copy-start | bytes 1179652
  48.6 6.4 %collective-permute-start.6 = (bf16[1,4,2,64,128]{4,3,2,1,0:T(8,128)(2,1)S(1)}, bf16[1,4,2,64,128]{4,3,2,1,0:T(8,128)(2,1)S(1)}, u32[]{:S(2)}, u32[]{:S(2)}) collective-permute-start(bf16[1,4,2,64,128]{4,3,2,1,0:T(8,128)(2,1)S(1)} %get-tuple-element.61), channel_id=1, source_target_pairs={{0,24},{1,25},{2,26},{3,27},{4,28},{5,29},{6,30},{7,31},{8,16},{9,... | collective-permute-start | bytes 393224 | tf_op jit(solution)/shard_map/ppermute | solution.py:33
  51.8 16.5 %collective-permute-start.8 = (bf16[1,2,3,16,2048]{4,3,2,1,0:T(8,128)(2,1)S(1)}, bf16[1,2,3,16,2048]{4,3,2,1,0:T(8,128)(2,1)S(1)}, u32[]{:S(2)}, u32[]{:S(2)}) collective-permute-start(bf16[1,2,3,16,2048]{4,3,2,1,0:T(8,128)(2,1)S(1)} %copy-done.1), channel_id=1, source_target_pairs={{0,64},{32,96},{64,0},{96,32},{1,65},{33,97},{65,1},{97,33},{2,66}... | collective-permute-start | bytes 1179656 | tf_op jit(solution)/shard_map/ppermute | solution.py:37
  63.2 8.0 %collective-permute-start.7 = (bf16[2,4,2,64,128]{4,3,2,1,0:T(8,128)(2,1)S(1)}, bf16[2,4,2,64,128]{4,3,2,1,0:T(8,128)(2,1)S(1)}, u32[]{:S(2)}, u32[]{:S(2)}) collective-permute-start(bf16[2,4,2,64,128]{4,3,2,1,0:T(8,128)(2,1)S(1)} %get-tuple-element.64), channel_id=1, source_target_pairs={{0,8},{1,9},{2,10},{3,11},{4,12},{5,13},{6,14},{7,15},{8,0},{9,1},... | collective-permute-start | bytes 786440 | tf_op jit(solution)/shard_map/ppermute | solution.py:33
  65.0 14.4 %collective-permute-start.1 = (bf16[1,2,3,16,2048]{4,3,2,1,0:T(8,128)(2,1)S(1)}, bf16[1,2,3,16,2048]{4,3,2,1,0:T(8,128)(2,1)S(1)}, u32[]{:S(2)}, u32[]{:S(2)}) collective-permute-start(bf16[1,2,3,16,2048]{4,3,2,1,0:T(8,128)(2,1)S(1)} %get-tuple-element.49.refs_0_), channel_id=1, source_target_pairs={{0,64},{32,96},{64,0},{96,32},{1,65},{33,97},{65,1},{97,33},{2,66}... | collective-permute-start | bytes 1179656 | tf_op jit(solution)/shard_map/ppermute | solution.py:37
  66.8 4.3 %collective-permute-start.9 = (bf16[2,2,64,128]{3,2,1,0:T(8,128)(2,1)S(1)}, bf16[2,2,64,128]{3,2,1,0:T(8,128)(2,1)S(1)}, u32[]{:S(2)}, u32[]{:S(2)}) collective-permute-start(bf16[2,2,64,128]{3,2,1,0:T(8,128)(2,1)S(1)} %get-tuple-element.69), channel_id=1, source_target_pairs={{0,1},{1,0},{2,3},{3,2},{4,5},{5,4},{6,7},{7,6},{8,9},{9,8},{10,11... | collective-permute-start | bytes 196616 | tf_op jit(solution)/shard_map/ppermute | solution.py:33
  71.2 8.2 %collective-permute-start.10 = (bf16[1,4,2,64,128]{4,3,2,1,0:T(8,128)(2,1)S(1)}, bf16[1,4,2,64,128]{4,3,2,1,0:T(8,128)(2,1)S(1)}, u32[]{:S(2)}, u32[]{:S(2)}) collective-permute-start(bf16[1,4,2,64,128]{4,3,2,1,0:T(8,128)(2,1)S(1)} %get-tuple-element.72), channel_id=1, source_target_pairs={{0,24},{1,25},{2,26},{3,27},{4,28},{5,29},{6,30},{7,31},{8,16},{9,... | collective-permute-start | bytes 393224 | tf_op jit(solution)/shard_map/ppermute | solution.py:33
  74.2 5.1 %collective-permute-start.11 = (bf16[1,2,64,128]{3,2,1,0:T(8,128)(2,1)S(1)}, bf16[1,2,64,128]{3,2,1,0:T(8,128)(2,1)S(1)}, u32[]{:S(2)}, u32[]{:S(2)}) collective-permute-start(bf16[1,2,64,128]{3,2,1,0:T(8,128)(2,1)S(1)} %get-tuple-element.74), channel_id=1, source_target_pairs={{0,3},{1,2},{2,1},{3,0},{4,7},{5,6},{6,5},{7,4},{8,11},{9,10},{10,... | collective-permute-start | bytes 98312 | tf_op jit(solution)/shard_map/ppermute | solution.py:33
  82.1 4.3 %collective-permute-start.12 = (bf16[2,1,2,64,128]{4,3,2,0,1:T(8,128)(2,1)S(1)}, bf16[2,1,2,64,128]{4,3,2,0,1:T(8,128)(2,1)S(1)}, u32[]{:S(2)}, u32[]{:S(2)}) collective-permute-start(bf16[2,1,2,64,128]{4,3,2,0,1:T(8,128)(2,1)S(1)} %bitcast.20), channel_id=1, source_target_pairs={{0,1},{1,0},{2,3},{3,2},{4,5},{5,4},{6,7},{7,6},{8,9},{9,8},{10,11... | collective-permute-start | bytes 196616 | tf_op jit(solution)/shard_map/ppermute | solution.py:33
  82.5 7.4 %collective-permute-start.14 = (f32[1,2,64,128]{3,2,1,0:T(8,128)S(1)}, f32[1,2,64,128]{3,2,1,0:T(8,128)S(1)}, u32[]{:S(2)}, u32[]{:S(2)}) collective-permute-start(f32[1,2,64,128]{3,2,1,0:T(8,128)S(1)} %get-tuple-element.82), channel_id=1, source_target_pairs={{0,4},{1,5},{2,6},{3,7},{4,0},{5,1},{6,2},{7,3},{8,12},{9,13},{10,... | collective-permute-start | bytes 196616 | tf_op jit(solution)/shard_map/ppermute | solution.py:33
  87.0 5.1 %collective-permute-start.13 = (bf16[1,2,64,128]{3,2,1,0:T(8,128)(2,1)S(1)}, bf16[1,2,64,128]{3,2,1,0:T(8,128)(2,1)S(1)}, u32[]{:S(2)}, u32[]{:S(2)}) collective-permute-start(bf16[1,2,64,128]{3,2,1,0:T(8,128)(2,1)S(1)} %get-tuple-element.81), channel_id=1, source_target_pairs={{0,3},{1,2},{2,1},{3,0},{4,7},{5,6},{6,5},{7,4},{8,11},{9,10},{10,... | collective-permute-start | bytes 98312 | tf_op jit(solution)/shard_map/ppermute | solution.py:33
  92.2 1.3 %collective-permute-start.15 = (f32[2,32,128]{2,1,0:T(8,128)S(1)}, f32[2,32,128]{2,1,0:T(8,128)S(1)}, u32[]{:S(2)}, u32[]{:S(2)}) collective-permute-start(f32[2,32,128]{2,1,0:T(8,128)S(1)} %get-tuple-element.84), channel_id=1, source_target_pairs={{0,32},{32,0},{64,96},{96,64},{1,33},{33,1},{65,97},{97,65},{2,34}... | collective-permute-start | bytes 98312 | tf_op jit(solution)/shard_map/ppermute | solution.py:37

commit v4 on v3

--- a/solution.py
+++ b/solution.py
@@ -155,8 +155,10 @@
     return turned, token
 
 
-def contract_body(by_part, added, pat_ref, cos_ref, sin_ref, own_ref, oth_ref, *refs):
-    highs, adds, outs = refs[:2], refs[2 : 2 + added], refs[3 + added : -2]
+def contract_body(by_part, blocks, based, added, pat_ref, cos_ref, sin_ref, own_ref, oth_ref, *refs):
+    highs, refs = refs[: len(blocks)], refs[len(blocks) :]
+    base_ref, refs = (refs[0], refs[1:]) if based else (None, refs)
+    adds, outs = refs[:added], refs[1 + added : -2]
     token_ref, acc_ref = refs[-2:]
     token_ref[...] = jnp.zeros_like(token_ref)
     n_moms, count = cos_ref.shape
@@ -189,8 +191,20 @@
 
     lax.fori_loop(0, 3, one, 0)
     half = 128
-    for block in range(2):
-        base = block * 256
+
+    def put(k, block, result):
+        for add in adds:
+            result = result + add[add.shape[0] - 1, k, block].astype(jnp.float32)
+        if by_part:
+            outs[k // 2][k % 2, 0, block] = result.astype(outs[k // 2].dtype)
+        else:
+            outs[0][0, k, block] = result.astype(outs[0].dtype)
+
+    if based:
+        for k in range(NX):
+            put(k, 0, base_ref[0, k, 0])
+    for place, block in enumerate(blocks):
+        base = place * 256
         pattern = pat_ref[0:1, block * half : block * half + half]
         is_spin = [jnp.broadcast_to(pattern == a, (16, half)) for a in range(4)]
         low_pair = pattern < 2
@@ -224,25 +238,16 @@
             for g in range(4):
                 turned = pltpu.roll(stacked[g], lax.rem(g - group + NX, NX) * 32, 1)
                 result = turned if result is None else jnp.where(lane == g, turned, result)
-            for add in adds:
-                result = result + add[add.shape[0] - 1, k, block].astype(jnp.float32)
-            if by_part == "each":
-                outs[k][0, block] = result.astype(outs[k].dtype)
-            elif by_part:
-                outs[k // 2][k % 2, 0, block] = result.astype(outs[k // 2].dtype)
-            else:
-                outs[0][0, k, block] = result.astype(outs[0].dtype)
-
-
-def contract(tables, lows, own, received, first, by_part, sent, after, limit, adds=()):
+            put(k, block, result)
+
+
+def contract(tables, lows, own, received, first, by_part, sent, after, limit, adds=(), base=None):
     colours, rows, count = lows[0].shape[1:]
-    number = own.shape[0]
-    unit = (2, 64, 128)
-    if by_part == "each":
-        kinds = [sent] * (NX - 1) + [jnp.float32]
-        shapes = [jax.ShapeDtypeStruct((number,) + unit, kind) for kind in kinds]
-        out_specs = [pl.BlockSpec((1,) + unit, lambda i: (i, 0, 0, 0))] * NX
-    elif by_part:
+    highs = [h for h in (own, received) if h is not None]
+    blocks = tuple(b for b, h in enumerate((own, received)) if h is not None)
+    number = highs[0].shape[0]
+    unit = (1 if received is None else 2, 64, 128)
+    if by_part:
         shapes = [
             jax.ShapeDtypeStruct((2, number) + unit, sent),
             jax.ShapeDtypeStruct((2, number) + unit, jnp.float32),
@@ -253,20 +258,22 @@
         out_specs = [pl.BlockSpec((1, NX) + unit, lambda i: (i, 0, 0, 0, 0))]
     high_spec = pl.BlockSpec((1, 2, colours, 16, count), lambda i: (i, 0, 0, 0, 0))
     low_spec = pl.BlockSpec((1, colours, rows, count), lambda i: (first + i, 0, 0, 0))
-    return pl.pallas_call(
-        functools.partial(contract_body, by_part, len(adds)),
+    extra = list(adds) if base is None else [base, *adds]
+    return pl.pallas_call(
+        functools.partial(contract_body, by_part, blocks, base is not None, len(adds)),
         grid=(number,),
         in_specs=[whole(t.shape) for t in tables]
-        + [low_spec, low_spec, high_spec, high_spec]
-        + [whole(a.shape) for a in adds]
+        + [low_spec, low_spec]
+        + [high_spec] * len(highs)
+        + [whole(a.shape) for a in extra]
         + [whole((8, 128))],
         out_specs=out_specs + [whole((8, 128))],
         out_shape=shapes + [TOKEN],
-        scratch_shapes=[pltpu.VMEM((256, 512), jnp.float32)],
+        scratch_shapes=[pltpu.VMEM((256, 256 * len(highs)), jnp.float32)],
         compiler_params=pltpu.CompilerParams(vmem_limit_bytes=limit),
         cost_estimate=TINY,
         name=f"contract_{first}_{number}",
-    )(*tables, *lows, own, received, *adds, after)
+    )(*tables, *lows, *highs, *extra, after)
 
 
 def fold_body(number, *refs):
@@ -378,7 +385,8 @@
     wide, narrow = jnp.float32, jnp.bfloat16
     *high, token = relayout_high(high_modes, (2, 2, 2, 1, 1))
     arrived = [flip(chunk, 2) for chunk in high]
-    low_oth = flip(low_modes, 1)
+    gated, token = lax.optimization_barrier((low_modes, token))
+    low_oth = flip(gated, 1)
     low_own, token = relayout_low(low_modes, token, (4, 4))
     low_oth, token = relayout_low(low_oth, token, (4, 4))
     many, few = zip(low_own, low_oth)
@@ -399,23 +407,25 @@
     )
     away, far, token = fold((far, far_got), narrow, token)
     far_got = trade(away, 3, 0, 0)
+    base, token = contract(tables, few, high[3], None, 2, False, wide, token, FEW_LIMIT)
     away, far, token = fold((far[0], far_got[0]), narrow, token)
     far_got = trade(away, 0, 0, 1)
+    last_base, token = contract(tables, few, high[4], None, 3, False, wide, token, FEW_LIMIT)
+    away, far, token = fold((far, far_got), narrow, token)
+    far_got = trade(away, 0, 0, 3)
     away, token = contract(
         tables, few, high[2], arrived[2], 0, False, narrow, token, FEW_LIMIT
     )
     near_got = trade(away, 1, 0, 0)
     near, token = contract(
-        tables, few, high[3], arrived[3], 2, False, wide, token, FEW_LIMIT
-    )
-    away, far, token = fold((far, far_got), narrow, token)
-    far_got = trade(away, 0, 0, 3)
+        tables, few, None, arrived[3], 2, False, wide, token, FEW_LIMIT, (), base
+    )
+    away, token = plus((far, far_got), wide, token)
+    across = trade(away, 0, 1, 0)
     away, token = plus((near, near_got), narrow, token)
     adds = (near_got, trade(away, 3, 0, 0))
-    away, token = plus((far, far_got), wide, token)
-    across = trade(away, 0, 1, 0)
     away, near, token = contract(
-        tables, few, high[4], arrived[4], 3, True, narrow, token, FEW_LIMIT, adds
+        tables, few, None, arrived[4], 3, True, narrow, token, FEW_LIMIT, adds, last_base
     )
     last_got = trade(away, 0, 0, 1)
     away, near, token = fold((near[:, 0], last_got[:, 0]), narrow, token)

time: 95.7 us -> 93.7 us (0.979)
  starting transfers between devices: 28.4 us -> 25.9 us
    ppermute x9, starting transfers between devices: 20.6 us -> 17.8 us  [trade(): return lax.ppermute(block, 'site', route)]
    ppermute x7, waiting for transfers between devices: 6.77 us -> 4.65 us  [flip(): return lax.ppermute(block, 'mode', [(i, i ^ mask) for i in range(4)])]
    ppermute x9, waiting for transfers between devices: 6.73 us -> 8.85 us  [trade(): return lax.ppermute(block, 'site', route)]
    pallas_call x5 -> x7, Pallas kernels: 25 us -> 26.6 us  [contract(): pl.pallas_call(functools.partial(contract_body, by_part, blocks, base is...]
  transfers between devices with their start and end apart: 16 -> 16, of which waited for: 9 -> 7; matrix products, arithmetic and copies ran while one was open for 2% -> 2% of each run, Pallas kernels for 49% -> 49%
where the time goes in v4:
time: 93.7 us; the launch traced here: 92.4 us
  Pallas kernels  50 us (53%)
  starting transfers between devices  25.9 us (28%)
  waiting for transfers between devices  13.5 us (14%)
  local copies, waits for them, and re-layouts  1.74 us (2%)
  other arithmetic  1.12 us (1%)
    pallas_call x7, Pallas kernels, contract(): pl.pallas_call(functools.partial(contract_body, by_part, blocks, base is...  26.6 us
    pallas_call x2, Pallas kernels, relayout_low(): pl.pallas_call(relayout_low_body, grid=(colours, two), in_specs=[pl.Block...  19.8 us
    ppermute x9, starting transfers between devices, trade(): return lax.ppermute(block, 'site', route)  17.8 us
    ppermute x9, waiting for transfers between devices, trade(): return lax.ppermute(block, 'site', route)  8.85 us
    ppermute x7, starting transfers between devices, flip(): return lax.ppermute(block, 'mode', [(i, i ^ mask) for i in range(4)])  8.02 us
    ppermute x7, waiting for transfers between devices, flip(): return lax.ppermute(block, 'mode', [(i, i ^ mask) for i in range(4)])  4.65 us
    pallas_call x1, Pallas kernels, relayout_high(): pl.pallas_call(relayout_high_body, in_specs=[pl.BlockSpec(memory_space=pl...  2.04 us
  transfers between devices with their start and end apart: 16, of which 7 were waited for; matrix products, arithmetic and copies ran while one was open for 2% of the time, Pallas kernels for 49%

profile of v4, /device:TPU:0, one launch (start us, length us, event | category | flops | bytes accessed | tf_op | source)
XLA Modules:
  0.0 92.4 jit_solution(16880380897387748879)
XLA Ops:
  0.0 2.0 %relayout_high.1 = (bf16[2,2,3,16,2048]{4,3,2,1,0:T(8,128)(2,1)S(1)}, bf16[2,2,3,16,2048]{4,3,2,1,0:T(8,128)(2,1)S(1)}, bf16[2,2,3,16,2048]{4,3,2,1,0:T(8,128)(2...) custom-call(bf16[16,2,3,8,2048]{4,3,2,1,0:T(8,128)(2,1)} %in_ref.2), custom_call_target="tpu_custom_call" | custom-call | tf_op jit(solution)/shard_map/relayout_high/pallas_call | solution.py:99
  2.8 2.0 %collective-permute-start.3 = (bf16[2,2,3,16,2048]{4,3,2,1,0:T(8,128)(2,1)S(1)}, bf16[2,2,3,16,2048]{4,3,2,1,0:T(8,128)(2,1)}, u32[]{:S(2)}, u32[]{:S(2)}) collective-permute-start(bf16[2,2,3,16,2048]{4,3,2,1,0:T(8,128)(2,1)S(1)} %get-tuple-element.61.refs_0_), channel_id=1, source_target_pairs={{0,64},{32,96},{64,0},{96,32},{1,65},{33,97},{65,1},{97,33},{2,66}... | collective-permute-start | bytes 2359304 | tf_op jit(solution)/shard_map/ppermute | solution.py:37
  4.9 2.0 %collective-permute-start.6 = (bf16[2,2,3,16,2048]{4,3,2,1,0:T(8,128)(2,1)S(1)}, bf16[2,2,3,16,2048]{4,3,2,1,0:T(8,128)(2,1)S(1)}, u32[]{:S(2)}, u32[]{:S(2)}) collective-permute-start(bf16[2,2,3,16,2048]{4,3,2,1,0:T(8,128)(2,1)S(1)} %get-tuple-element.74.refs_0_), channel_id=1, source_target_pairs={{0,64},{32,96},{64,0},{96,32},{1,65},{33,97},{65,1},{97,33},{2,66}... | collective-permute-start | bytes 2359304 | tf_op jit(solution)/shard_map/ppermute | solution.py:37
  8.6 9.9 %relayout_low.2 = (bf16[4,3,2,4,16,2048]{5,4,3,2,1,0:T(8,128)(2,1)}, bf16[4,3,2,4,16,2048]{5,4,3,2,1,0:T(8,128)(2,1)S(1)}, f32[8,128]{1,0:T(8,128)S(1)}) custom-call(bf16[16,4,2,3,8,2048]{5,4,3,2,1,0:T(8,128)(2,1)} %in_ref.3, f32[8,128]{1,0:T(8,128)S(1)} %get-tuple-element.52.after_ref), custom_call_target="tpu_custom_call" | custom-call | tf_op jit(solution)/shard_map/relayout_low/pallas_call | solution.py:132
  18.9 3.4 %collective-permute-done.in_ref = bf16[16,4,2,3,8,2048]{5,4,3,2,1,0:T(8,128)(2,1)} collective-permute-done((bf16[16,4,2,3,8,2048]{5,4,3,2,1,0:T(8,128)(2,1)}, bf16[16,4,2,3,8,2048]{5,4,3,2,1,0:T(8,128)(2,1)}, u32[]{:S(2)}, u32[]{:S(2)}) %collective-permute-start) | collective-permute-done | bytes 12582944 | tf_op jit(solution)/shard_map/ppermute | solution.py:37
  22.3 9.9 %relayout_low.3 = (bf16[4,3,2,4,16,2048]{5,4,3,2,1,0:T(8,128)(2,1)}, bf16[4,3,2,4,16,2048]{5,4,3,2,1,0:T(8,128)(2,1)S(1)}, f32[8,128]{1,0:T(8,128)S(1)}) custom-call(bf16[16,4,2,3,8,2048]{5,4,3,2,1,0:T(8,128)(2,1)} %collective-permute-done.in_ref, f32[8,128]{1,0:T(8,128)S(1)} %get-tuple-element.55.after_ref), custom_call_target="tpu_custom_call" | custom-call | tf_op jit(solution)/shard_map/relayout_low/pallas_call | solution.py:132
  32.2 7.1 %contract_0_2.2 = (bf16[2,4,2,64,128]{4,3,2,1,0:T(8,128)(2,1)S(1)}, f32[8,128]{1,0:T(8,128)S(1)}) custom-call(s32[8,256]{1,0:T(8,128)S(1)} %broadcast.183.pat_ref, f32[8,2048]{1,0:T(8,128)S(1)} %get-tuple-element.98.cos_ref, f32[8,2048]{1,0:T(8,128)S(1)} %get-tuple-element.97.sin_ref, bf16[4,3,128,2048]{3,2,1,0:T(8,128)(2,1)} %bitcast.25, ...), custom_call_target="tpu_custom_call" | custom-call | tf_op jit(solution)/shard_map/contract_0_2/pallas_call | solution.py:262
  39.3 1.8 %collective-permute-start.4 = (bf16[2,4,2,64,128]{4,3,2,1,0:T(8,128)(2,1)S(1)}, bf16[2,4,2,64,128]{4,3,2,1,0:T(8,128)(2,1)S(1)}, u32[]{:S(2)}, u32[]{:S(2)}) collective-permute-start(bf16[2,4,2,64,128]{4,3,2,1,0:T(8,128)(2,1)S(1)} %get-tuple-element.65), channel_id=1, source_target_pairs={{0,8},{1,9},{2,10},{3,11},{4,12},{5,13},{6,14},{7,15},{8,0},{9,1},... | collective-permute-start | bytes 786440 | tf_op jit(solution)/shard_map/ppermute | solution.py:33
  41.1 7.4 %contract_2_2.1 = (f32[2,4,2,64,128]{4,3,2,1,0:T(8,128)S(1)}, f32[8,128]{1,0:T(8,128)S(1)}) custom-call(s32[8,256]{1,0:T(8,128)S(1)} %broadcast.183.pat_ref, f32[8,2048]{1,0:T(8,128)S(1)} %get-tuple-element.98.cos_ref, f32[8,2048]{1,0:T(8,128)S(1)} %get-tuple-element.97.sin_ref, bf16[4,3,128,2048]{3,2,1,0:T(8,128)(2,1)} %bitcast.26, ...), custom_call_target="tpu_custom_call" | custom-call | tf_op jit(solution)/shard_map/contract_2_2/pallas_call | solution.py:262
  48.5 2.3 %collective-permute-start.5 = (bf16[1,4,2,64,128]{4,3,2,1,0:T(8,128)(2,1)S(1)}, bf16[1,4,2,64,128]{4,3,2,1,0:T(8,128)(2,1)S(1)}, u32[]{:S(2)}, u32[]{:S(2)}) collective-permute-start(bf16[1,4,2,64,128]{4,3,2,1,0:T(8,128)(2,1)S(1)} %get-tuple-element.68), channel_id=1, source_target_pairs={{0,24},{1,25},{2,26},{3,27},{4,28},{5,29},{6,30},{7,31},{8,16},{9,... | collective-permute-start | bytes 393224 | tf_op jit(solution)/shard_map/ppermute | solution.py:33
  50.9 1.9 %collective-permute-start.9 = (bf16[1,2,3,16,2048]{4,3,2,1,0:T(8,128)(2,1)S(1)}, bf16[1,2,3,16,2048]{4,3,2,1,0:T(8,128)(2,1)S(1)}, u32[]{:S(2)}, u32[]{:S(2)}) collective-permute-start(bf16[1,2,3,16,2048]{4,3,2,1,0:T(8,128)(2,1)S(1)} %copy-done.1), channel_id=1, source_target_pairs={{0,64},{32,96},{64,0},{96,32},{1,65},{33,97},{65,1},{97,33},{2,66}... | collective-permute-start | bytes 1179656 | tf_op jit(solution)/shard_map/ppermute | solution.py:37
  52.8 1.7 %contract_2_1.2 = (f32[1,4,1,64,128]{4,3,2,1,0:T(8,128)S(1)}, f32[8,128]{1,0:T(8,128)S(1)}) custom-call(s32[8,256]{1,0:T(8,128)S(1)} %broadcast.183.pat_ref, f32[8,2048]{1,0:T(8,128)S(1)} %get-tuple-element.98.cos_ref, f32[8,2048]{1,0:T(8,128)S(1)} %get-tuple-element.97.sin_ref, bf16[4,3,128,2048]{3,2,1,0:T(8,128)(2,1)S(1)} %bitcast.10, ...), custom_call_target="tpu_custom_call" | custom-call | tf_op jit(solution)/shard_map/contract_2_1/pallas_call | solution.py:262
  55.1 1.6 %collective-permute-start.7 = (bf16[2,2,64,128]{3,2,1,0:T(8,128)(2,1)S(1)}, bf16[2,2,64,128]{3,2,1,0:T(8,128)(2,1)S(1)}, u32[]{:S(2)}, u32[]{:S(2)}) collective-permute-start(bf16[2,2,64,128]{3,2,1,0:T(8,128)(2,1)S(1)} %get-tuple-element.76), channel_id=1, source_target_pairs={{0,1},{1,0},{2,3},{3,2},{4,5},{5,4},{6,7},{7,6},{8,9},{9,8},{10,11... | collective-permute-start | bytes 196616 | tf_op jit(solution)/shard_map/ppermute | solution.py:33
  56.7 1.7 %contract_3_1.2 = (f32[1,4,1,64,128]{4,3,2,1,0:T(8,128)S(1)}, f32[8,128]{1,0:T(8,128)S(1)}) custom-call(s32[8,256]{1,0:T(8,128)S(1)} %broadcast.183.pat_ref, f32[8,2048]{1,0:T(8,128)S(1)} %get-tuple-element.98.cos_ref, f32[8,2048]{1,0:T(8,128)S(1)} %get-tuple-element.97.sin_ref, bf16[4,3,128,2048]{3,2,1,0:T(8,128)(2,1)S(1)} %bitcast.11, ...), custom_call_target="tpu_custom_call" | custom-call | tf_op jit(solution)/shard_map/contract_3_1/pallas_call | solution.py:262
  59.5 5.1 %contract_0_2.3 = (bf16[2,4,2,64,128]{4,3,2,1,0:T(8,128)(2,1)S(1)}, f32[8,128]{1,0:T(8,128)S(1)}) custom-call(s32[8,256]{1,0:T(8,128)S(1)} %broadcast.183.pat_ref, f32[8,2048]{1,0:T(8,128)S(1)} %get-tuple-element.98.cos_ref, f32[8,2048]{1,0:T(8,128)S(1)} %get-tuple-element.97.sin_ref, bf16[4,3,128,2048]{3,2,1,0:T(8,128)(2,1)S(1)} %bitcast.12, ...), custom_call_target="tpu_custom_call" | custom-call | tf_op jit(solution)/shard_map/contract_0_2/pallas_call | solution.py:262
  64.7 2.0 %collective-permute-start.1 = (bf16[1,2,3,16,2048]{4,3,2,1,0:T(8,128)(2,1)S(1)}, bf16[1,2,3,16,2048]{4,3,2,1,0:T(8,128)(2,1)S(1)}, u32[]{:S(2)}, u32[]{:S(2)}) collective-permute-start(bf16[1,2,3,16,2048]{4,3,2,1,0:T(8,128)(2,1)S(1)} %get-tuple-element.57.refs_0_), channel_id=1, source_target_pairs={{0,64},{32,96},{64,0},{96,32},{1,65},{33,97},{65,1},{97,33},{2,66}... | collective-permute-start | bytes 1179656 | tf_op jit(solution)/shard_map/ppermute | solution.py:37
  66.7 2.8 %collective-permute-start.10 = (bf16[1,2,64,128]{3,2,1,0:T(8,128)(2,1)S(1)}, bf16[1,2,64,128]{3,2,1,0:T(8,128)(2,1)S(1)}, u32[]{:S(2)}, u32[]{:S(2)}) collective-permute-start(bf16[1,2,64,128]{3,2,1,0:T(8,128)(2,1)S(1)} %get-tuple-element.84), channel_id=1, source_target_pairs={{0,3},{1,2},{2,1},{3,0},{4,7},{5,6},{6,5},{7,4},{8,11},{9,10},{10,... | collective-permute-start | bytes 98312 | tf_op jit(solution)/shard_map/ppermute | solution.py:33
  69.5 1.7 %contract_2_1.3 = (f32[1,4,2,64,128]{4,3,2,1,0:T(8,128)S(1)}, f32[8,128]{1,0:T(8,128)S(1)}) custom-call(s32[8,256]{1,0:T(8,128)S(1)} %broadcast.183.pat_ref, f32[8,2048]{1,0:T(8,128)S(1)} %get-tuple-element.98.cos_ref, f32[8,2048]{1,0:T(8,128)S(1)} %get-tuple-element.97.sin_ref, bf16[4,3,128,2048]{3,2,1,0:T(8,128)(2,1)S(1)} %bitcast.13, ...), custom_call_target="tpu_custom_call" | custom-call | tf_op jit(solution)/shard_map/contract_2_1/pallas_call | solution.py:262
  71.9 2.2 %collective-permute-start.11 = (bf16[1,4,2,64,128]{4,3,2,1,0:T(8,128)(2,1)S(1)}, bf16[1,4,2,64,128]{4,3,2,1,0:T(8,128)(2,1)S(1)}, u32[]{:S(2)}, u32[]{:S(2)}) collective-permute-start(bf16[1,4,2,64,128]{4,3,2,1,0:T(8,128)(2,1)S(1)} %get-tuple-element.87), channel_id=1, source_target_pairs={{0,24},{1,25},{2,26},{3,27},{4,28},{5,29},{6,30},{7,31},{8,16},{9,... | collective-permute-start | bytes 393224 | tf_op jit(solution)/shard_map/ppermute | solution.py:33
  74.1 4.0 %collective-permute-done.11.refs_3_ = bf16[1,4,2,64,128]{4,3,2,1,0:T(8,128)(2,1)S(1)} collective-permute-done((bf16[1,4,2,64,128]{4,3,2,1,0:T(8,128)(2,1)S(1)}, bf16[1,4,2,64,128]{4,3,2,1,0:T(8,128)(2,1)S(1)}, u32[]{:S(2)}, u32[]{:S(2)}) %collective-permute-start.11) | collective-permute-done | bytes 131104 | tf_op jit(solution)/shard_map/ppermute | solution.py:33
  78.2 1.7 %contract_3_1.3 = (bf16[2,1,2,64,128]{4,3,2,1,0:T(8,128)(2,1)S(1)}, f32[2,1,2,64,128]{4,3,2,1,0:T(8,128)S(1)}, f32[8,128]{1,0:T(8,128)S(1)}) custom-call(s32[8,256]{1,0:T(8,128)S(1)} %broadcast.183.pat_ref, f32[8,2048]{1,0:T(8,128)S(1)} %get-tuple-element.98.cos_ref, f32[8,2048]{1,0:T(8,128)S(1)} %get-tuple-element.97.sin_ref, ...), custom_call_target="tpu_custom_call" | custom-call | tf_op jit(solution)/shard_map/contract_3_1/pallas_call | solution.py:262
  80.7 3.8 %collective-permute-start.14 = (f32[1,2,64,128]{3,2,1,0:T(8,128)S(1)}, f32[1,2,64,128]{3,2,1,0:T(8,128)S(1)}, u32[]{:S(2)}, u32[]{:S(2)}) collective-permute-start(f32[1,2,64,128]{3,2,1,0:T(8,128)S(1)} %get-tuple-element.94), channel_id=1, source_target_pairs={{0,4},{1,5},{2,6},{3,7},{4,0},{5,1},{6,2},{7,3},{8,12},{9,13},{10,... | collective-permute-start | bytes 196616 | tf_op jit(solution)/shard_map/ppermute | solution.py:33
  85.1 2.5 %collective-permute-start.13 = (bf16[1,2,64,128]{3,2,1,0:T(8,128)(2,1)S(1)}, bf16[1,2,64,128]{3,2,1,0:T(8,128)(2,1)S(1)}, u32[]{:S(2)}, u32[]{:S(2)}) collective-permute-start(bf16[1,2,64,128]{3,2,1,0:T(8,128)(2,1)S(1)} %get-tuple-element.93), channel_id=1, source_target_pairs={{0,3},{1,2},{2,1},{3,0},{4,7},{5,6},{6,5},{7,4},{8,11},{9,10},{10,... | collective-permute-start | bytes 98312 | tf_op jit(solution)/shard_map/ppermute | solution.py:33
  87.6 2.6 %collective-permute-done.13.last_ref = bf16[1,2,64,128]{3,2,1,0:T(8,128)(2,1)S(1)} collective-permute-done((bf16[1,2,64,128]{3,2,1,0:T(8,128)(2,1)S(1)}, bf16[1,2,64,128]{3,2,1,0:T(8,128)(2,1)S(1)}, u32[]{:S(2)}, u32[]{:S(2)}) %collective-permute-start.13) | collective-permute-done | bytes 32800 | tf_op jit(solution)/shard_map/ppermute | solution.py:33
  (46 shorter events, 8.9 us)
Async XLA Ops:
  2.0 0.8 copy-start
  2.8 19.5 %collective-permute-start = (bf16[16,4,2,3,8,2048]{5,4,3,2,1,0:T(8,128)(2,1)}, bf16[16,4,2,3,8,2048]{5,4,3,2,1,0:T(8,128)(2,1)}, u32[]{:S(2)}, u32[]{:S(2)}) collective-permute-start(bf16[16,4,2,3,8,2048]{5,4,3,2,1,0:T(8,128)(2,1)} %in_ref.3), channel_id=1, source_target_pairs={{0,32},{32,0},{64,96},{96,64},{1,33},{33,1},{65,97},{97,65},{2,34}... | collective-permute-start | bytes 37748744 | tf_op jit(solution)/shard_map/ppermute | solution.py:37
  2.8 29.4 %collective-permute-start.3 = (bf16[2,2,3,16,2048]{4,3,2,1,0:T(8,128)(2,1)S(1)}, bf16[2,2,3,16,2048]{4,3,2,1,0:T(8,128)(2,1)}, u32[]{:S(2)}, u32[]{:S(2)}) collective-permute-start(bf16[2,2,3,16,2048]{4,3,2,1,0:T(8,128)(2,1)S(1)} %get-tuple-element.61.refs_0_), channel_id=1, source_target_pairs={{0,64},{32,96},{64,0},{96,32},{1,65},{33,97},{65,1},{97,33},{2,66}... | collective-permute-start | bytes 2359304 | tf_op jit(solution)/shard_map/ppermute | solution.py:37
  4.8 36.3 %collective-permute-start.2 = (bf16[2,2,3,16,2048]{4,3,2,1,0:T(8,128)(2,1)S(1)}, bf16[2,2,3,16,2048]{4,3,2,1,0:T(8,128)(2,1)}, u32[]{:S(2)}, u32[]{:S(2)}) collective-permute-start(bf16[2,2,3,16,2048]{4,3,2,1,0:T(8,128)(2,1)S(1)} %get-tuple-element.60.refs_0_), channel_id=1, source_target_pairs={{0,64},{32,96},{64,0},{96,32},{1,65},{33,97},{65,1},{97,33},{2,66}... | collective-permute-start | bytes 2359304 | tf_op jit(solution)/shard_map/ppermute | solution.py:37
  4.9 54.6 %collective-permute-start.6 = (bf16[2,2,3,16,2048]{4,3,2,1,0:T(8,128)(2,1)S(1)}, bf16[2,2,3,16,2048]{4,3,2,1,0:T(8,128)(2,1)S(1)}, u32[]{:S(2)}, u32[]{:S(2)}) collective-permute-start(bf16[2,2,3,16,2048]{4,3,2,1,0:T(8,128)(2,1)S(1)} %get-tuple-element.74.refs_0_), channel_id=1, source_target_pairs={{0,64},{32,96},{64,0},{96,32},{1,65},{33,97},{65,1},{97,33},{2,66}... | collective-permute-start | bytes 2359304 | tf_op jit(solution)/shard_map/ppermute | solution.py:37
  8.6 9.9 %copy-start.2 = (s32[3,2048]{1,0:T(4,128)S(1)}, s32[3,2048]{1,0:T(4,128)}, u32[]{:S(2)}) copy-start(s32[3,2048]{1,0:T(4,128)} %pad_add_fusion) | copy-start | bytes 73732
  8.6 9.9 %copy-start.3 = (s32[8,3]{0,1:T(4,128)S(1)}, s32[8,3]{0,1:T(4,128)}, u32[]{:S(2)}) copy-start(s32[8,3]{0,1:T(4,128)} %param.7) | copy-start | bytes 292
  39.3 9.2 %collective-permute-start.4 = (bf16[2,4,2,64,128]{4,3,2,1,0:T(8,128)(2,1)S(1)}, bf16[2,4,2,64,128]{4,3,2,1,0:T(8,128)(2,1)S(1)}, u32[]{:S(2)}, u32[]{:S(2)}) collective-permute-start(bf16[2,4,2,64,128]{4,3,2,1,0:T(8,128)(2,1)S(1)} %get-tuple-element.65), channel_id=1, source_target_pairs={{0,8},{1,9},{2,10},{3,11},{4,12},{5,13},{6,14},{7,15},{8,0},{9,1},... | collective-permute-start | bytes 786440 | tf_op jit(solution)/shard_map/ppermute | solution.py:33
  41.1 9.8 %copy-start.1 = (bf16[1,2,3,16,2048]{4,3,2,1,0:T(8,128)(2,1)S(1)}, bf16[1,2,3,16,2048]{4,3,2,1,0:T(8,128)(2,1)}, u32[]{:S(2)}) copy-start(bf16[1,2,3,16,2048]{4,3,2,1,0:T(8,128)(2,1)} %copy-done) | copy-start | bytes 1179652
  48.5 6.5 %collective-permute-start.5 = (bf16[1,4,2,64,128]{4,3,2,1,0:T(8,128)(2,1)S(1)}, bf16[1,4,2,64,128]{4,3,2,1,0:T(8,128)(2,1)S(1)}, u32[]{:S(2)}, u32[]{:S(2)}) collective-permute-start(bf16[1,4,2,64,128]{4,3,2,1,0:T(8,128)(2,1)S(1)} %get-tuple-element.68), channel_id=1, source_target_pairs={{0,24},{1,25},{2,26},{3,27},{4,28},{5,29},{6,30},{7,31},{8,16},{9,... | collective-permute-start | bytes 393224 | tf_op jit(solution)/shard_map/ppermute | solution.py:33
  50.9 18.6 %collective-permute-start.9 = (bf16[1,2,3,16,2048]{4,3,2,1,0:T(8,128)(2,1)S(1)}, bf16[1,2,3,16,2048]{4,3,2,1,0:T(8,128)(2,1)S(1)}, u32[]{:S(2)}, u32[]{:S(2)}) collective-permute-start(bf16[1,2,3,16,2048]{4,3,2,1,0:T(8,128)(2,1)S(1)} %copy-done.1), channel_id=1, source_target_pairs={{0,64},{32,96},{64,0},{96,32},{1,65},{33,97},{65,1},{97,33},{2,66}... | collective-permute-start | bytes 1179656 | tf_op jit(solution)/shard_map/ppermute | solution.py:37
  55.1 4.3 %collective-permute-start.7 = (bf16[2,2,64,128]{3,2,1,0:T(8,128)(2,1)S(1)}, bf16[2,2,64,128]{3,2,1,0:T(8,128)(2,1)S(1)}, u32[]{:S(2)}, u32[]{:S(2)}) collective-permute-start(bf16[2,2,64,128]{3,2,1,0:T(8,128)(2,1)S(1)} %get-tuple-element.76), channel_id=1, source_target_pairs={{0,1},{1,0},{2,3},{3,2},{4,5},{5,4},{6,7},{7,6},{8,9},{9,8},{10,11... | collective-permute-start | bytes 196616 | tf_op jit(solution)/shard_map/ppermute | solution.py:33
  64.6 7.2 %collective-permute-start.8 = (bf16[2,4,2,64,128]{4,3,2,1,0:T(8,128)(2,1)S(1)}, bf16[2,4,2,64,128]{4,3,2,1,0:T(8,128)(2,1)S(1)}, u32[]{:S(2)}, u32[]{:S(2)}) collective-permute-start(bf16[2,4,2,64,128]{4,3,2,1,0:T(8,128)(2,1)S(1)} %get-tuple-element.79), channel_id=1, source_target_pairs={{0,8},{1,9},{2,10},{3,11},{4,12},{5,13},{6,14},{7,15},{8,0},{9,1},... | collective-permute-start | bytes 786440 | tf_op jit(solution)/shard_map/ppermute | solution.py:33
  64.7 9.4 %collective-permute-start.1 = (bf16[1,2,3,16,2048]{4,3,2,1,0:T(8,128)(2,1)S(1)}, bf16[1,2,3,16,2048]{4,3,2,1,0:T(8,128)(2,1)S(1)}, u32[]{:S(2)}, u32[]{:S(2)}) collective-permute-start(bf16[1,2,3,16,2048]{4,3,2,1,0:T(8,128)(2,1)S(1)} %get-tuple-element.57.refs_0_), channel_id=1, source_target_pairs={{0,64},{32,96},{64,0},{96,32},{1,65},{33,97},{65,1},{97,33},{2,66}... | collective-permute-start | bytes 1179656 | tf_op jit(solution)/shard_map/ppermute | solution.py:37
  66.7 5.1 %collective-permute-start.10 = (bf16[1,2,64,128]{3,2,1,0:T(8,128)(2,1)S(1)}, bf16[1,2,64,128]{3,2,1,0:T(8,128)(2,1)S(1)}, u32[]{:S(2)}, u32[]{:S(2)}) collective-permute-start(bf16[1,2,64,128]{3,2,1,0:T(8,128)(2,1)S(1)} %get-tuple-element.84), channel_id=1, source_target_pairs={{0,3},{1,2},{2,1},{3,0},{4,7},{5,6},{6,5},{7,4},{8,11},{9,10},{10,... | collective-permute-start | bytes 98312 | tf_op jit(solution)/shard_map/ppermute | solution.py:33
  71.9 6.3 %collective-permute-start.11 = (bf16[1,4,2,64,128]{4,3,2,1,0:T(8,128)(2,1)S(1)}, bf16[1,4,2,64,128]{4,3,2,1,0:T(8,128)(2,1)S(1)}, u32[]{:S(2)}, u32[]{:S(2)}) collective-permute-start(bf16[1,4,2,64,128]{4,3,2,1,0:T(8,128)(2,1)S(1)} %get-tuple-element.87), channel_id=1, source_target_pairs={{0,24},{1,25},{2,26},{3,27},{4,28},{5,29},{6,30},{7,31},{8,16},{9,... | collective-permute-start | bytes 393224 | tf_op jit(solution)/shard_map/ppermute | solution.py:33
  79.9 4.6 %collective-permute-start.12 = (bf16[2,1,2,64,128]{4,3,2,0,1:T(8,128)(2,1)S(1)}, bf16[2,1,2,64,128]{4,3,2,0,1:T(8,128)(2,1)S(1)}, u32[]{:S(2)}, u32[]{:S(2)}) collective-permute-start(bf16[2,1,2,64,128]{4,3,2,0,1:T(8,128)(2,1)S(1)} %bitcast.24), channel_id=1, source_target_pairs={{0,1},{1,0},{2,3},{3,2},{4,5},{5,4},{6,7},{7,6},{8,9},{9,8},{10,11... | collective-permute-start | bytes 196616 | tf_op jit(solution)/shard_map/ppermute | solution.py:33
  80.7 6.9 %collective-permute-start.14 = (f32[1,2,64,128]{3,2,1,0:T(8,128)S(1)}, f32[1,2,64,128]{3,2,1,0:T(8,128)S(1)}, u32[]{:S(2)}, u32[]{:S(2)}) collective-permute-start(f32[1,2,64,128]{3,2,1,0:T(8,128)S(1)} %get-tuple-element.94), channel_id=1, source_target_pairs={{0,4},{1,5},{2,6},{3,7},{4,0},{5,1},{6,2},{7,3},{8,12},{9,13},{10,... | collective-permute-start | bytes 196616 | tf_op jit(solution)/shard_map/ppermute | solution.py:33
  85.1 5.1 %collective-permute-start.13 = (bf16[1,2,64,128]{3,2,1,0:T(8,128)(2,1)S(1)}, bf16[1,2,64,128]{3,2,1,0:T(8,128)(2,1)S(1)}, u32[]{:S(2)}, u32[]{:S(2)}) collective-permute-start(bf16[1,2,64,128]{3,2,1,0:T(8,128)(2,1)S(1)} %get-tuple-element.93), channel_id=1, source_target_pairs={{0,3},{1,2},{2,1},{3,0},{4,7},{5,6},{6,5},{7,4},{8,11},{9,10},{10,... | collective-permute-start | bytes 98312 | tf_op jit(solution)/shard_map/ppermute | solution.py:33
  90.3 1.3 %collective-permute-start.15 = (f32[2,32,128]{2,1,0:T(8,128)S(1)}, f32[2,32,128]{2,1,0:T(8,128)S(1)}, u32[]{:S(2)}, u32[]{:S(2)}) collective-permute-start(f32[2,32,128]{2,1,0:T(8,128)S(1)} %get-tuple-element.96), channel_id=1, source_target_pairs={{0,32},{32,0},{64,96},{96,64},{1,33},{33,1},{65,97},{97,65},{2,34}... | collective-permute-start | bytes 98312 | tf_op jit(solution)/shard_map/ppermute | solution.py:37

commit v5 on v4

--- a/solution.py
+++ b/solution.py
@@ -423,12 +423,13 @@
     away, token = plus((far, far_got), wide, token)
     across = trade(away, 0, 1, 0)
     away, token = plus((near, near_got), narrow, token)
-    adds = (near_got, trade(away, 3, 0, 0))
-    away, near, token = contract(
-        tables, few, None, arrived[4], 3, True, narrow, token, FEW_LIMIT, adds, last_base
-    )
+    near_last = trade(away, 3, 0, 0)
+    near, token = contract(
+        tables, few, None, arrived[4], 3, False, wide, token, FEW_LIMIT, (near_got,), last_base
+    )
+    away, near, token = fold((near[0], near_last[0]), narrow, token)
     last_got = trade(away, 0, 0, 1)
-    away, near, token = fold((near[:, 0], last_got[:, 0]), narrow, token)
+    away, near, token = fold((near, last_got), narrow, token)
     last_got = trade(away, 0, 0, 3)
     mine, other = finish(near, last_got, across)
     pieces = (mine, flip(other, 1))

time: 93.7 us -> 92.1 us (0.983)
  waiting for transfers between devices: 13.5 us -> 11.8 us
    ppermute x9, waiting for transfers between devices: 8.85 us -> 7.1 us  [trade(): return lax.ppermute(block, 'site', route)]
  transfers between devices with their start and end apart: 16 -> 16, of which waited for: 7 -> 7; matrix products, arithmetic and copies ran while one was open for 2% -> 2% of each run, Pallas kernels for 49% -> 52%
where the time goes in v5:
time: 92.1 us; the launch traced here: 90.7 us
  Pallas kernels  50.1 us (54%)
  starting transfers between devices  25.8 us (28%)
  waiting for transfers between devices  11.8 us (13%)
  local copies, waits for them, and re-layouts  1.75 us (2%)
  other arithmetic  1.12 us (1%)
    pallas_call x7, Pallas kernels, contract(): pl.pallas_call(functools.partial(contract_body, by_part, blocks, base is...  26.6 us
    pallas_call x2, Pallas kernels, relayout_low(): pl.pallas_call(relayout_low_body, grid=(colours, two), in_specs=[pl.Block...  19.8 us
    ppermute x9, starting transfers between devices, trade(): return lax.ppermute(block, 'site', route)  17.8 us
    ppermute x7, starting transfers between devices, flip(): return lax.ppermute(block, 'mode', [(i, i ^ mask) for i in range(4)])  8.03 us
    ppermute x9, waiting for transfers between devices, trade(): return lax.ppermute(block, 'site', route)  7.1 us
    ppermute x7, waiting for transfers between devices, flip(): return lax.ppermute(block, 'mode', [(i, i ^ mask) for i in range(4)])  4.68 us
    pallas_call x1, Pallas kernels, relayout_high(): pl.pallas_call(relayout_high_body, in_specs=[pl.BlockSpec(memory_space=pl...  2.04 us
  transfers between devices with their start and end apart: 16, of which 7 were waited for; matrix products, arithmetic and copies ran while one was open for 2% of the time, Pallas kernels for 52%

profile of v5, /device:TPU:0, one launch (start us, length us, event | category | flops | bytes accessed | tf_op | source)
XLA Modules:
  0.0 90.7 jit_solution(13942974432144039726)
XLA Ops:
  0.0 2.0 %relayout_high.1 = (bf16[2,2,3,16,2048]{4,3,2,1,0:T(8,128)(2,1)S(1)}, bf16[2,2,3,16,2048]{4,3,2,1,0:T(8,128)(2,1)S(1)}, bf16[2,2,3,16,2048]{4,3,2,1,0:T(8,128)(2...) custom-call(bf16[16,2,3,8,2048]{4,3,2,1,0:T(8,128)(2,1)} %in_ref.2), custom_call_target="tpu_custom_call" | custom-call | tf_op jit(solution)/shard_map/relayout_high/pallas_call | solution.py:99
  2.8 2.0 %collective-permute-start.3 = (bf16[2,2,3,16,2048]{4,3,2,1,0:T(8,128)(2,1)S(1)}, bf16[2,2,3,16,2048]{4,3,2,1,0:T(8,128)(2,1)}, u32[]{:S(2)}, u32[]{:S(2)}) collective-permute-start(bf16[2,2,3,16,2048]{4,3,2,1,0:T(8,128)(2,1)S(1)} %get-tuple-element.63.refs_0_), channel_id=1, source_target_pairs={{0,64},{32,96},{64,0},{96,32},{1,65},{33,97},{65,1},{97,33},{2,66}... | collective-permute-start | bytes 2359304 | tf_op jit(solution)/shard_map/ppermute | solution.py:37
  4.9 2.0 %collective-permute-start.6 = (bf16[2,2,3,16,2048]{4,3,2,1,0:T(8,128)(2,1)S(1)}, bf16[2,2,3,16,2048]{4,3,2,1,0:T(8,128)(2,1)S(1)}, u32[]{:S(2)}, u32[]{:S(2)}) collective-permute-start(bf16[2,2,3,16,2048]{4,3,2,1,0:T(8,128)(2,1)S(1)} %get-tuple-element.76.refs_0_), channel_id=1, source_target_pairs={{0,64},{32,96},{64,0},{96,32},{1,65},{33,97},{65,1},{97,33},{2,66}... | collective-permute-start | bytes 2359304 | tf_op jit(solution)/shard_map/ppermute | solution.py:37
  8.6 9.9 %relayout_low.2 = (bf16[4,3,2,4,16,2048]{5,4,3,2,1,0:T(8,128)(2,1)}, bf16[4,3,2,4,16,2048]{5,4,3,2,1,0:T(8,128)(2,1)S(1)}, f32[8,128]{1,0:T(8,128)S(1)}) custom-call(bf16[16,4,2,3,8,2048]{5,4,3,2,1,0:T(8,128)(2,1)} %in_ref.3, f32[8,128]{1,0:T(8,128)S(1)} %get-tuple-element.54.after_ref), custom_call_target="tpu_custom_call" | custom-call | tf_op jit(solution)/shard_map/relayout_low/pallas_call | solution.py:132
  18.9 3.4 %collective-permute-done.in_ref = bf16[16,4,2,3,8,2048]{5,4,3,2,1,0:T(8,128)(2,1)} collective-permute-done((bf16[16,4,2,3,8,2048]{5,4,3,2,1,0:T(8,128)(2,1)}, bf16[16,4,2,3,8,2048]{5,4,3,2,1,0:T(8,128)(2,1)}, u32[]{:S(2)}, u32[]{:S(2)}) %collective-permute-start) | collective-permute-done | bytes 12582944 | tf_op jit(solution)/shard_map/ppermute | solution.py:37
  22.3 9.9 %relayout_low.3 = (bf16[4,3,2,4,16,2048]{5,4,3,2,1,0:T(8,128)(2,1)}, bf16[4,3,2,4,16,2048]{5,4,3,2,1,0:T(8,128)(2,1)S(1)}, f32[8,128]{1,0:T(8,128)S(1)}) custom-call(bf16[16,4,2,3,8,2048]{5,4,3,2,1,0:T(8,128)(2,1)} %collective-permute-done.in_ref, f32[8,128]{1,0:T(8,128)S(1)} %get-tuple-element.57.after_ref), custom_call_target="tpu_custom_call" | custom-call | tf_op jit(solution)/shard_map/relayout_low/pallas_call | solution.py:132
  32.2 7.1 %contract_0_2.2 = (bf16[2,4,2,64,128]{4,3,2,1,0:T(8,128)(2,1)S(1)}, f32[8,128]{1,0:T(8,128)S(1)}) custom-call(s32[8,256]{1,0:T(8,128)S(1)} %broadcast.183.pat_ref, f32[8,2048]{1,0:T(8,128)S(1)} %get-tuple-element.102.cos_ref, f32[8,2048]{1,0:T(8,128)S(1)} %get-tuple-element.101.sin_ref, bf16[4,3,128,2048]{3,2,1,0:T(8,128)(2,1)} %bitcast.23, ...), custom_call_target="tpu_custom_call" | custom-call | tf_op jit(solution)/shard_map/contract_0_2/pallas_call | solution.py:262
  39.3 1.8 %collective-permute-start.4 = (bf16[2,4,2,64,128]{4,3,2,1,0:T(8,128)(2,1)S(1)}, bf16[2,4,2,64,128]{4,3,2,1,0:T(8,128)(2,1)S(1)}, u32[]{:S(2)}, u32[]{:S(2)}) collective-permute-start(bf16[2,4,2,64,128]{4,3,2,1,0:T(8,128)(2,1)S(1)} %get-tuple-element.67), channel_id=1, source_target_pairs={{0,8},{1,9},{2,10},{3,11},{4,12},{5,13},{6,14},{7,15},{8,0},{9,1},... | collective-permute-start | bytes 786440 | tf_op jit(solution)/shard_map/ppermute | solution.py:33
  41.1 7.4 %contract_2_2.1 = (f32[2,4,2,64,128]{4,3,2,1,0:T(8,128)S(1)}, f32[8,128]{1,0:T(8,128)S(1)}) custom-call(s32[8,256]{1,0:T(8,128)S(1)} %broadcast.183.pat_ref, f32[8,2048]{1,0:T(8,128)S(1)} %get-tuple-element.102.cos_ref, f32[8,2048]{1,0:T(8,128)S(1)} %get-tuple-element.101.sin_ref, bf16[4,3,128,2048]{3,2,1,0:T(8,128)(2,1)} %bitcast.24, ...), custom_call_target="tpu_custom_call" | custom-call | tf_op jit(solution)/shard_map/contract_2_2/pallas_call | solution.py:262
  48.6 2.4 %collective-permute-start.5 = (bf16[1,4,2,64,128]{4,3,2,1,0:T(8,128)(2,1)S(1)}, bf16[1,4,2,64,128]{4,3,2,1,0:T(8,128)(2,1)S(1)}, u32[]{:S(2)}, u32[]{:S(2)}) collective-permute-start(bf16[1,4,2,64,128]{4,3,2,1,0:T(8,128)(2,1)S(1)} %get-tuple-element.70), channel_id=1, source_target_pairs={{0,24},{1,25},{2,26},{3,27},{4,28},{5,29},{6,30},{7,31},{8,16},{9,... | collective-permute-start | bytes 393224 | tf_op jit(solution)/shard_map/ppermute | solution.py:33
  50.9 1.9 %collective-permute-start.9 = (bf16[1,2,3,16,2048]{4,3,2,1,0:T(8,128)(2,1)S(1)}, bf16[1,2,3,16,2048]{4,3,2,1,0:T(8,128)(2,1)S(1)}, u32[]{:S(2)}, u32[]{:S(2)}) collective-permute-start(bf16[1,2,3,16,2048]{4,3,2,1,0:T(8,128)(2,1)S(1)} %copy-done.1), channel_id=1, source_target_pairs={{0,64},{32,96},{64,0},{96,32},{1,65},{33,97},{65,1},{97,33},{2,66}... | collective-permute-start | bytes 1179656 | tf_op jit(solution)/shard_map/ppermute | solution.py:37
  52.8 1.7 %contract_2_1.2 = (f32[1,4,1,64,128]{4,3,2,1,0:T(8,128)S(1)}, f32[8,128]{1,0:T(8,128)S(1)}) custom-call(s32[8,256]{1,0:T(8,128)S(1)} %broadcast.183.pat_ref, f32[8,2048]{1,0:T(8,128)S(1)} %get-tuple-element.102.cos_ref, f32[8,2048]{1,0:T(8,128)S(1)} %get-tuple-element.101.sin_ref, bf16[4,3,128,2048]{3,2,1,0:T(8,128)(2,1)S(1)} %bitcast.9, ...), custom_call_target="tpu_custom_call" | custom-call | tf_op jit(solution)/shard_map/contract_2_1/pallas_call | solution.py:262
  55.1 1.6 %collective-permute-start.7 = (bf16[2,2,64,128]{3,2,1,0:T(8,128)(2,1)S(1)}, bf16[2,2,64,128]{3,2,1,0:T(8,128)(2,1)S(1)}, u32[]{:S(2)}, u32[]{:S(2)}) collective-permute-start(bf16[2,2,64,128]{3,2,1,0:T(8,128)(2,1)S(1)} %get-tuple-element.78), channel_id=1, source_target_pairs={{0,1},{1,0},{2,3},{3,2},{4,5},{5,4},{6,7},{7,6},{8,9},{9,8},{10,11... | collective-permute-start | bytes 196616 | tf_op jit(solution)/shard_map/ppermute | solution.py:33
  56.7 1.7 %contract_3_1.2 = (f32[1,4,1,64,128]{4,3,2,1,0:T(8,128)S(1)}, f32[8,128]{1,0:T(8,128)S(1)}) custom-call(s32[8,256]{1,0:T(8,128)S(1)} %broadcast.183.pat_ref, f32[8,2048]{1,0:T(8,128)S(1)} %get-tuple-element.102.cos_ref, f32[8,2048]{1,0:T(8,128)S(1)} %get-tuple-element.101.sin_ref, bf16[4,3,128,2048]{3,2,1,0:T(8,128)(2,1)S(1)} %bitcast.10, ...), custom_call_target="tpu_custom_call" | custom-call | tf_op jit(solution)/shard_map/contract_3_1/pallas_call | solution.py:262
  59.5 5.1 %contract_0_2.3 = (bf16[2,4,2,64,128]{4,3,2,1,0:T(8,128)(2,1)S(1)}, f32[8,128]{1,0:T(8,128)S(1)}) custom-call(s32[8,256]{1,0:T(8,128)S(1)} %broadcast.183.pat_ref, f32[8,2048]{1,0:T(8,128)S(1)} %get-tuple-element.102.cos_ref, f32[8,2048]{1,0:T(8,128)S(1)} %get-tuple-element.101.sin_ref, bf16[4,3,128,2048]{3,2,1,0:T(8,128)(2,1)S(1)} %bitcast.11, ...), custom_call_target="tpu_custom_call" | custom-call | tf_op jit(solution)/shard_map/contract_0_2/pallas_call | solution.py:262
  64.8 2.0 %collective-permute-start.1 = (bf16[1,2,3,16,2048]{4,3,2,1,0:T(8,128)(2,1)S(1)}, bf16[1,2,3,16,2048]{4,3,2,1,0:T(8,128)(2,1)S(1)}, u32[]{:S(2)}, u32[]{:S(2)}) collective-permute-start(bf16[1,2,3,16,2048]{4,3,2,1,0:T(8,128)(2,1)S(1)} %get-tuple-element.59.refs_0_), channel_id=1, source_target_pairs={{0,64},{32,96},{64,0},{96,32},{1,65},{33,97},{65,1},{97,33},{2,66}... | collective-permute-start | bytes 1179656 | tf_op jit(solution)/shard_map/ppermute | solution.py:37
  66.8 2.8 %collective-permute-start.10 = (bf16[1,2,64,128]{3,2,1,0:T(8,128)(2,1)S(1)}, bf16[1,2,64,128]{3,2,1,0:T(8,128)(2,1)S(1)}, u32[]{:S(2)}, u32[]{:S(2)}) collective-permute-start(bf16[1,2,64,128]{3,2,1,0:T(8,128)(2,1)S(1)} %get-tuple-element.86), channel_id=1, source_target_pairs={{0,3},{1,2},{2,1},{3,0},{4,7},{5,6},{6,5},{7,4},{8,11},{9,10},{10,... | collective-permute-start | bytes 98312 | tf_op jit(solution)/shard_map/ppermute | solution.py:33
  69.5 1.7 %contract_2_1.3 = (f32[1,4,2,64,128]{4,3,2,1,0:T(8,128)S(1)}, f32[8,128]{1,0:T(8,128)S(1)}) custom-call(s32[8,256]{1,0:T(8,128)S(1)} %broadcast.183.pat_ref, f32[8,2048]{1,0:T(8,128)S(1)} %get-tuple-element.102.cos_ref, f32[8,2048]{1,0:T(8,128)S(1)} %get-tuple-element.101.sin_ref, bf16[4,3,128,2048]{3,2,1,0:T(8,128)(2,1)S(1)} %bitcast.12, ...), custom_call_target="tpu_custom_call" | custom-call | tf_op jit(solution)/shard_map/contract_2_1/pallas_call | solution.py:262
  72.0 2.2 %collective-permute-start.11 = (bf16[1,4,2,64,128]{4,3,2,1,0:T(8,128)(2,1)S(1)}, bf16[1,4,2,64,128]{4,3,2,1,0:T(8,128)(2,1)S(1)}, u32[]{:S(2)}, u32[]{:S(2)}) collective-permute-start(bf16[1,4,2,64,128]{4,3,2,1,0:T(8,128)(2,1)S(1)} %get-tuple-element.91), channel_id=1, source_target_pairs={{0,24},{1,25},{2,26},{3,27},{4,28},{5,29},{6,30},{7,31},{8,16},{9,... | collective-permute-start | bytes 393224 | tf_op jit(solution)/shard_map/ppermute | solution.py:33
  74.2 1.7 %contract_3_1.3 = (f32[1,4,2,64,128]{4,3,2,1,0:T(8,128)S(1)}, f32[8,128]{1,0:T(8,128)S(1)}) custom-call(s32[8,256]{1,0:T(8,128)S(1)} %broadcast.183.pat_ref, f32[8,2048]{1,0:T(8,128)S(1)} %get-tuple-element.102.cos_ref, f32[8,2048]{1,0:T(8,128)S(1)} %get-tuple-element.101.sin_ref, bf16[4,3,128,2048]{3,2,1,0:T(8,128)(2,1)S(1)} %bitcast.13, ...), custom_call_target="tpu_custom_call" | custom-call | tf_op jit(solution)/shard_map/contract_3_1/pallas_call | solution.py:262
  75.9 2.3 %collective-permute-done.11 = bf16[1,4,2,64,128]{4,3,2,1,0:T(8,128)(2,1)S(1)} collective-permute-done((bf16[1,4,2,64,128]{4,3,2,1,0:T(8,128)(2,1)S(1)}, bf16[1,4,2,64,128]{4,3,2,1,0:T(8,128)(2,1)S(1)}, u32[]{:S(2)}, u32[]{:S(2)}) %collective-permute-start.11) | collective-permute-done | bytes 131104 | tf_op jit(solution)/shard_map/ppermute | solution.py:33
  79.0 3.8 %collective-permute-start.14 = (f32[1,2,64,128]{3,2,1,0:T(8,128)S(1)}, f32[1,2,64,128]{3,2,1,0:T(8,128)S(1)}, u32[]{:S(2)}, u32[]{:S(2)}) collective-permute-start(f32[1,2,64,128]{3,2,1,0:T(8,128)S(1)} %get-tuple-element.98), channel_id=1, source_target_pairs={{0,4},{1,5},{2,6},{3,7},{4,0},{5,1},{6,2},{7,3},{8,12},{9,13},{10,... | collective-permute-start | bytes 196616 | tf_op jit(solution)/shard_map/ppermute | solution.py:33
  83.4 2.5 %collective-permute-start.13 = (bf16[1,2,64,128]{3,2,1,0:T(8,128)(2,1)S(1)}, bf16[1,2,64,128]{3,2,1,0:T(8,128)(2,1)S(1)}, u32[]{:S(2)}, u32[]{:S(2)}) collective-permute-start(bf16[1,2,64,128]{3,2,1,0:T(8,128)(2,1)S(1)} %get-tuple-element.97), channel_id=1, source_target_pairs={{0,3},{1,2},{2,1},{3,0},{4,7},{5,6},{6,5},{7,4},{8,11},{9,10},{10,... | collective-permute-start | bytes 98312 | tf_op jit(solution)/shard_map/ppermute | solution.py:33
  86.0 2.6 %collective-permute-done.13.last_ref = bf16[1,2,64,128]{3,2,1,0:T(8,128)(2,1)S(1)} collective-permute-done((bf16[1,2,64,128]{3,2,1,0:T(8,128)(2,1)S(1)}, bf16[1,2,64,128]{3,2,1,0:T(8,128)(2,1)S(1)}, u32[]{:S(2)}, u32[]{:S(2)}) %collective-permute-start.13) | collective-permute-done | bytes 32800 | tf_op jit(solution)/shard_map/ppermute | solution.py:33
  (47 shorter events, 9.0 us)
Async XLA Ops:
  2.0 0.8 copy-start
  2.8 19.5 %collective-permute-start = (bf16[16,4,2,3,8,2048]{5,4,3,2,1,0:T(8,128)(2,1)}, bf16[16,4,2,3,8,2048]{5,4,3,2,1,0:T(8,128)(2,1)}, u32[]{:S(2)}, u32[]{:S(2)}) collective-permute-start(bf16[16,4,2,3,8,2048]{5,4,3,2,1,0:T(8,128)(2,1)} %in_ref.3), channel_id=1, source_target_pairs={{0,32},{32,0},{64,96},{96,64},{1,33},{33,1},{65,97},{97,65},{2,34}... | collective-permute-start | bytes 37748744 | tf_op jit(solution)/shard_map/ppermute | solution.py:37
  2.8 29.4 %collective-permute-start.3 = (bf16[2,2,3,16,2048]{4,3,2,1,0:T(8,128)(2,1)S(1)}, bf16[2,2,3,16,2048]{4,3,2,1,0:T(8,128)(2,1)}, u32[]{:S(2)}, u32[]{:S(2)}) collective-permute-start(bf16[2,2,3,16,2048]{4,3,2,1,0:T(8,128)(2,1)S(1)} %get-tuple-element.63.refs_0_), channel_id=1, source_target_pairs={{0,64},{32,96},{64,0},{96,32},{1,65},{33,97},{65,1},{97,33},{2,66}... | collective-permute-start | bytes 2359304 | tf_op jit(solution)/shard_map/ppermute | solution.py:37
  4.8 36.3 %collective-permute-start.2 = (bf16[2,2,3,16,2048]{4,3,2,1,0:T(8,128)(2,1)S(1)}, bf16[2,2,3,16,2048]{4,3,2,1,0:T(8,128)(2,1)}, u32[]{:S(2)}, u32[]{:S(2)}) collective-permute-start(bf16[2,2,3,16,2048]{4,3,2,1,0:T(8,128)(2,1)S(1)} %get-tuple-element.62.refs_0_), channel_id=1, source_target_pairs={{0,64},{32,96},{64,0},{96,32},{1,65},{33,97},{65,1},{97,33},{2,66}... | collective-permute-start | bytes 2359304 | tf_op jit(solution)/shard_map/ppermute | solution.py:37
  4.9 54.6 %collective-permute-start.6 = (bf16[2,2,3,16,2048]{4,3,2,1,0:T(8,128)(2,1)S(1)}, bf16[2,2,3,16,2048]{4,3,2,1,0:T(8,128)(2,1)S(1)}, u32[]{:S(2)}, u32[]{:S(2)}) collective-permute-start(bf16[2,2,3,16,2048]{4,3,2,1,0:T(8,128)(2,1)S(1)} %get-tuple-element.76.refs_0_), channel_id=1, source_target_pairs={{0,64},{32,96},{64,0},{96,32},{1,65},{33,97},{65,1},{97,33},{2,66}... | collective-permute-start | bytes 2359304 | tf_op jit(solution)/shard_map/ppermute | solution.py:37
  8.6 9.9 %copy-start.2 = (s32[3,2048]{1,0:T(4,128)S(1)}, s32[3,2048]{1,0:T(4,128)}, u32[]{:S(2)}) copy-start(s32[3,2048]{1,0:T(4,128)} %pad_add_fusion) | copy-start | bytes 73732
  8.6 9.9 %copy-start.3 = (s32[8,3]{0,1:T(4,128)S(1)}, s32[8,3]{0,1:T(4,128)}, u32[]{:S(2)}) copy-start(s32[8,3]{0,1:T(4,128)} %param.7) | copy-start | bytes 292
  39.3 9.2 %collective-permute-start.4 = (bf16[2,4,2,64,128]{4,3,2,1,0:T(8,128)(2,1)S(1)}, bf16[2,4,2,64,128]{4,3,2,1,0:T(8,128)(2,1)S(1)}, u32[]{:S(2)}, u32[]{:S(2)}) collective-permute-start(bf16[2,4,2,64,128]{4,3,2,1,0:T(8,128)(2,1)S(1)} %get-tuple-element.67), channel_id=1, source_target_pairs={{0,8},{1,9},{2,10},{3,11},{4,12},{5,13},{6,14},{7,15},{8,0},{9,1},... | collective-permute-start | bytes 786440 | tf_op jit(solution)/shard_map/ppermute | solution.py:33
  41.1 9.8 %copy-start.1 = (bf16[1,2,3,16,2048]{4,3,2,1,0:T(8,128)(2,1)S(1)}, bf16[1,2,3,16,2048]{4,3,2,1,0:T(8,128)(2,1)}, u32[]{:S(2)}) copy-start(bf16[1,2,3,16,2048]{4,3,2,1,0:T(8,128)(2,1)} %copy-done) | copy-start | bytes 1179652
  48.6 6.6 %collective-permute-start.5 = (bf16[1,4,2,64,128]{4,3,2,1,0:T(8,128)(2,1)S(1)}, bf16[1,4,2,64,128]{4,3,2,1,0:T(8,128)(2,1)S(1)}, u32[]{:S(2)}, u32[]{:S(2)}) collective-permute-start(bf16[1,4,2,64,128]{4,3,2,1,0:T(8,128)(2,1)S(1)} %get-tuple-element.70), channel_id=1, source_target_pairs={{0,24},{1,25},{2,26},{3,27},{4,28},{5,29},{6,30},{7,31},{8,16},{9,... | collective-permute-start | bytes 393224 | tf_op jit(solution)/shard_map/ppermute | solution.py:33
  50.9 18.6 %collective-permute-start.9 = (bf16[1,2,3,16,2048]{4,3,2,1,0:T(8,128)(2,1)S(1)}, bf16[1,2,3,16,2048]{4,3,2,1,0:T(8,128)(2,1)S(1)}, u32[]{:S(2)}, u32[]{:S(2)}) collective-permute-start(bf16[1,2,3,16,2048]{4,3,2,1,0:T(8,128)(2,1)S(1)} %copy-done.1), channel_id=1, source_target_pairs={{0,64},{32,96},{64,0},{96,32},{1,65},{33,97},{65,1},{97,33},{2,66}... | collective-permute-start | bytes 1179656 | tf_op jit(solution)/shard_map/ppermute | solution.py:37
  55.1 4.3 %collective-permute-start.7 = (bf16[2,2,64,128]{3,2,1,0:T(8,128)(2,1)S(1)}, bf16[2,2,64,128]{3,2,1,0:T(8,128)(2,1)S(1)}, u32[]{:S(2)}, u32[]{:S(2)}) collective-permute-start(bf16[2,2,64,128]{3,2,1,0:T(8,128)(2,1)S(1)} %get-tuple-element.78), channel_id=1, source_target_pairs={{0,1},{1,0},{2,3},{3,2},{4,5},{5,4},{6,7},{7,6},{8,9},{9,8},{10,11... | collective-permute-start | bytes 196616 | tf_op jit(solution)/shard_map/ppermute | solution.py:33
  64.7 7.2 %collective-permute-start.8 = (bf16[2,4,2,64,128]{4,3,2,1,0:T(8,128)(2,1)S(1)}, bf16[2,4,2,64,128]{4,3,2,1,0:T(8,128)(2,1)S(1)}, u32[]{:S(2)}, u32[]{:S(2)}) collective-permute-start(bf16[2,4,2,64,128]{4,3,2,1,0:T(8,128)(2,1)S(1)} %get-tuple-element.81), channel_id=1, source_target_pairs={{0,8},{1,9},{2,10},{3,11},{4,12},{5,13},{6,14},{7,15},{8,0},{9,1},... | collective-permute-start | bytes 786440 | tf_op jit(solution)/shard_map/ppermute | solution.py:33
  64.8 9.4 %collective-permute-start.1 = (bf16[1,2,3,16,2048]{4,3,2,1,0:T(8,128)(2,1)S(1)}, bf16[1,2,3,16,2048]{4,3,2,1,0:T(8,128)(2,1)S(1)}, u32[]{:S(2)}, u32[]{:S(2)}) collective-permute-start(bf16[1,2,3,16,2048]{4,3,2,1,0:T(8,128)(2,1)S(1)} %get-tuple-element.59.refs_0_), channel_id=1, source_target_pairs={{0,64},{32,96},{64,0},{96,32},{1,65},{33,97},{65,1},{97,33},{2,66}... | collective-permute-start | bytes 1179656 | tf_op jit(solution)/shard_map/ppermute | solution.py:37
  66.8 5.1 %collective-permute-start.10 = (bf16[1,2,64,128]{3,2,1,0:T(8,128)(2,1)S(1)}, bf16[1,2,64,128]{3,2,1,0:T(8,128)(2,1)S(1)}, u32[]{:S(2)}, u32[]{:S(2)}) collective-permute-start(bf16[1,2,64,128]{3,2,1,0:T(8,128)(2,1)S(1)} %get-tuple-element.86), channel_id=1, source_target_pairs={{0,3},{1,2},{2,1},{3,0},{4,7},{5,6},{6,5},{7,4},{8,11},{9,10},{10,... | collective-permute-start | bytes 98312 | tf_op jit(solution)/shard_map/ppermute | solution.py:33
  72.0 6.3 %collective-permute-start.11 = (bf16[1,4,2,64,128]{4,3,2,1,0:T(8,128)(2,1)S(1)}, bf16[1,4,2,64,128]{4,3,2,1,0:T(8,128)(2,1)S(1)}, u32[]{:S(2)}, u32[]{:S(2)}) collective-permute-start(bf16[1,4,2,64,128]{4,3,2,1,0:T(8,128)(2,1)S(1)} %get-tuple-element.91), channel_id=1, source_target_pairs={{0,24},{1,25},{2,26},{3,27},{4,28},{5,29},{6,30},{7,31},{8,16},{9,... | collective-permute-start | bytes 393224 | tf_op jit(solution)/shard_map/ppermute | solution.py:33
  78.2 4.6 %collective-permute-start.12 = (bf16[2,2,64,128]{3,2,1,0:T(8,128)(2,1)S(1)}, bf16[2,2,64,128]{3,2,1,0:T(8,128)(2,1)S(1)}, u32[]{:S(2)}, u32[]{:S(2)}) collective-permute-start(bf16[2,2,64,128]{3,2,1,0:T(8,128)(2,1)S(1)} %get-tuple-element.94), channel_id=1, source_target_pairs={{0,1},{1,0},{2,3},{3,2},{4,5},{5,4},{6,7},{7,6},{8,9},{9,8},{10,11... | collective-permute-start | bytes 196616 | tf_op jit(solution)/shard_map/ppermute | solution.py:33
  79.0 6.9 %collective-permute-start.14 = (f32[1,2,64,128]{3,2,1,0:T(8,128)S(1)}, f32[1,2,64,128]{3,2,1,0:T(8,128)S(1)}, u32[]{:S(2)}, u32[]{:S(2)}) collective-permute-start(f32[1,2,64,128]{3,2,1,0:T(8,128)S(1)} %get-tuple-element.98), channel_id=1, source_target_pairs={{0,4},{1,5},{2,6},{3,7},{4,0},{5,1},{6,2},{7,3},{8,12},{9,13},{10,... | collective-permute-start | bytes 196616 | tf_op jit(solution)/shard_map/ppermute | solution.py:33
  83.4 5.1 %collective-permute-start.13 = (bf16[1,2,64,128]{3,2,1,0:T(8,128)(2,1)S(1)}, bf16[1,2,64,128]{3,2,1,0:T(8,128)(2,1)S(1)}, u32[]{:S(2)}, u32[]{:S(2)}) collective-permute-start(bf16[1,2,64,128]{3,2,1,0:T(8,128)(2,1)S(1)} %get-tuple-element.97), channel_id=1, source_target_pairs={{0,3},{1,2},{2,1},{3,0},{4,7},{5,6},{6,5},{7,4},{8,11},{9,10},{10,... | collective-permute-start | bytes 98312 | tf_op jit(solution)/shard_map/ppermute | solution.py:33
  88.6 1.3 %collective-permute-start.15 = (f32[2,32,128]{2,1,0:T(8,128)S(1)}, f32[2,32,128]{2,1,0:T(8,128)S(1)}, u32[]{:S(2)}, u32[]{:S(2)}) collective-permute-start(f32[2,32,128]{2,1,0:T(8,128)S(1)} %get-tuple-element.100), channel_id=1, source_target_pairs={{0,32},{32,0},{64,96},{96,64},{1,33},{33,1},{65,97},{97,65},{2,34}... | collective-permute-start | bytes 98312 | tf_op jit(solution)/shard_map/ppermute | solution.py:37

commit v6 on v5

--- a/solution.py
+++ b/solution.py
@@ -50,9 +50,9 @@
 
 VMEM = pl.BlockSpec(memory_space=pltpu.VMEM)
 STEP = 512
-HIGH_LIMIT = 12 * 2**20
-LOW_LIMIT = 16 * 2**20
-MANY_LIMIT = 24 * 2**20
+HIGH_LIMIT = 6 * 2**20
+LOW_LIMIT = 10 * 2**20
+MANY_LIMIT = 14 * 2**20
 FEW_LIMIT = 14 * 2**20
 SMALL = pltpu.CompilerParams(vmem_limit_bytes=4 * 2**20)
 TOKEN = jax.ShapeDtypeStruct((8, 128), jnp.float32)

time: 92.1 us -> 92.1 us (level)
  no operation moved by 1% of the time
where the time goes in v6:
time: 92.1 us; the launch traced here: 90.7 us
  Pallas kernels  50.1 us (54%)
  starting transfers between devices  25.9 us (28%)
  waiting for transfers between devices  11.8 us (13%)
  local copies, waits for them, and re-layouts  1.75 us (2%)
  other arithmetic  1.12 us (1%)
    pallas_call x7, Pallas kernels, contract(): pl.pallas_call(functools.partial(contract_body, by_part, blocks, base is...  26.6 us
    pallas_call x2, Pallas kernels, relayout_low(): pl.pallas_call(relayout_low_body, grid=(colours, two), in_specs=[pl.Block...  19.8 us
    ppermute x9, starting transfers between devices, trade(): return lax.ppermute(block, 'site', route)  17.8 us
    ppermute x7, starting transfers between devices, flip(): return lax.ppermute(block, 'mode', [(i, i ^ mask) for i in range(4)])  8.03 us
    ppermute x9, waiting for transfers between devices, trade(): return lax.ppermute(block, 'site', route)  7.08 us
    ppermute x7, waiting for transfers between devices, flip(): return lax.ppermute(block, 'mode', [(i, i ^ mask) for i in range(4)])  4.67 us
    pallas_call x1, Pallas kernels, relayout_high(): pl.pallas_call(relayout_high_body, in_specs=[pl.BlockSpec(memory_space=pl...  2.04 us
  transfers between devices with their start and end apart: 16, of which 7 were waited for; matrix products, arithmetic and copies ran while one was open for 2% of the time, Pallas kernels for 52%

profile of v6, /device:TPU:0, one launch (start us, length us, event | category | flops | bytes accessed | tf_op | source)
XLA Modules:
  0.0 90.7 jit_solution(3594686749402301252)
XLA Ops:
  0.0 2.0 %relayout_high.1 = (bf16[2,2,3,16,2048]{4,3,2,1,0:T(8,128)(2,1)S(1)}, bf16[2,2,3,16,2048]{4,3,2,1,0:T(8,128)(2,1)S(1)}, bf16[2,2,3,16,2048]{4,3,2,1,0:T(8,128)(2...) custom-call(bf16[16,2,3,8,2048]{4,3,2,1,0:T(8,128)(2,1)} %in_ref.2), custom_call_target="tpu_custom_call" | custom-call | tf_op jit(solution)/shard_map/relayout_high/pallas_call | solution.py:99
  2.8 2.0 %collective-permute-start.3 = (bf16[2,2,3,16,2048]{4,3,2,1,0:T(8,128)(2,1)S(1)}, bf16[2,2,3,16,2048]{4,3,2,1,0:T(8,128)(2,1)}, u32[]{:S(2)}, u32[]{:S(2)}) collective-permute-start(bf16[2,2,3,16,2048]{4,3,2,1,0:T(8,128)(2,1)S(1)} %get-tuple-element.63.refs_0_), channel_id=1, source_target_pairs={{0,64},{32,96},{64,0},{96,32},{1,65},{33,97},{65,1},{97,33},{2,66}... | collective-permute-start | bytes 2359304 | tf_op jit(solution)/shard_map/ppermute | solution.py:37
  4.9 2.0 %collective-permute-start.6 = (bf16[2,2,3,16,2048]{4,3,2,1,0:T(8,128)(2,1)S(1)}, bf16[2,2,3,16,2048]{4,3,2,1,0:T(8,128)(2,1)S(1)}, u32[]{:S(2)}, u32[]{:S(2)}) collective-permute-start(bf16[2,2,3,16,2048]{4,3,2,1,0:T(8,128)(2,1)S(1)} %get-tuple-element.76.refs_0_), channel_id=1, source_target_pairs={{0,64},{32,96},{64,0},{96,32},{1,65},{33,97},{65,1},{97,33},{2,66}... | collective-permute-start | bytes 2359304 | tf_op jit(solution)/shard_map/ppermute | solution.py:37
  8.6 9.9 %relayout_low.2 = (bf16[4,3,2,4,16,2048]{5,4,3,2,1,0:T(8,128)(2,1)}, bf16[4,3,2,4,16,2048]{5,4,3,2,1,0:T(8,128)(2,1)S(1)}, f32[8,128]{1,0:T(8,128)S(1)}) custom-call(bf16[16,4,2,3,8,2048]{5,4,3,2,1,0:T(8,128)(2,1)} %in_ref.3, f32[8,128]{1,0:T(8,128)S(1)} %get-tuple-element.54.after_ref), custom_call_target="tpu_custom_call" | custom-call | tf_op jit(solution)/shard_map/relayout_low/pallas_call | solution.py:132
  18.9 3.4 %collective-permute-done.in_ref = bf16[16,4,2,3,8,2048]{5,4,3,2,1,0:T(8,128)(2,1)} collective-permute-done((bf16[16,4,2,3,8,2048]{5,4,3,2,1,0:T(8,128)(2,1)}, bf16[16,4,2,3,8,2048]{5,4,3,2,1,0:T(8,128)(2,1)}, u32[]{:S(2)}, u32[]{:S(2)}) %collective-permute-start) | collective-permute-done | bytes 12582944 | tf_op jit(solution)/shard_map/ppermute | solution.py:37
  22.3 9.9 %relayout_low.3 = (bf16[4,3,2,4,16,2048]{5,4,3,2,1,0:T(8,128)(2,1)}, bf16[4,3,2,4,16,2048]{5,4,3,2,1,0:T(8,128)(2,1)S(1)}, f32[8,128]{1,0:T(8,128)S(1)}) custom-call(bf16[16,4,2,3,8,2048]{5,4,3,2,1,0:T(8,128)(2,1)} %collective-permute-done.in_ref, f32[8,128]{1,0:T(8,128)S(1)} %get-tuple-element.57.after_ref), custom_call_target="tpu_custom_call" | custom-call | tf_op jit(solution)/shard_map/relayout_low/pallas_call | solution.py:132
  32.2 7.1 %contract_0_2.2 = (bf16[2,4,2,64,128]{4,3,2,1,0:T(8,128)(2,1)S(1)}, f32[8,128]{1,0:T(8,128)S(1)}) custom-call(s32[8,256]{1,0:T(8,128)S(1)} %broadcast.183.pat_ref, f32[8,2048]{1,0:T(8,128)S(1)} %get-tuple-element.102.cos_ref, f32[8,2048]{1,0:T(8,128)S(1)} %get-tuple-element.101.sin_ref, bf16[4,3,128,2048]{3,2,1,0:T(8,128)(2,1)} %bitcast.23, ...), custom_call_target="tpu_custom_call" | custom-call | tf_op jit(solution)/shard_map/contract_0_2/pallas_call | solution.py:262
  39.3 1.8 %collective-permute-start.4 = (bf16[2,4,2,64,128]{4,3,2,1,0:T(8,128)(2,1)S(1)}, bf16[2,4,2,64,128]{4,3,2,1,0:T(8,128)(2,1)S(1)}, u32[]{:S(2)}, u32[]{:S(2)}) collective-permute-start(bf16[2,4,2,64,128]{4,3,2,1,0:T(8,128)(2,1)S(1)} %get-tuple-element.67), channel_id=1, source_target_pairs={{0,8},{1,9},{2,10},{3,11},{4,12},{5,13},{6,14},{7,15},{8,0},{9,1},... | collective-permute-start | bytes 786440 | tf_op jit(solution)/shard_map/ppermute | solution.py:33
  41.1 7.4 %contract_2_2.1 = (f32[2,4,2,64,128]{4,3,2,1,0:T(8,128)S(1)}, f32[8,128]{1,0:T(8,128)S(1)}) custom-call(s32[8,256]{1,0:T(8,128)S(1)} %broadcast.183.pat_ref, f32[8,2048]{1,0:T(8,128)S(1)} %get-tuple-element.102.cos_ref, f32[8,2048]{1,0:T(8,128)S(1)} %get-tuple-element.101.sin_ref, bf16[4,3,128,2048]{3,2,1,0:T(8,128)(2,1)} %bitcast.24, ...), custom_call_target="tpu_custom_call" | custom-call | tf_op jit(solution)/shard_map/contract_2_2/pallas_call | solution.py:262
  48.6 2.4 %collective-permute-start.5 = (bf16[1,4,2,64,128]{4,3,2,1,0:T(8,128)(2,1)S(1)}, bf16[1,4,2,64,128]{4,3,2,1,0:T(8,128)(2,1)S(1)}, u32[]{:S(2)}, u32[]{:S(2)}) collective-permute-start(bf16[1,4,2,64,128]{4,3,2,1,0:T(8,128)(2,1)S(1)} %get-tuple-element.70), channel_id=1, source_target_pairs={{0,24},{1,25},{2,26},{3,27},{4,28},{5,29},{6,30},{7,31},{8,16},{9,... | collective-permute-start | bytes 393224 | tf_op jit(solution)/shard_map/ppermute | solution.py:33
  50.9 1.9 %collective-permute-start.9 = (bf16[1,2,3,16,2048]{4,3,2,1,0:T(8,128)(2,1)S(1)}, bf16[1,2,3,16,2048]{4,3,2,1,0:T(8,128)(2,1)S(1)}, u32[]{:S(2)}, u32[]{:S(2)}) collective-permute-start(bf16[1,2,3,16,2048]{4,3,2,1,0:T(8,128)(2,1)S(1)} %copy-done.1), channel_id=1, source_target_pairs={{0,64},{32,96},{64,0},{96,32},{1,65},{33,97},{65,1},{97,33},{2,66}... | collective-permute-start | bytes 1179656 | tf_op jit(solution)/shard_map/ppermute | solution.py:37
  52.8 1.7 %contract_2_1.2 = (f32[1,4,1,64,128]{4,3,2,1,0:T(8,128)S(1)}, f32[8,128]{1,0:T(8,128)S(1)}) custom-call(s32[8,256]{1,0:T(8,128)S(1)} %broadcast.183.pat_ref, f32[8,2048]{1,0:T(8,128)S(1)} %get-tuple-element.102.cos_ref, f32[8,2048]{1,0:T(8,128)S(1)} %get-tuple-element.101.sin_ref, bf16[4,3,128,2048]{3,2,1,0:T(8,128)(2,1)S(1)} %bitcast.9, ...), custom_call_target="tpu_custom_call" | custom-call | tf_op jit(solution)/shard_map/contract_2_1/pallas_call | solution.py:262
  55.1 1.6 %collective-permute-start.7 = (bf16[2,2,64,128]{3,2,1,0:T(8,128)(2,1)S(1)}, bf16[2,2,64,128]{3,2,1,0:T(8,128)(2,1)S(1)}, u32[]{:S(2)}, u32[]{:S(2)}) collective-permute-start(bf16[2,2,64,128]{3,2,1,0:T(8,128)(2,1)S(1)} %get-tuple-element.78), channel_id=1, source_target_pairs={{0,1},{1,0},{2,3},{3,2},{4,5},{5,4},{6,7},{7,6},{8,9},{9,8},{10,11... | collective-permute-start | bytes 196616 | tf_op jit(solution)/shard_map/ppermute | solution.py:33
  56.7 1.7 %contract_3_1.2 = (f32[1,4,1,64,128]{4,3,2,1,0:T(8,128)S(1)}, f32[8,128]{1,0:T(8,128)S(1)}) custom-call(s32[8,256]{1,0:T(8,128)S(1)} %broadcast.183.pat_ref, f32[8,2048]{1,0:T(8,128)S(1)} %get-tuple-element.102.cos_ref, f32[8,2048]{1,0:T(8,128)S(1)} %get-tuple-element.101.sin_ref, bf16[4,3,128,2048]{3,2,1,0:T(8,128)(2,1)S(1)} %bitcast.10, ...), custom_call_target="tpu_custom_call" | custom-call | tf_op jit(solution)/shard_map/contract_3_1/pallas_call | solution.py:262
  59.5 5.1 %contract_0_2.3 = (bf16[2,4,2,64,128]{4,3,2,1,0:T(8,128)(2,1)S(1)}, f32[8,128]{1,0:T(8,128)S(1)}) custom-call(s32[8,256]{1,0:T(8,128)S(1)} %broadcast.183.pat_ref, f32[8,2048]{1,0:T(8,128)S(1)} %get-tuple-element.102.cos_ref, f32[8,2048]{1,0:T(8,128)S(1)} %get-tuple-element.101.sin_ref, bf16[4,3,128,2048]{3,2,1,0:T(8,128)(2,1)S(1)} %bitcast.11, ...), custom_call_target="tpu_custom_call" | custom-call | tf_op jit(solution)/shard_map/contract_0_2/pallas_call | solution.py:262
  64.8 2.0 %collective-permute-start.1 = (bf16[1,2,3,16,2048]{4,3,2,1,0:T(8,128)(2,1)S(1)}, bf16[1,2,3,16,2048]{4,3,2,1,0:T(8,128)(2,1)S(1)}, u32[]{:S(2)}, u32[]{:S(2)}) collective-permute-start(bf16[1,2,3,16,2048]{4,3,2,1,0:T(8,128)(2,1)S(1)} %get-tuple-element.59.refs_0_), channel_id=1, source_target_pairs={{0,64},{32,96},{64,0},{96,32},{1,65},{33,97},{65,1},{97,33},{2,66}... | collective-permute-start | bytes 1179656 | tf_op jit(solution)/shard_map/ppermute | solution.py:37
  66.8 2.8 %collective-permute-start.10 = (bf16[1,2,64,128]{3,2,1,0:T(8,128)(2,1)S(1)}, bf16[1,2,64,128]{3,2,1,0:T(8,128)(2,1)S(1)}, u32[]{:S(2)}, u32[]{:S(2)}) collective-permute-start(bf16[1,2,64,128]{3,2,1,0:T(8,128)(2,1)S(1)} %get-tuple-element.86), channel_id=1, source_target_pairs={{0,3},{1,2},{2,1},{3,0},{4,7},{5,6},{6,5},{7,4},{8,11},{9,10},{10,... | collective-permute-start | bytes 98312 | tf_op jit(solution)/shard_map/ppermute | solution.py:33
  69.5 1.7 %contract_2_1.3 = (f32[1,4,2,64,128]{4,3,2,1,0:T(8,128)S(1)}, f32[8,128]{1,0:T(8,128)S(1)}) custom-call(s32[8,256]{1,0:T(8,128)S(1)} %broadcast.183.pat_ref, f32[8,2048]{1,0:T(8,128)S(1)} %get-tuple-element.102.cos_ref, f32[8,2048]{1,0:T(8,128)S(1)} %get-tuple-element.101.sin_ref, bf16[4,3,128,2048]{3,2,1,0:T(8,128)(2,1)S(1)} %bitcast.12, ...), custom_call_target="tpu_custom_call" | custom-call | tf_op jit(solution)/shard_map/contract_2_1/pallas_call | solution.py:262
  71.9 2.2 %collective-permute-start.11 = (bf16[1,4,2,64,128]{4,3,2,1,0:T(8,128)(2,1)S(1)}, bf16[1,4,2,64,128]{4,3,2,1,0:T(8,128)(2,1)S(1)}, u32[]{:S(2)}, u32[]{:S(2)}) collective-permute-start(bf16[1,4,2,64,128]{4,3,2,1,0:T(8,128)(2,1)S(1)} %get-tuple-element.91), channel_id=1, source_target_pairs={{0,24},{1,25},{2,26},{3,27},{4,28},{5,29},{6,30},{7,31},{8,16},{9,... | collective-permute-start | bytes 393224 | tf_op jit(solution)/shard_map/ppermute | solution.py:33
  74.2 1.7 %contract_3_1.3 = (f32[1,4,2,64,128]{4,3,2,1,0:T(8,128)S(1)}, f32[8,128]{1,0:T(8,128)S(1)}) custom-call(s32[8,256]{1,0:T(8,128)S(1)} %broadcast.183.pat_ref, f32[8,2048]{1,0:T(8,128)S(1)} %get-tuple-element.102.cos_ref, f32[8,2048]{1,0:T(8,128)S(1)} %get-tuple-element.101.sin_ref, bf16[4,3,128,2048]{3,2,1,0:T(8,128)(2,1)S(1)} %bitcast.13, ...), custom_call_target="tpu_custom_call" | custom-call | tf_op jit(solution)/shard_map/contract_3_1/pallas_call | solution.py:262
  75.9 2.3 %collective-permute-done.11 = bf16[1,4,2,64,128]{4,3,2,1,0:T(8,128)(2,1)S(1)} collective-permute-done((bf16[1,4,2,64,128]{4,3,2,1,0:T(8,128)(2,1)S(1)}, bf16[1,4,2,64,128]{4,3,2,1,0:T(8,128)(2,1)S(1)}, u32[]{:S(2)}, u32[]{:S(2)}) %collective-permute-start.11) | collective-permute-done | bytes 131104 | tf_op jit(solution)/shard_map/ppermute | solution.py:33
  79.0 3.8 %collective-permute-start.14 = (f32[1,2,64,128]{3,2,1,0:T(8,128)S(1)}, f32[1,2,64,128]{3,2,1,0:T(8,128)S(1)}, u32[]{:S(2)}, u32[]{:S(2)}) collective-permute-start(f32[1,2,64,128]{3,2,1,0:T(8,128)S(1)} %get-tuple-element.98), channel_id=1, source_target_pairs={{0,4},{1,5},{2,6},{3,7},{4,0},{5,1},{6,2},{7,3},{8,12},{9,13},{10,... | collective-permute-start | bytes 196616 | tf_op jit(solution)/shard_map/ppermute | solution.py:33
  83.5 2.5 %collective-permute-start.13 = (bf16[1,2,64,128]{3,2,1,0:T(8,128)(2,1)S(1)}, bf16[1,2,64,128]{3,2,1,0:T(8,128)(2,1)S(1)}, u32[]{:S(2)}, u32[]{:S(2)}) collective-permute-start(bf16[1,2,64,128]{3,2,1,0:T(8,128)(2,1)S(1)} %get-tuple-element.97), channel_id=1, source_target_pairs={{0,3},{1,2},{2,1},{3,0},{4,7},{5,6},{6,5},{7,4},{8,11},{9,10},{10,... | collective-permute-start | bytes 98312 | tf_op jit(solution)/shard_map/ppermute | solution.py:33
  86.0 2.6 %collective-permute-done.13.last_ref = bf16[1,2,64,128]{3,2,1,0:T(8,128)(2,1)S(1)} collective-permute-done((bf16[1,2,64,128]{3,2,1,0:T(8,128)(2,1)S(1)}, bf16[1,2,64,128]{3,2,1,0:T(8,128)(2,1)S(1)}, u32[]{:S(2)}, u32[]{:S(2)}) %collective-permute-start.13) | collective-permute-done | bytes 32800 | tf_op jit(solution)/shard_map/ppermute | solution.py:33
  (47 shorter events, 8.9 us)
Async XLA Ops:
  2.0 0.8 copy-start
  2.8 19.5 %collective-permute-start = (bf16[16,4,2,3,8,2048]{5,4,3,2,1,0:T(8,128)(2,1)}, bf16[16,4,2,3,8,2048]{5,4,3,2,1,0:T(8,128)(2,1)}, u32[]{:S(2)}, u32[]{:S(2)}) collective-permute-start(bf16[16,4,2,3,8,2048]{5,4,3,2,1,0:T(8,128)(2,1)} %in_ref.3), channel_id=1, source_target_pairs={{0,32},{32,0},{64,96},{96,64},{1,33},{33,1},{65,97},{97,65},{2,34}... | collective-permute-start | bytes 37748744 | tf_op jit(solution)/shard_map/ppermute | solution.py:37
  2.8 29.4 %collective-permute-start.3 = (bf16[2,2,3,16,2048]{4,3,2,1,0:T(8,128)(2,1)S(1)}, bf16[2,2,3,16,2048]{4,3,2,1,0:T(8,128)(2,1)}, u32[]{:S(2)}, u32[]{:S(2)}) collective-permute-start(bf16[2,2,3,16,2048]{4,3,2,1,0:T(8,128)(2,1)S(1)} %get-tuple-element.63.refs_0_), channel_id=1, source_target_pairs={{0,64},{32,96},{64,0},{96,32},{1,65},{33,97},{65,1},{97,33},{2,66}... | collective-permute-start | bytes 2359304 | tf_op jit(solution)/shard_map/ppermute | solution.py:37
  4.8 36.3 %collective-permute-start.2 = (bf16[2,2,3,16,2048]{4,3,2,1,0:T(8,128)(2,1)S(1)}, bf16[2,2,3,16,2048]{4,3,2,1,0:T(8,128)(2,1)}, u32[]{:S(2)}, u32[]{:S(2)}) collective-permute-start(bf16[2,2,3,16,2048]{4,3,2,1,0:T(8,128)(2,1)S(1)} %get-tuple-element.62.refs_0_), channel_id=1, source_target_pairs={{0,64},{32,96},{64,0},{96,32},{1,65},{33,97},{65,1},{97,33},{2,66}... | collective-permute-start | bytes 2359304 | tf_op jit(solution)/shard_map/ppermute | solution.py:37
  4.9 54.6 %collective-permute-start.6 = (bf16[2,2,3,16,2048]{4,3,2,1,0:T(8,128)(2,1)S(1)}, bf16[2,2,3,16,2048]{4,3,2,1,0:T(8,128)(2,1)S(1)}, u32[]{:S(2)}, u32[]{:S(2)}) collective-permute-start(bf16[2,2,3,16,2048]{4,3,2,1,0:T(8,128)(2,1)S(1)} %get-tuple-element.76.refs_0_), channel_id=1, source_target_pairs={{0,64},{32,96},{64,0},{96,32},{1,65},{33,97},{65,1},{97,33},{2,66}... | collective-permute-start | bytes 2359304 | tf_op jit(solution)/shard_map/ppermute | solution.py:37
  8.6 9.9 %copy-start.2 = (s32[3,2048]{1,0:T(4,128)S(1)}, s32[3,2048]{1,0:T(4,128)}, u32[]{:S(2)}) copy-start(s32[3,2048]{1,0:T(4,128)} %pad_add_fusion) | copy-start | bytes 73732
  8.6 9.9 %copy-start.3 = (s32[8,3]{0,1:T(4,128)S(1)}, s32[8,3]{0,1:T(4,128)}, u32[]{:S(2)}) copy-start(s32[8,3]{0,1:T(4,128)} %param.7) | copy-start | bytes 292
  39.3 9.2 %collective-permute-start.4 = (bf16[2,4,2,64,128]{4,3,2,1,0:T(8,128)(2,1)S(1)}, bf16[2,4,2,64,128]{4,3,2,1,0:T(8,128)(2,1)S(1)}, u32[]{:S(2)}, u32[]{:S(2)}) collective-permute-start(bf16[2,4,2,64,128]{4,3,2,1,0:T(8,128)(2,1)S(1)} %get-tuple-element.67), channel_id=1, source_target_pairs={{0,8},{1,9},{2,10},{3,11},{4,12},{5,13},{6,14},{7,15},{8,0},{9,1},... | collective-permute-start | bytes 786440 | tf_op jit(solution)/shard_map/ppermute | solution.py:33
  41.1 9.8 %copy-start.1 = (bf16[1,2,3,16,2048]{4,3,2,1,0:T(8,128)(2,1)S(1)}, bf16[1,2,3,16,2048]{4,3,2,1,0:T(8,128)(2,1)}, u32[]{:S(2)}) copy-start(bf16[1,2,3,16,2048]{4,3,2,1,0:T(8,128)(2,1)} %copy-done) | copy-start | bytes 1179652
  48.6 6.6 %collective-permute-start.5 = (bf16[1,4,2,64,128]{4,3,2,1,0:T(8,128)(2,1)S(1)}, bf16[1,4,2,64,128]{4,3,2,1,0:T(8,128)(2,1)S(1)}, u32[]{:S(2)}, u32[]{:S(2)}) collective-permute-start(bf16[1,4,2,64,128]{4,3,2,1,0:T(8,128)(2,1)S(1)} %get-tuple-element.70), channel_id=1, source_target_pairs={{0,24},{1,25},{2,26},{3,27},{4,28},{5,29},{6,30},{7,31},{8,16},{9,... | collective-permute-start | bytes 393224 | tf_op jit(solution)/shard_map/ppermute | solution.py:33
  50.9 18.6 %collective-permute-start.9 = (bf16[1,2,3,16,2048]{4,3,2,1,0:T(8,128)(2,1)S(1)}, bf16[1,2,3,16,2048]{4,3,2,1,0:T(8,128)(2,1)S(1)}, u32[]{:S(2)}, u32[]{:S(2)}) collective-permute-start(bf16[1,2,3,16,2048]{4,3,2,1,0:T(8,128)(2,1)S(1)} %copy-done.1), channel_id=1, source_target_pairs={{0,64},{32,96},{64,0},{96,32},{1,65},{33,97},{65,1},{97,33},{2,66}... | collective-permute-start | bytes 1179656 | tf_op jit(solution)/shard_map/ppermute | solution.py:37
  55.1 4.3 %collective-permute-start.7 = (bf16[2,2,64,128]{3,2,1,0:T(8,128)(2,1)S(1)}, bf16[2,2,64,128]{3,2,1,0:T(8,128)(2,1)S(1)}, u32[]{:S(2)}, u32[]{:S(2)}) collective-permute-start(bf16[2,2,64,128]{3,2,1,0:T(8,128)(2,1)S(1)} %get-tuple-element.78), channel_id=1, source_target_pairs={{0,1},{1,0},{2,3},{3,2},{4,5},{5,4},{6,7},{7,6},{8,9},{9,8},{10,11... | collective-permute-start | bytes 196616 | tf_op jit(solution)/shard_map/ppermute | solution.py:33
  64.7 7.2 %collective-permute-start.8 = (bf16[2,4,2,64,128]{4,3,2,1,0:T(8,128)(2,1)S(1)}, bf16[2,4,2,64,128]{4,3,2,1,0:T(8,128)(2,1)S(1)}, u32[]{:S(2)}, u32[]{:S(2)}) collective-permute-start(bf16[2,4,2,64,128]{4,3,2,1,0:T(8,128)(2,1)S(1)} %get-tuple-element.81), channel_id=1, source_target_pairs={{0,8},{1,9},{2,10},{3,11},{4,12},{5,13},{6,14},{7,15},{8,0},{9,1},... | collective-permute-start | bytes 786440 | tf_op jit(solution)/shard_map/ppermute | solution.py:33
  64.8 9.4 %collective-permute-start.1 = (bf16[1,2,3,16,2048]{4,3,2,1,0:T(8,128)(2,1)S(1)}, bf16[1,2,3,16,2048]{4,3,2,1,0:T(8,128)(2,1)S(1)}, u32[]{:S(2)}, u32[]{:S(2)}) collective-permute-start(bf16[1,2,3,16,2048]{4,3,2,1,0:T(8,128)(2,1)S(1)} %get-tuple-element.59.refs_0_), channel_id=1, source_target_pairs={{0,64},{32,96},{64,0},{96,32},{1,65},{33,97},{65,1},{97,33},{2,66}... | collective-permute-start | bytes 1179656 | tf_op jit(solution)/shard_map/ppermute | solution.py:37
  66.8 5.1 %collective-permute-start.10 = (bf16[1,2,64,128]{3,2,1,0:T(8,128)(2,1)S(1)}, bf16[1,2,64,128]{3,2,1,0:T(8,128)(2,1)S(1)}, u32[]{:S(2)}, u32[]{:S(2)}) collective-permute-start(bf16[1,2,64,128]{3,2,1,0:T(8,128)(2,1)S(1)} %get-tuple-element.86), channel_id=1, source_target_pairs={{0,3},{1,2},{2,1},{3,0},{4,7},{5,6},{6,5},{7,4},{8,11},{9,10},{10,... | collective-permute-start | bytes 98312 | tf_op jit(solution)/shard_map/ppermute | solution.py:33
  71.9 6.3 %collective-permute-start.11 = (bf16[1,4,2,64,128]{4,3,2,1,0:T(8,128)(2,1)S(1)}, bf16[1,4,2,64,128]{4,3,2,1,0:T(8,128)(2,1)S(1)}, u32[]{:S(2)}, u32[]{:S(2)}) collective-permute-start(bf16[1,4,2,64,128]{4,3,2,1,0:T(8,128)(2,1)S(1)} %get-tuple-element.91), channel_id=1, source_target_pairs={{0,24},{1,25},{2,26},{3,27},{4,28},{5,29},{6,30},{7,31},{8,16},{9,... | collective-permute-start | bytes 393224 | tf_op jit(solution)/shard_map/ppermute | solution.py:33
  78.2 4.6 %collective-permute-start.12 = (bf16[2,2,64,128]{3,2,1,0:T(8,128)(2,1)S(1)}, bf16[2,2,64,128]{3,2,1,0:T(8,128)(2,1)S(1)}, u32[]{:S(2)}, u32[]{:S(2)}) collective-permute-start(bf16[2,2,64,128]{3,2,1,0:T(8,128)(2,1)S(1)} %get-tuple-element.94), channel_id=1, source_target_pairs={{0,1},{1,0},{2,3},{3,2},{4,5},{5,4},{6,7},{7,6},{8,9},{9,8},{10,11... | collective-permute-start | bytes 196616 | tf_op jit(solution)/shard_map/ppermute | solution.py:33
  79.0 6.9 %collective-permute-start.14 = (f32[1,2,64,128]{3,2,1,0:T(8,128)S(1)}, f32[1,2,64,128]{3,2,1,0:T(8,128)S(1)}, u32[]{:S(2)}, u32[]{:S(2)}) collective-permute-start(f32[1,2,64,128]{3,2,1,0:T(8,128)S(1)} %get-tuple-element.98), channel_id=1, source_target_pairs={{0,4},{1,5},{2,6},{3,7},{4,0},{5,1},{6,2},{7,3},{8,12},{9,13},{10,... | collective-permute-start | bytes 196616 | tf_op jit(solution)/shard_map/ppermute | solution.py:33
  83.5 5.1 %collective-permute-start.13 = (bf16[1,2,64,128]{3,2,1,0:T(8,128)(2,1)S(1)}, bf16[1,2,64,128]{3,2,1,0:T(8,128)(2,1)S(1)}, u32[]{:S(2)}, u32[]{:S(2)}) collective-permute-start(bf16[1,2,64,128]{3,2,1,0:T(8,128)(2,1)S(1)} %get-tuple-element.97), channel_id=1, source_target_pairs={{0,3},{1,2},{2,1},{3,0},{4,7},{5,6},{6,5},{7,4},{8,11},{9,10},{10,... | collective-permute-start | bytes 98312 | tf_op jit(solution)/shard_map/ppermute | solution.py:33
  88.6 1.3 %collective-permute-start.15 = (f32[2,32,128]{2,1,0:T(8,128)S(1)}, f32[2,32,128]{2,1,0:T(8,128)S(1)}, u32[]{:S(2)}, u32[]{:S(2)}) collective-permute-start(f32[2,32,128]{2,1,0:T(8,128)S(1)} %get-tuple-element.100), channel_id=1, source_target_pairs={{0,32},{32,0},{64,96},{96,64},{1,33},{33,1},{65,97},{97,65},{2,34}... | collective-permute-start | bytes 98312 | tf_op jit(solution)/shard_map/ppermute | solution.py:37
